TPU v7x, 32 devices: a whole 2x2x4 slice. The times are simulated.
32 devices in a mesh: clip: 4 (over y, core), coarse: 4 (over z), fine: 2 (over x).
Axes of the slice: x: 2, y: 2, z: 4, core: 2. Of those that a mesh axis runs over, the one named last changes fastest.
Arguments:
- frames_in: bfloat16 [12, 1024, 1024], P('clip', ('coarse', 'fine')), may hold values from -6 to 6
- clip_lengths: int32 [12], P('clip'), may hold values from 512 to 1024, as said below
- out_grad: bfloat16 [12, 1024, 1024], P('clip', ('coarse', 'fine')), may hold values from -6 to 6
- first_up: float32 [1024, 4096], P('clip', ('coarse', 'fine')), may hold values from -0.1875 to 0.1875
- first_down: float32 [4096, 1024], P('clip', ('coarse', 'fine')), may hold values from -0.1875 to 0.1875
- query_weight: float32 [1024, 1024], P('clip', ('coarse', 'fine')), may hold values from -0.1875 to 0.1875
- key_weight: float32 [1024, 1024], P('clip', ('coarse', 'fine')), may hold values from -0.1875 to 0.1875
- value_weight: float32 [1024, 1024], P('clip', ('coarse', 'fine')), may hold values from -0.1875 to 0.1875
- output_weight: float32 [1024, 1024], P('clip', ('coarse', 'fine')), may hold values from -1.5 to 1.5
- pointwise_in: float32 [1024, 2048], P('clip', ('coarse', 'fine')), may hold values from -0.1875 to 0.1875
- pointwise_out: float32 [1024, 1024], P('clip', ('coarse', 'fine')), may hold values from -0.25 to 0.25
- second_up: float32 [1024, 4096], P('clip', ('coarse', 'fine')), may hold values from -0.1875 to 0.1875
- second_down: float32 [4096, 1024], P('clip', ('coarse', 'fine')), may hold values from -0.1875 to 0.1875
- norm_scales: float32 [6, 1024], replicated, may hold values from 0.25 to 1.75
- norm_shifts: float32 [6, 1024], replicated, may hold values from -1.75 to 1.75
- hidden_biases: float32 [2, 4096], replicated, may hold values from -3 to 3
- width_biases: float32 [4, 1024], replicated, may hold values from -1.75 to 1.75
- value_bias: float32 [1024], replicated, may hold values from -0.1875 to 0.1875
- relative_table: float32 [73, 64], replicated, may hold values from -6 to 6
- depth_kernel: float32 [31, 1024], replicated, may hold values from -1 to 1
Outputs:
- layer_out: bfloat16 [12, 1024, 1024], P('clip', ('coarse', 'fine'))
- in_grad: bfloat16 [12, 1024, 1024], P('clip', ('coarse', 'fine'))
- first_up_grad: float32 [1024, 4096], P('clip', ('coarse', 'fine'))
- first_down_grad: float32 [4096, 1024], P('clip', ('coarse', 'fine'))
- query_weight_grad: float32 [1024, 1024], P('clip', ('coarse', 'fine'))
- key_weight_grad: float32 [1024, 1024], P('clip', ('coarse', 'fine'))
- value_weight_grad: float32 [1024, 1024], P('clip', ('coarse', 'fine'))
- output_weight_grad: float32 [1024, 1024], P('clip', ('coarse', 'fine'))
- pointwise_in_grad: float32 [1024, 2048], P('clip', ('coarse', 'fine'))
- pointwise_out_grad: float32 [1024, 1024], P('clip', ('coarse', 'fine'))
- second_up_grad: float32 [1024, 4096], P('clip', ('coarse', 'fine'))
- second_down_grad: float32 [4096, 1024], P('clip', ('coarse', 'fine'))
- norm_scales_grad: float32 [6, 1024], replicated
- norm_shifts_grad: float32 [6, 1024], replicated
- hidden_biases_grad: float32 [2, 4096], replicated
- width_biases_grad: float32 [4, 1024], replicated
- value_bias_grad: float32 [1024], replicated
- relative_table_grad: float32 [73, 64], replicated
- depth_kernel_grad: float32 [31, 1024], replicated
Inputs may be any that keep to these rules, and one draw needn't show every extreme that they name: `clip_lengths`: in each aligned block of 3 clips, at least one clip has all 1024 frames valid.
All inputs are finite; a program needn't handle non-finite values.
Results may differ from a plain program's by a relative error of at most 0.023.
Values may be sent and summed in bfloat16 or wider, within the bound.
No kernel may reach another device: no remote copies, remote signals or barrier semaphores. Data moves between devices by JAX's collectives and lax.ppermute only.
A program may use at most 320 MiB of HBM per device.

v0:
```python
import jax
import jax.numpy as jnp
from jax import lax
from jax.sharding import PartitionSpec as P

D = 1024
HEADS = 16
HEAD_SIZE = 64
KERNEL = 31
BACK_REACH = 64
FORE_REACH = 8
OFFSETS = 73
CLIPS_MB = 1


negative_fill = -1e30


def passed_along(shard, axis, by):
    peers = lax.axis_size(axis)
    pairs = [(i, i + by) for i in range(peers) if 0 <= i + by < peers]
    return lax.ppermute(shard, axis, pairs)


def layer_norm(rows, scale, shift):
    middle = jnp.mean(rows, -1, keepdims=True)
    centered = rows - middle
    spread = jnp.mean(centered * centered, -1, keepdims=True)
    return centered * lax.rsqrt(spread + 1e-05) * scale + shift


def norm_back(rows, scale, shift, grad):
    unused, pull = jax.vjp(layer_norm, rows, scale, shift)
    return pull(grad)


def glu_gate(doubled):
    half = doubled.shape[-1] // 2
    return doubled[..., :half] * jax.nn.sigmoid(doubled[..., half:])


def post_norm(mixed, scale, shift):
    return jax.nn.silu(layer_norm(mixed, scale, shift))


def depthwise(extended, kernel):
    count = extended.shape[1] - kernel.shape[0] + 1
    return sum((kernel[tap] * extended[:, tap : tap + count] for tap in range(kernel.shape[0])))


def product(left, right):
    return jnp.dot(left, right, preferred_element_type=jnp.float32)


def weight_grad(left, right):
    return lax.dot_general(
        left, right, (((0,), (0,)), ((), ())), preferred_element_type=jnp.float32
    )


def back_product(grad, weight):
    return lax.dot_general(
        grad, weight, (((1,), (1,)), ((), ())), preferred_element_type=jnp.float32
    )


def column_sum(values):
    return jnp.sum(values.astype(jnp.float32), 0)


def feed_forward(hidden, scale, shift, w_in, b_in, w_out, b_out):
    normed = layer_norm(hidden, scale, shift).astype(jnp.bfloat16)
    upper = product(normed, w_in) + b_in
    acted = jax.nn.silu(upper).astype(jnp.bfloat16)
    return (product(acted, w_out) + b_out, (normed, upper, acted))


def feed_back(grad, hidden, scale, shift, w_in, w_out, saved):
    normed, upper, acted = saved
    grad_low = grad.astype(jnp.bfloat16)
    unused, silu_pull = jax.vjp(jax.nn.silu, upper)
    upper_grad = silu_pull(back_product(grad_low, w_out))[0].astype(jnp.bfloat16)
    hidden_grad, scale_grad, shift_grad = norm_back(
        hidden, scale, shift, back_product(upper_grad, w_in)
    )
    return (
        hidden_grad,
        weight_grad(normed, upper_grad),
        weight_grad(acted, grad_low),
        scale_grad,
        shift_grad,
        column_sum(upper_grad),
        column_sum(grad_low),
    )


def offsets_table(query_pos, key_pos):
    offset = jnp.clip(key_pos[None, :] - query_pos[:, None], -BACK_REACH, FORE_REACH) + BACK_REACH
    return (offset[None, :, :] == jnp.arange(OFFSETS, dtype=jnp.int32)[:, None, None]).astype(
        jnp.bfloat16
    )


def relative_rows(query_heads, table_low):
    return jnp.einsum(
        "cihd,rd->chir", query_heads, table_low, preferred_element_type=jnp.float32
    ).astype(jnp.bfloat16)


def attention_scores(query_heads, relative, key_heads, onehot, key_valid):
    dotted = jnp.einsum(
        "cihd,cjhd->chij", query_heads, key_heads, preferred_element_type=jnp.float32
    )
    bias = jnp.einsum("chir,rij->chij", relative, onehot, preferred_element_type=jnp.float32)
    scaled = (dotted + bias) * HEAD_SIZE ** (-0.5)
    return jnp.where(key_valid[:, None, None, :], scaled, negative_fill)


def per_device(
    frames_in,
    clip_lengths,
    out_grad,
    first_up,
    first_down,
    query_weight,
    key_weight,
    value_weight,
    output_weight,
    pointwise_in,
    pointwise_out,
    second_up,
    second_down,
    norm_scales,
    norm_shifts,
    hidden_biases,
    width_biases,
    value_bias,
    relative_table,
    depth_kernel,
):
    columns = (
        lax.all_gather(first_up.astype(jnp.bfloat16), ("coarse", "fine"), axis=1, tiled=True),
        lax.all_gather(first_down.astype(jnp.bfloat16), ("coarse", "fine"), axis=1, tiled=True),
        lax.all_gather(query_weight.astype(jnp.bfloat16), ("coarse", "fine"), axis=1, tiled=True),
        lax.all_gather(key_weight.astype(jnp.bfloat16), ("coarse", "fine"), axis=1, tiled=True),
        lax.all_gather(value_weight.astype(jnp.bfloat16), ("coarse", "fine"), axis=1, tiled=True),
        lax.all_gather(output_weight.astype(jnp.bfloat16), ("coarse", "fine"), axis=1, tiled=True),
        lax.all_gather(pointwise_in.astype(jnp.bfloat16), ("coarse", "fine"), axis=1, tiled=True),
        lax.all_gather(pointwise_out.astype(jnp.bfloat16), ("coarse", "fine"), axis=1, tiled=True),
        lax.all_gather(second_up.astype(jnp.bfloat16), ("coarse", "fine"), axis=1, tiled=True),
        lax.all_gather(second_down.astype(jnp.bfloat16), ("coarse", "fine"), axis=1, tiled=True),
    )
    weights = (
        lax.all_gather(columns[0], "clip", axis=0, tiled=True),
        lax.all_gather(columns[1], "clip", axis=0, tiled=True),
        lax.all_gather(columns[2], "clip", axis=0, tiled=True),
        lax.all_gather(columns[3], "clip", axis=0, tiled=True),
        lax.all_gather(columns[4], "clip", axis=0, tiled=True),
        lax.all_gather(columns[5], "clip", axis=0, tiled=True),
        lax.all_gather(columns[6], "clip", axis=0, tiled=True),
        lax.all_gather(columns[7], "clip", axis=0, tiled=True),
        lax.all_gather(columns[8], "clip", axis=0, tiled=True),
        lax.all_gather(columns[9], "clip", axis=0, tiled=True),
    )
    (
        up_first,
        down_first,
        query_full,
        key_full,
        value_full,
        output_full,
        inner_full,
        outer_full,
        up_second,
        down_second,
    ) = weights
    frames = frames_in.shape[1]
    length = frames * lax.axis_size(("coarse", "fine"))
    rows = CLIPS_MB * frames
    base = lax.axis_index(("coarse", "fine")) * frames
    table_low = relative_table.astype(jnp.bfloat16)
    scale_head = HEAD_SIZE ** (-0.5)
    query_pos = base + jnp.arange(frames, dtype=jnp.int32)
    key_pos = jnp.arange(length, dtype=jnp.int32)
    onehot = offsets_table(query_pos, key_pos)
    totals = [jnp.zeros(matrix.shape, jnp.float32) for matrix in weights]
    scale_total = jnp.zeros_like(norm_scales)
    shift_total = jnp.zeros_like(norm_shifts)
    hidden_total = jnp.zeros_like(hidden_biases)
    width_total = jnp.zeros_like(width_biases)
    value_total = jnp.zeros_like(value_bias)
    table_total = jnp.zeros_like(relative_table)
    kernel_total = jnp.zeros_like(depth_kernel)
    outputs = []
    input_grads = []
    for micro in range(frames_in.shape[0] // CLIPS_MB):
        first_clip = micro * CLIPS_MB
        lengths = clip_lengths[first_clip : first_clip + CLIPS_MB]
        local_valid = query_pos[None, :] < lengths[:, None]
        frame_valid = local_valid.reshape(rows, 1)
        key_valid = key_pos[None, :] < lengths[:, None]
        start_rows = (
            frames_in[first_clip : first_clip + CLIPS_MB].astype(jnp.float32).reshape(rows, D)
        )
        branch_one, first_saved = feed_forward(
            start_rows,
            norm_scales[0],
            norm_shifts[0],
            up_first,
            hidden_biases[0],
            down_first,
            width_biases[0],
        )
        after_first = start_rows + 0.5 * branch_one
        att_normed = layer_norm(after_first, norm_scales[1], norm_shifts[1]).astype(jnp.bfloat16)
        query_rows = (product(att_normed, query_full) + width_biases[1]).astype(jnp.bfloat16)
        key_rows = product(att_normed, key_full).astype(jnp.bfloat16)
        value_rows = (product(att_normed, value_full) + value_bias).astype(jnp.bfloat16)
        key_all, value_all = (
            lax.all_gather(
                key_rows.reshape(CLIPS_MB, frames, D), ("coarse", "fine"), axis=1, tiled=True
            ),
            lax.all_gather(
                value_rows.reshape(CLIPS_MB, frames, D), ("coarse", "fine"), axis=1, tiled=True
            ),
        )
        query_heads = query_rows.reshape(CLIPS_MB, frames, HEADS, HEAD_SIZE)
        key_heads = key_all.reshape(CLIPS_MB, length, HEADS, HEAD_SIZE)
        value_heads = value_all.reshape(CLIPS_MB, length, HEADS, HEAD_SIZE)
        relative = relative_rows(query_heads, table_low)
        scores = attention_scores(query_heads, relative, key_heads, onehot, key_valid)
        top_score = jnp.max(scores, -1, keepdims=True)
        log_total = jnp.log(jnp.sum(jnp.exp(scores - top_score), -1, keepdims=True)) + top_score
        probs = jnp.exp(scores - log_total)
        mixed = (
            jnp.einsum(
                "chij,cjhd->cihd",
                probs.astype(jnp.bfloat16),
                value_heads,
                preferred_element_type=jnp.float32,
            )
            .astype(jnp.bfloat16)
            .reshape(rows, D)
        )
        after_attention = after_first + product(mixed, output_full) + width_biases[2]
        conv_normed = jnp.where(
            frame_valid, layer_norm(after_attention, norm_scales[2], norm_shifts[2]), 0.0
        ).astype(jnp.bfloat16)
        doubled = product(conv_normed, inner_full)
        gated = glu_gate(doubled).astype(jnp.bfloat16).reshape(CLIPS_MB, frames, D)
        carried = passed_along(gated[:, frames - KERNEL + 1 :], ("coarse", "fine"), 1)
        extended = jnp.concatenate([carried, gated], 1).astype(jnp.float32)
        mixed_conv = depthwise(extended, depth_kernel).reshape(rows, D)
        conv_acted = post_norm(mixed_conv, norm_scales[3], norm_shifts[3]).astype(jnp.bfloat16)
        after_conv = after_attention + product(conv_acted, outer_full)
        branch_two, second_saved = feed_forward(
            after_conv,
            norm_scales[4],
            norm_shifts[4],
            up_second,
            hidden_biases[1],
            down_second,
            width_biases[3],
        )
        after_second = after_conv + 0.5 * branch_two
        outputs.append(
            layer_norm(after_second, norm_scales[5], norm_shifts[5])
            .astype(jnp.bfloat16)
            .reshape(CLIPS_MB, frames, D)
        )
        final_grad, final_scale, final_shift = norm_back(
            after_second,
            norm_scales[5],
            norm_shifts[5],
            out_grad[first_clip : first_clip + CLIPS_MB].astype(jnp.float32).reshape(rows, D),
        )
        (
            second_in,
            second_up_g,
            second_down_g,
            second_scale,
            second_shift,
            second_hidden,
            second_width,
        ) = feed_back(
            0.5 * final_grad,
            after_conv,
            norm_scales[4],
            norm_shifts[4],
            up_second,
            down_second,
            second_saved,
        )
        grad_conv = final_grad + second_in
        conv_low = grad_conv.astype(jnp.bfloat16)
        outer_g = weight_grad(conv_acted, conv_low)
        unused, post_pull = jax.vjp(post_norm, mixed_conv, norm_scales[3], norm_shifts[3])
        mixed_g, depth_scale, depth_shift = post_pull(back_product(conv_low, outer_full))
        unused, depth_pull = jax.vjp(depthwise, extended, depth_kernel)
        extended_g, kernel_g = depth_pull(mixed_g.reshape(CLIPS_MB, frames, D))
        returned = passed_along(
            extended_g[:, : KERNEL - 1].astype(jnp.bfloat16), ("coarse", "fine"), -1
        ).astype(jnp.float32)
        own_g = extended_g[:, KERNEL - 1 :]
        gated_g = jnp.concatenate(
            [own_g[:, : frames - KERNEL + 1], own_g[:, frames - KERNEL + 1 :] + returned], 1
        ).reshape(rows, D)
        unused, glu_pull = jax.vjp(glu_gate, doubled)
        doubled_g = glu_pull(gated_g)[0].astype(jnp.bfloat16)
        inner_g = weight_grad(conv_normed, doubled_g)
        normed_g = jnp.where(frame_valid, back_product(doubled_g, inner_full), 0.0)
        conv_in_g, conv_scale, conv_shift = norm_back(
            after_attention, norm_scales[2], norm_shifts[2], normed_g
        )
        grad_att = grad_conv + conv_in_g
        att_low = grad_att.astype(jnp.bfloat16)
        output_g = weight_grad(mixed, att_low)
        mixed_grad = back_product(att_low, output_full).astype(jnp.bfloat16)
        mixed_heads = mixed_grad.reshape(CLIPS_MB, frames, HEADS, HEAD_SIZE)
        scores = attention_scores(query_heads, relative, key_heads, onehot, key_valid)
        probs = jnp.exp(scores - log_total)
        probs_g = jnp.einsum(
            "cihd,cjhd->chij", mixed_heads, value_heads, preferred_element_type=jnp.float32
        )
        inner_sum = jnp.sum(probs * probs_g, -1, keepdims=True)
        scores_g = (probs * (probs_g - inner_sum)).astype(jnp.bfloat16)
        relative_g = (
            jnp.einsum("chij,rij->chir", scores_g, onehot, preferred_element_type=jnp.float32)
            * scale_head
        ).astype(jnp.bfloat16)
        query_g = jnp.einsum(
            "chij,cjhd->cihd", scores_g, key_heads, preferred_element_type=jnp.float32
        ) * scale_head + jnp.einsum(
            "chir,rd->cihd", relative_g, table_low, preferred_element_type=jnp.float32
        )
        table_g = jnp.einsum(
            "chir,cihd->rd", relative_g, query_heads, preferred_element_type=jnp.float32
        )
        key_terms = (
            jnp.einsum("chij,cihd->cjhd", scores_g, query_heads, preferred_element_type=jnp.float32)
            * scale_head
        )
        value_terms = jnp.einsum(
            "chij,cihd->cjhd",
            probs.astype(jnp.bfloat16),
            mixed_heads,
            preferred_element_type=jnp.float32,
        )
        key_g, value_g = (
            lax.psum_scatter(
                key_terms.reshape(CLIPS_MB, length, D).astype(jnp.bfloat16),
                ("coarse", "fine"),
                scatter_dimension=1,
                tiled=True,
            ).astype(jnp.float32),
            lax.psum_scatter(
                value_terms.reshape(CLIPS_MB, length, D).astype(jnp.bfloat16),
                ("coarse", "fine"),
                scatter_dimension=1,
                tiled=True,
            ).astype(jnp.float32),
        )
        key_low = key_g.reshape(rows, D).astype(jnp.bfloat16)
        value_low = value_g.reshape(rows, D).astype(jnp.bfloat16)
        query_low = query_g.reshape(rows, D).astype(jnp.bfloat16)
        query_wg = weight_grad(att_normed, query_low)
        key_wg = weight_grad(att_normed, key_low)
        value_wg = weight_grad(att_normed, value_low)
        normed_back = (
            back_product(query_low, query_full)
            + back_product(key_low, key_full)
            + back_product(value_low, value_full)
        )
        att_in_g, att_scale, att_shift = norm_back(
            after_first, norm_scales[1], norm_shifts[1], normed_back
        )
        grad_first = grad_att + att_in_g
        first_in, first_up_g, first_down_g, first_scale, first_shift, first_hidden, first_width = (
            feed_back(
                0.5 * grad_first,
                start_rows,
                norm_scales[0],
                norm_shifts[0],
                up_first,
                down_first,
                first_saved,
            )
        )
        input_grads.append(
            (grad_first + first_in).astype(jnp.bfloat16).reshape(CLIPS_MB, frames, D)
        )
        fresh = [
            first_up_g,
            first_down_g,
            query_wg,
            key_wg,
            value_wg,
            output_g,
            inner_g,
            outer_g,
            second_up_g,
            second_down_g,
        ]
        totals = [running + update for running, update in zip(totals, fresh)]
        scale_total = scale_total + jnp.stack(
            [first_scale, att_scale, conv_scale, depth_scale, second_scale, final_scale]
        )
        shift_total = shift_total + jnp.stack(
            [first_shift, att_shift, conv_shift, depth_shift, second_shift, final_shift]
        )
        hidden_total = hidden_total + jnp.stack([first_hidden, second_hidden])
        width_total = width_total + jnp.stack(
            [first_width, column_sum(query_low), column_sum(att_low), second_width]
        )
        value_total = value_total + column_sum(value_low)
        table_total = table_total + table_g
        kernel_total = kernel_total + kernel_g
    row_sums = (
        lax.psum_scatter(
            totals[0].astype(jnp.bfloat16), "clip", scatter_dimension=0, tiled=True
        ).astype(jnp.float32),
        lax.psum_scatter(
            totals[1].astype(jnp.bfloat16), "clip", scatter_dimension=0, tiled=True
        ).astype(jnp.float32),
        lax.psum_scatter(
            totals[2].astype(jnp.bfloat16), "clip", scatter_dimension=0, tiled=True
        ).astype(jnp.float32),
        lax.psum_scatter(
            totals[3].astype(jnp.bfloat16), "clip", scatter_dimension=0, tiled=True
        ).astype(jnp.float32),
        lax.psum_scatter(
            totals[4].astype(jnp.bfloat16), "clip", scatter_dimension=0, tiled=True
        ).astype(jnp.float32),
        lax.psum_scatter(
            totals[5].astype(jnp.bfloat16), "clip", scatter_dimension=0, tiled=True
        ).astype(jnp.float32),
        lax.psum_scatter(
            totals[6].astype(jnp.bfloat16), "clip", scatter_dimension=0, tiled=True
        ).astype(jnp.float32),
        lax.psum_scatter(
            totals[7].astype(jnp.bfloat16), "clip", scatter_dimension=0, tiled=True
        ).astype(jnp.float32),
        lax.psum_scatter(
            totals[8].astype(jnp.bfloat16), "clip", scatter_dimension=0, tiled=True
        ).astype(jnp.float32),
        lax.psum_scatter(
            totals[9].astype(jnp.bfloat16), "clip", scatter_dimension=0, tiled=True
        ).astype(jnp.float32),
    )
    block_sums = (
        lax.psum_scatter(
            row_sums[0].astype(jnp.bfloat16), ("coarse", "fine"), scatter_dimension=1, tiled=True
        ).astype(jnp.float32),
        lax.psum_scatter(
            row_sums[1].astype(jnp.bfloat16), ("coarse", "fine"), scatter_dimension=1, tiled=True
        ).astype(jnp.float32),
        lax.psum_scatter(
            row_sums[2].astype(jnp.bfloat16), ("coarse", "fine"), scatter_dimension=1, tiled=True
        ).astype(jnp.float32),
        lax.psum_scatter(
            row_sums[3].astype(jnp.bfloat16), ("coarse", "fine"), scatter_dimension=1, tiled=True
        ).astype(jnp.float32),
        lax.psum_scatter(
            row_sums[4].astype(jnp.bfloat16), ("coarse", "fine"), scatter_dimension=1, tiled=True
        ).astype(jnp.float32),
        lax.psum_scatter(
            row_sums[5].astype(jnp.bfloat16), ("coarse", "fine"), scatter_dimension=1, tiled=True
        ).astype(jnp.float32),
        lax.psum_scatter(
            row_sums[6].astype(jnp.bfloat16), ("coarse", "fine"), scatter_dimension=1, tiled=True
        ).astype(jnp.float32),
        lax.psum_scatter(
            row_sums[7].astype(jnp.bfloat16), ("coarse", "fine"), scatter_dimension=1, tiled=True
        ).astype(jnp.float32),
        lax.psum_scatter(
            row_sums[8].astype(jnp.bfloat16), ("coarse", "fine"), scatter_dimension=1, tiled=True
        ).astype(jnp.float32),
        lax.psum_scatter(
            row_sums[9].astype(jnp.bfloat16), ("coarse", "fine"), scatter_dimension=1, tiled=True
        ).astype(jnp.float32),
    )
    small_sums = lax.psum(
        (
            scale_total,
            shift_total,
            hidden_total,
            width_total,
            value_total,
            table_total,
            kernel_total,
        ),
        ("clip", "coarse", "fine"),
    )
    return (
        jnp.concatenate(outputs, 0),
        jnp.concatenate(input_grads, 0),
        block_sums[0],
        block_sums[1],
        block_sums[2],
        block_sums[3],
        block_sums[4],
        block_sums[5],
        block_sums[6],
        block_sums[7],
        block_sums[8],
        block_sums[9],
        small_sums[0],
        small_sums[1],
        small_sums[2],
        small_sums[3],
        small_sums[4],
        small_sums[5],
        small_sums[6],
    )


def solution(mesh):
    in_specs = (
        P("clip", ("coarse", "fine"), None),
        P("clip"),
        P("clip", ("coarse", "fine"), None),
        P("clip", ("coarse", "fine")),
        P("clip", ("coarse", "fine")),
        P("clip", ("coarse", "fine")),
        P("clip", ("coarse", "fine")),
        P("clip", ("coarse", "fine")),
        P("clip", ("coarse", "fine")),
        P("clip", ("coarse", "fine")),
        P("clip", ("coarse", "fine")),
        P("clip", ("coarse", "fine")),
        P("clip", ("coarse", "fine")),
        P(),
        P(),
        P(),
        P(),
        P(),
        P(),
        P(),
    )
    out_specs = (
        P("clip", ("coarse", "fine"), None),
        P("clip", ("coarse", "fine"), None),
        P("clip", ("coarse", "fine")),
        P("clip", ("coarse", "fine")),
        P("clip", ("coarse", "fine")),
        P("clip", ("coarse", "fine")),
        P("clip", ("coarse", "fine")),
        P("clip", ("coarse", "fine")),
        P("clip", ("coarse", "fine")),
        P("clip", ("coarse", "fine")),
        P("clip", ("coarse", "fine")),
        P("clip", ("coarse", "fine")),
        P(),
        P(),
        P(),
        P(),
        P(),
        P(),
        P(),
    )
    return jax.shard_map(
        per_device, mesh=mesh, in_specs=in_specs, out_specs=out_specs, check_vma=False
    )
```

profile of v0, /device:TPU:0, one launch (start us, length us, event | category | flops | bytes accessed | tf_op | source)
XLA Modules:
  0.0 2981.0 jit_solution(3502474634366375128)
XLA Ops:
  11.1 53.4 %all-gather.28.cloned.1.call-done = bf16[256,4096]{1,0:T(8,128)(2,1)} async-done(((bf16[256,512]{1,0:T(8,128)(2,1)}), bf16[256,4096]{1,0:T(8,128)(2,1)}) %all-gather.28.cloned.1.call-update) | async-done | bytes 2097168 | tf_op jit(solution)/shard_map/all_gather | solution.py:142
  64.6 51.8 %all-gather.32.cloned.1.call-done = bf16[1024,1024]{1,0:T(8,128)(2,1)} async-done(((bf16[1024,128]{1,0:T(8,128)(2,1)}), bf16[1024,1024]{1,0:T(8,128)(2,1)}) %all-gather.32.cloned.1.call-update) | async-done | bytes 2097168 | tf_op jit(solution)/shard_map/all_gather | solution.py:143
  116.5 28.7 all_gather.87
  145.3 28.4 all_gather.82
  176.3 28.4 all_gather.85
  212.2 22.0 all-gather.34.cloned.1.call-done
  261.3 21.0 all-gather.36.cloned.1.call-done
  286.1 29.1 all_gather.90
  315.3 12.1 all-gather.44.cloned.1.call-done
  336.6 30.4 %all_gather.94 = bf16[256,1024]{1,0:T(8,128)(2,1)} all-gather(bf16[256,128]{1,0:T(8,128)(2,1)S(1)} %convert_element_type.741), channel_id=1, replica_groups=mesh['clip'=4,'coarse'=4,'fine'=2] {'coarse','fine'}, dimensions={1}, use_global_device_ids=true | all-gather | bytes 589824 | tf_op jit(solution)/shard_map/all_gather | solution.py:149
  367.0 17.4 all-gather.50.cloned.1.call-done
  396.0 40.7 %all-gather.54.cloned.1.call-done = bf16[1024,1024]{1,0:T(8,128)(2,1)} async-done(((bf16[1024,128]{1,0:T(8,128)(2,1)}), bf16[1024,1024]{1,0:T(8,128)(2,1)}) %all-gather.54.cloned.1.call-update) | async-done | bytes 2097168 | tf_op jit(solution)/shard_map/all_gather | solution.py:151
  436.7 22.1 all-gather.38.cloned.1.call-done
  513.2 12.3 fusion.434
  525.6 34.6 %all-gather.58.cloned.1.call-done = bf16[1024,1024]{1,0:T(8,128)(2,1)} async-done(((bf16[128,1024]{1,0:T(8,128)(2,1)}), bf16[1024,1024]{1,0:T(8,128)(2,1)}) %all-gather.58.cloned.1.call-update) | async-done | bytes 2097168 | tf_op jit(solution)/shard_map/all_gather | solution.py:223
  585.3 33.5 %all-gather.46.cloned.1.call-done = bf16[1024,2048]{1,0:T(8,128)(2,1)} async-done(((bf16[256,2048]{1,0:T(8,128)(2,1)}), bf16[1024,2048]{1,0:T(8,128)(2,1)}) %all-gather.46.cloned.1.call-update) | async-done | bytes 4194320 | tf_op jit(solution)/shard_map/all_gather | solution.py:160
  628.3 41.7 %all-gather.64.cloned.1.call-done = bf16[1024,1024]{1,0:T(8,128)(2,1)} async-done(((bf16[128,1024]{1,0:T(8,128)(2,1)}), bf16[1024,1024]{1,0:T(8,128)(2,1)}) %all-gather.64.cloned.1.call-update) | async-done | bytes 2097168 | tf_op jit(solution)/shard_map/all_gather | solution.py:220
  673.1 46.7 %all-gather.62.cloned.1.call-done = bf16[1024,1024]{1,0:T(8,128)(2,1)} async-done(((bf16[128,1024]{1,0:T(8,128)(2,1)}), bf16[1024,1024]{1,0:T(8,128)(2,1)}) %all-gather.62.cloned.1.call-update) | async-done | bytes 2097168 | tf_op jit(solution)/shard_map/all_gather | solution.py:223
  746.8 23.5 all-gather.68.cloned.1.call-done
  774.4 46.3 %all-gather.66.cloned.1.call-done = bf16[1024,1024]{1,0:T(8,128)(2,1)} async-done(((bf16[128,1024]{1,0:T(8,128)(2,1)}), bf16[1024,1024]{1,0:T(8,128)(2,1)}) %all-gather.66.cloned.1.call-update) | async-done | bytes 2097168 | tf_op jit(solution)/shard_map/all_gather | solution.py:223
  855.2 47.9 %all-gather.52.cloned.1.call-done = bf16[1024,4096]{1,0:T(8,128)(2,1)} async-done(((bf16[256,4096]{1,0:T(8,128)(2,1)}), bf16[1024,4096]{1,0:T(8,128)(2,1)}) %all-gather.52.cloned.1.call-update) | async-done | bytes 8388624 | tf_op jit(solution)/shard_map/all_gather | solution.py:162
  909.4 53.6 %all-gather.56.cloned.1.call-done = bf16[4096,1024]{1,0:T(8,128)(2,1)} async-done(((bf16[1024,1024]{1,0:T(8,128)(2,1)}), bf16[4096,1024]{1,0:T(8,128)(2,1)}) %all-gather.56.cloned.1.call-update) | async-done | bytes 8388624 | tf_op jit(solution)/shard_map/all_gather | solution.py:163
  1111.2 10.9 copy.144
  1284.2 25.7 reduce-scatter.89.cloned.1.call-done
  1315.3 65.0 %reduce-scatter.79.cloned.1.call-done = bf16[128,1024]{1,0:T(8,128)(2,1)} async-done(((bf16[1024,1024]{1,0:T(8,128)(2,1)}), bf16[128,1024]{1,0:T(8,128)(2,1)}) %reduce-scatter.79.cloned.1.call-update) | async-done | bytes 262160
  1382.0 68.6 %reduce-scatter.83.cloned.1.call-done = bf16[128,1024]{1,0:T(8,128)(2,1)} async-done(((bf16[1024,1024]{1,0:T(8,128)(2,1)}), bf16[128,1024]{1,0:T(8,128)(2,1)}) %reduce-scatter.83.cloned.1.call-update) | async-done | bytes 262160
  1452.2 68.4 %reduce-scatter.87.cloned.1.call-done = bf16[128,1024]{1,0:T(8,128)(2,1)} async-done(((bf16[1024,1024]{1,0:T(8,128)(2,1)}), bf16[128,1024]{1,0:T(8,128)(2,1)}) %reduce-scatter.87.cloned.1.call-update) | async-done | bytes 262160
  1550.5 15.7 add_convert_fusion
  1585.7 15.8 add_convert_fusion.1
  1630.7 16.3 add_convert_fusion.2
  1684.1 15.8 add_convert_fusion.3
  1711.1 25.9 reduce-scatter.67.cloned.1.call-done
  1737.0 74.2 %reduce-scatter.77.cloned.1.call-done = bf16[1024,1024]{1,0:T(8,128)(2,1)} async-done(((bf16[4096,1024]{1,0:T(8,128)(2,1)}), bf16[1024,1024]{1,0:T(8,128)(2,1)}) %reduce-scatter.77.cloned.1.call-update) | async-done | bytes 2097168 | tf_op jit(solution)/shard_map/reduce_scatter | solution.py:446
  1815.3 70.5 %reduce-scatter.73.cloned.1.call-done = bf16[256,4096]{1,0:T(8,128)(2,1)} async-done(((bf16[1024,4096]{1,0:T(8,128)(2,1)}), bf16[256,4096]{1,0:T(8,128)(2,1)}) %reduce-scatter.73.cloned.1.call-update) | async-done | bytes 2097168 | tf_op jit(solution)/shard_map/reduce_scatter | solution.py:443
  1885.9 74.1 %reduce-scatter.57.cloned.1.call-done = bf16[1024,1024]{1,0:T(8,128)(2,1)} async-done(((bf16[4096,1024]{1,0:T(8,128)(2,1)}), bf16[1024,1024]{1,0:T(8,128)(2,1)}) %reduce-scatter.57.cloned.1.call-update) | async-done | bytes 2097168 | tf_op jit(solution)/shard_map/reduce_scatter | solution.py:422
  1963.9 70.3 %reduce-scatter.53.cloned.1.call-done = bf16[256,4096]{1,0:T(8,128)(2,1)} async-done(((bf16[1024,4096]{1,0:T(8,128)(2,1)}), bf16[256,4096]{1,0:T(8,128)(2,1)}) %reduce-scatter.53.cloned.1.call-update) | async-done | bytes 2097168 | tf_op jit(solution)/shard_map/reduce_scatter | solution.py:419
  2074.2 25.4 reduce-scatter.101.cloned.1.call-done
  2101.2 62.9 %reduce-scatter.99.cloned.1.call-done = bf16[128,256]{1,0:T(8,128)(2,1)} async-done(((bf16[1024,256]{1,0:T(8,128)(2,1)}), bf16[128,256]{1,0:T(8,128)(2,1)}) %reduce-scatter.99.cloned.1.call-update) | async-done | bytes 65552
  2165.8 63.3 %reduce-scatter.93.cloned.1.call-done = bf16[128,256]{1,0:T(8,128)(2,1)} async-done(((bf16[1024,256]{1,0:T(8,128)(2,1)}), bf16[128,256]{1,0:T(8,128)(2,1)}) %reduce-scatter.93.cloned.1.call-update) | async-done | bytes 65552
  2230.7 63.0 %reduce-scatter.97.cloned.1.call-done = bf16[128,256]{1,0:T(8,128)(2,1)} async-done(((bf16[1024,256]{1,0:T(8,128)(2,1)}), bf16[128,256]{1,0:T(8,128)(2,1)}) %reduce-scatter.97.cloned.1.call-update) | async-done | bytes 65552
  2295.3 62.7 %reduce-scatter.95.cloned.1.call-done = bf16[128,256]{1,0:T(8,128)(2,1)} async-done(((bf16[1024,256]{1,0:T(8,128)(2,1)}), bf16[128,256]{1,0:T(8,128)(2,1)}) %reduce-scatter.95.cloned.1.call-update) | async-done | bytes 65552
  2359.7 65.0 %reduce-scatter.69.cloned.1.call-done = bf16[256,256]{1,0:T(8,128)(2,1)} async-done(((bf16[256,2048]{1,0:T(8,128)(2,1)}), bf16[256,256]{1,0:T(8,128)(2,1)}) %reduce-scatter.69.cloned.1.call-update) | async-done | bytes 131088 | tf_op jit(solution)/shard_map/reduce_scatter | solution.py:469
  2426.2 68.7 %reduce-scatter.103.cloned.1.call-done = bf16[128,1024]{1,0:T(8,128)(2,1)} async-done(((bf16[1024,1024]{1,0:T(8,128)(2,1)}), bf16[128,1024]{1,0:T(8,128)(2,1)}) %reduce-scatter.103.cloned.1.call-update) | async-done | bytes 262160
  2496.9 68.5 %reduce-scatter.75.cloned.1.call-done = bf16[256,512]{1,0:T(8,128)(2,1)} async-done(((bf16[256,4096]{1,0:T(8,128)(2,1)}), bf16[256,512]{1,0:T(8,128)(2,1)}) %reduce-scatter.75.cloned.1.call-update) | async-done | bytes 262160 | tf_op jit(solution)/shard_map/reduce_scatter | solution.py:475
  2567.3 68.3 %reduce-scatter.91.cloned.1.call-done = bf16[128,1024]{1,0:T(8,128)(2,1)} async-done(((bf16[1024,1024]{1,0:T(8,128)(2,1)}), bf16[128,1024]{1,0:T(8,128)(2,1)}) %reduce-scatter.91.cloned.1.call-update) | async-done | bytes 262160
  2637.5 68.7 %reduce-scatter.55.cloned.1.call-done = bf16[256,512]{1,0:T(8,128)(2,1)} async-done(((bf16[256,4096]{1,0:T(8,128)(2,1)}), bf16[256,512]{1,0:T(8,128)(2,1)}) %reduce-scatter.55.cloned.1.call-update) | async-done | bytes 262160 | tf_op jit(solution)/shard_map/reduce_scatter | solution.py:451
  2708.1 125.6 %all-reduce.196.cloned.1.call-done = f32[31,1024]{1,0:T(8,128)} async-done(((f32[31,1024]{1,0:T(8,128)}), f32[31,1024]{1,0:T(8,128)}) %all-reduce.196.cloned.1.call-update) | async-done | bytes 126992 | tf_op jit(solution)/shard_map/psum | solution.py:482
  2833.7 130.4 %all-reduce.198.cloned.1.call-done = (f32[6,1024]{1,0:T(8,128)}, f32[6,1024]{1,0:T(8,128)}, f32[2,4096]{1,0:T(2,128)}, f32[4,1024]{1,0:T(4,128)}, f32[1024]{0:T(1024)}, /*index=5*/f32[73,64]{0,1:T(8,128)}) async-done(((f32[6,1024]{1,0:T(8,128)}, f32[6,1024]{1,0:T(8,128)}, f32[2,4096]{1,0:T(2,128)}, f32[4,1024]{1,0:T(4,128)}, f32[1024]{0:T(1024)}, /*index=5*/f32[73,64]{0,1:T(8,128)}), (f32[6,1024]{1,0:T(8,128)}, ...) | async-done | bytes 121104 | tf_op jit(solution)/shard_map/psum | solution.py:482
  (1398 shorter events, 743.6 us)
Async XLA Ops:
  11.0 196.4 %all-gather.30.cloned.1.call-start = ((), (), s32[]{:S(2)}) async-start(), calls=%async_computation.27 | async-start | bytes 10485760 | tf_op jit(solution)/shard_map/all_gather | solution.py:154
  64.5 169.7 %all-gather.34.cloned.1.call-start = ((), (), s32[]{:S(2)}) async-start(), calls=%async_computation.29 | async-start | bytes 10485760 | tf_op jit(solution)/shard_map/all_gather | solution.py:155
  116.5 141.8 %all-gather.40.cloned.1.call-start = ((), (), s32[]{:S(2)}) async-start(), calls=%async_computation.32 | async-start | bytes 2621440 | tf_op jit(solution)/shard_map/all_gather | solution.py:157
  173.8 153.6 %all-gather.44.cloned.1.call-start = ((), (), s32[]{:S(2)}) async-start(), calls=%async_computation.34 | async-start | bytes 1179648 | tf_op jit(solution)/shard_map/all_gather | solution.py:148
  174.6 209.9 %all-gather.50.cloned.1.call-start = ((), (), s32[]{:S(2)}) async-start(), calls=%async_computation.37 | async-start | bytes 2359296 | tf_op jit(solution)/shard_map/all_gather | solution.py:150
  175.4 261.3 %all-gather.54.cloned.1.call-start = ((), (), s32[]{:S(2)}) async-start(), calls=%async_computation.39 | async-start | bytes 2359296 | tf_op jit(solution)/shard_map/all_gather | solution.py:151
  176.2 282.7 %all-gather.38.cloned.1.call-start = ((), (), s32[]{:S(2)}) async-start(), calls=%async_computation.31 | async-start | bytes 2621440 | tf_op jit(solution)/shard_map/all_gather | solution.py:156
  204.7 305.6 %all-gather.60.cloned.1.call-start = ((), (), s32[]{:S(2)}) async-start(), calls=%async_computation.56 | async-start | bytes 2359296 | tf_op jit(solution)/shard_map/all_gather | solution.py:220
  261.0 299.1 %all-gather.58.cloned.1.call-start = ((), (), s32[]{:S(2)}) async-start(), calls=%async_computation.55 | async-start | bytes 2359296 | tf_op jit(solution)/shard_map/all_gather | solution.py:223
  285.2 297.7 %all-gather.42.cloned.1.call-start = ((), (), s32[]{:S(2)}) async-start(), calls=%async_computation.33 | async-start | bytes 2621440 | tf_op jit(solution)/shard_map/all_gather | solution.py:159
  315.3 303.5 %all-gather.46.cloned.1.call-start = ((), (), s32[]{:S(2)}) async-start(), calls=%async_computation.35 | async-start | bytes 5242880 | tf_op jit(solution)/shard_map/all_gather | solution.py:160
  327.5 342.6 %all-gather.64.cloned.1.call-start = ((), (), s32[]{:S(2)}) async-start(), calls=%async_computation.58 | async-start | bytes 2359296 | tf_op jit(solution)/shard_map/all_gather | solution.py:220
  330.3 389.5 %all-gather.62.cloned.1.call-start = ((), (), s32[]{:S(2)}) async-start(), calls=%async_computation.57 | async-start | bytes 2359296 | tf_op jit(solution)/shard_map/all_gather | solution.py:223
  331.5 438.7 %all-gather.68.cloned.1.call-start = ((), (), s32[]{:S(2)}) async-start(), calls=%async_computation.60 | async-start | bytes 2359296 | tf_op jit(solution)/shard_map/all_gather | solution.py:220
  334.4 486.3 %all-gather.66.cloned.1.call-start = ((), (), s32[]{:S(2)}) async-start(), calls=%async_computation.59 | async-start | bytes 2359296 | tf_op jit(solution)/shard_map/all_gather | solution.py:223
  335.6 515.7 %all-gather.48.cloned.1.call-start = ((), (), s32[]{:S(2)}) async-start(), calls=%async_computation.36 | async-start | bytes 2621440 | tf_op jit(solution)/shard_map/all_gather | solution.py:161
  367.0 536.1 %all-gather.52.cloned.1.call-start = ((), (), s32[]{:S(2)}) async-start(), calls=%async_computation.38 | async-start | bytes 10485760 | tf_op jit(solution)/shard_map/all_gather | solution.py:162
  384.5 578.5 %all-gather.56.cloned.1.call-start = ((), (), s32[]{:S(2)}) async-start(), calls=%async_computation.40 | async-start | bytes 10485760 | tf_op jit(solution)/shard_map/all_gather | solution.py:163
  436.7 844.1 %reduce-scatter.81.cloned.1.call-start = ((), (), s32[]{:S(2)}) async-start(), calls=%async_computation.62 | async-start | bytes 2359296
  624.2 222.3 %collective-permute-start = (bf16[1,30,1024]{2,1,0:T(8,128)(2,1)}, bf16[1,30,1024]{2,1,0:T(8,128)(2,1)}, u32[]{:S(2)}, u32[]{:S(2)}) collective-permute-start(bf16[1,30,1024]{2,1,0:T(8,128)(2,1)} %slice.1001), channel_id=1, source_target_pairs={{0,1},{1,2},{2,3},{3,4},{4,5},{5,6},{6,7},{8,9},{9,10},{10,11},{11... | collective-permute-start | bytes 184328 | tf_op jit(solution)/shard_map/ppermute | solution.py:22
  743.6 225.1 %collective-permute-start.1 = (bf16[1,30,1024]{2,1,0:T(8,128)(2,1)}, bf16[1,30,1024]{2,1,0:T(8,128)(2,1)}, u32[]{:S(2)}, u32[]{:S(2)}) collective-permute-start(bf16[1,30,1024]{2,1,0:T(8,128)(2,1)} %slice.1035), channel_id=1, source_target_pairs={{0,1},{1,2},{2,3},{3,4},{4,5},{5,6},{6,7},{8,9},{9,10},{10,11},{11... | collective-permute-start | bytes 184328 | tf_op jit(solution)/shard_map/ppermute | solution.py:22
  1099.5 183.0 %reduce-scatter.85.cloned.1.call-start = ((), (), s32[]{:S(2)}) async-start(), calls=%async_computation.64 | async-start | bytes 2359296
  1126.6 183.3 %reduce-scatter.89.cloned.1.call-start = ((), (), s32[]{:S(2)}) async-start(), calls=%async_computation.66 | async-start | bytes 2359296
  1149.6 230.7 %reduce-scatter.79.cloned.1.call-start = ((), (), s32[]{:S(2)}) async-start(), calls=%async_computation.61 | async-start | bytes 2359296
  1174.9 275.6 %reduce-scatter.83.cloned.1.call-start = ((), (), s32[]{:S(2)}) async-start(), calls=%async_computation.63 | async-start | bytes 2359296
  1200.8 319.9 %reduce-scatter.87.cloned.1.call-start = ((), (), s32[]{:S(2)}) async-start(), calls=%async_computation.65 | async-start | bytes 2359296
  1224.9 475.1 %reduce-scatter.71.cloned.1.call-start = ((), (), s32[]{:S(2)}) async-start(), calls=%async_computation.50 | async-start | bytes 2621440 | tf_op jit(solution)/shard_map/reduce_scatter | solution.py:440
  1229.1 473.3 %reduce-scatter.65.cloned.1.call-start = ((), (), s32[]{:S(2)}) async-start(), calls=%async_computation.47 | async-start | bytes 2621440 | tf_op jit(solution)/shard_map/reduce_scatter | solution.py:434
  1253.0 451.6 %reduce-scatter.59.cloned.1.call-start = ((), (), s32[]{:S(2)}) async-start(), calls=%async_computation.44 | async-start | bytes 2621440 | tf_op jit(solution)/shard_map/reduce_scatter | solution.py:425
  1280.3 426.5 %reduce-scatter.63.cloned.1.call-start = ((), (), s32[]{:S(2)}) async-start(), calls=%async_computation.46 | async-start | bytes 2621440 | tf_op jit(solution)/shard_map/reduce_scatter | solution.py:431
  1315.3 393.6 %reduce-scatter.61.cloned.1.call-start = ((), (), s32[]{:S(2)}) async-start(), calls=%async_computation.45 | async-start | bytes 2621440 | tf_op jit(solution)/shard_map/reduce_scatter | solution.py:428
  1526.0 210.9 %reduce-scatter.67.cloned.1.call-start = ((), (), s32[]{:S(2)}) async-start(), calls=%async_computation.48 | async-start | bytes 5242880 | tf_op jit(solution)/shard_map/reduce_scatter | solution.py:437
  1532.5 278.8 %reduce-scatter.77.cloned.1.call-start = ((), (), s32[]{:S(2)}) async-start(), calls=%async_computation.53 | async-start | bytes 10485760 | tf_op jit(solution)/shard_map/reduce_scatter | solution.py:446
  1566.3 319.5 %reduce-scatter.73.cloned.1.call-start = ((), (), s32[]{:S(2)}) async-start(), calls=%async_computation.51 | async-start | bytes 10485760 | tf_op jit(solution)/shard_map/reduce_scatter | solution.py:443
  1601.5 358.4 %reduce-scatter.57.cloned.1.call-start = ((), (), s32[]{:S(2)}) async-start(), calls=%async_computation.43 | async-start | bytes 10485760 | tf_op jit(solution)/shard_map/reduce_scatter | solution.py:422
  1647.1 387.2 %reduce-scatter.53.cloned.1.call-start = ((), (), s32[]{:S(2)}) async-start(), calls=%async_computation.41 | async-start | bytes 10485760 | tf_op jit(solution)/shard_map/reduce_scatter | solution.py:419
  1700.0 399.6 %reduce-scatter.101.cloned.1.call-start = ((), (), s32[]{:S(2)}) async-start(), calls=%async_computation.72 | async-start | bytes 589824
  1702.4 461.8 %reduce-scatter.99.cloned.1.call-start = ((), (), s32[]{:S(2)}) async-start(), calls=%async_computation.71 | async-start | bytes 589824
  1704.6 524.5 %reduce-scatter.93.cloned.1.call-start = ((), (), s32[]{:S(2)}) async-start(), calls=%async_computation.68 | async-start | bytes 589824
  1706.7 587.0 %reduce-scatter.97.cloned.1.call-start = ((), (), s32[]{:S(2)}) async-start(), calls=%async_computation.70 | async-start | bytes 589824
  1708.8 649.2 %reduce-scatter.95.cloned.1.call-start = ((), (), s32[]{:S(2)}) async-start(), calls=%async_computation.69 | async-start | bytes 589824
  1711.0 713.6 %reduce-scatter.69.cloned.1.call-start = ((), (), s32[]{:S(2)}) async-start(), calls=%async_computation.49 | async-start | bytes 1179648 | tf_op jit(solution)/shard_map/reduce_scatter | solution.py:469
  1737.0 758.0 %reduce-scatter.103.cloned.1.call-start = ((), (), s32[]{:S(2)}) async-start(), calls=%async_computation.73 | async-start | bytes 2359296
  1815.2 750.2 %reduce-scatter.75.cloned.1.call-start = ((), (), s32[]{:S(2)}) async-start(), calls=%async_computation.52 | async-start | bytes 2359296 | tf_op jit(solution)/shard_map/reduce_scatter | solution.py:475
  1885.8 749.7 %reduce-scatter.91.cloned.1.call-start = ((), (), s32[]{:S(2)}) async-start(), calls=%async_computation.67 | async-start | bytes 2359296
  1963.9 742.4 %reduce-scatter.55.cloned.1.call-start = ((), (), s32[]{:S(2)}) async-start(), calls=%async_computation.42 | async-start | bytes 2359296 | tf_op jit(solution)/shard_map/reduce_scatter | solution.py:451
  2034.3 799.3 %all-reduce.196.cloned.1.call-start = ((), (), s32[]{:S(2)}) async-start(), calls=%async_computation.54 | async-start | bytes 262144 | tf_op jit(solution)/shard_map/psum | solution.py:482
  2043.8 920.2 %all-reduce.198.cloned.1.call-start = ((), (), s32[]{:S(2)}) async-start(), calls=%async_computation.74 | async-start | bytes 303104 | tf_op jit(solution)/shard_map/psum | solution.py:482
  (447 other events, 9652.1 us)
Sparse Core Ops, SparseCore 0:
  10.7 53.7 all-gather.27
  67.1 49.2 all-gather.31
  117.9 56.4 all-gather.29
  175.9 58.2 all-gather.33
  235.6 22.5 all-gather.39
  259.6 22.5 all-gather.35
  284.9 42.5 all-gather.43
  330.1 54.3 all-gather.49
  387.1 49.5 all-gather.53
  461.0 49.2 all-gather.59
  512.3 47.7 all-gather.57
  561.7 21.1 all-gather.41
  584.3 34.4 all-gather.45
  620.7 49.2 all-gather.63
  672.0 47.7 all-gather.61
  721.8 48.4 all-gather.67
  772.8 47.8 all-gather.65
  822.2 21.0 all-gather.47
  844.7 58.2 all-gather.51
  904.6 58.3 all-gather.55
  1099.6 69.6 reduce-scatter.80
  1172.8 66.8 reduce-scatter.84
  1243.1 66.7 reduce-scatter.88
  1313.4 66.7 reduce-scatter.78
  1383.7 66.8 reduce-scatter.82
  1453.9 66.6 reduce-scatter.86
  1523.2 30.4 reduce-scatter.70
  1556.3 31.4 reduce-scatter.64
  1590.2 31.4 reduce-scatter.58
  1624.3 31.4 reduce-scatter.62
  1658.4 31.4 reduce-scatter.60
  1692.4 44.5 reduce-scatter.66
  1739.5 71.6 reduce-scatter.76
  1814.0 71.6 reduce-scatter.72
  1888.2 71.7 reduce-scatter.56
  1962.5 71.6 reduce-scatter.52
  2037.6 61.9 reduce-scatter.100
  2103.2 60.9 reduce-scatter.98
  2168.1 60.9 reduce-scatter.92
  2232.8 60.8 reduce-scatter.96
  2297.0 60.9 reduce-scatter.94
  2361.7 62.9 reduce-scatter.68
  2428.1 66.7 reduce-scatter.102
  2498.3 67.0 reduce-scatter.74
  2568.8 66.6 reduce-scatter.90
  2638.9 67.2 reduce-scatter.54
  2712.2 121.4 all-reduce.195
  2841.1 122.8 all-reduce.197
  (1 shorter events, 20.7 us)
where the time goes:
time: 2990 us; the launch traced here: 2980 us
  waiting for transfers between devices  2020 us (68%)
  matrix products  459 us (15%)
  local copies, waits for them, and re-layouts  199 us (7%)
  blocking collectives  145 us (5%)
  other arithmetic  120 us (4%)
    unnamed x62, waiting for transfers between devices  643 us
    psum x2, waiting for transfers between devices, per_device(): lax.psum((scale_total, shift_total, hidden_total, width_total, value_tota...  256 us
    unnamed x925, local copies, waits for them, and re-layouts  157 us
    dot_general x30, matrix products, weight_grad(): lax.dot_general(left, right, (((0,), (0,)), ((), ())), preferred_element_...  155 us
    all_gather x3, waiting for transfers between devices, per_device(): lax.all_gather(value_rows.reshape(CLIPS_MB, frames, D), ('coarse', 'fine'...  128 us
    dot_general x30, matrix products, back_product(): lax.dot_general(grad, weight, (((1,), (1,)), ((), ())), preferred_element...  88.3 us
    reduce_scatter x1, waiting for transfers between devices, per_device(): lax.psum_scatter(totals[9].astype(jnp.bfloat16), 'clip', scatter_dimensio...  74.2 us
    reduce_scatter x1, waiting for transfers between devices, per_device(): lax.psum_scatter(totals[1].astype(jnp.bfloat16), 'clip', scatter_dimensio...  74.1 us
  transfers between devices with their start and end apart: 55, of which 42 were waited for; matrix products, arithmetic and copies ran while one was open for 21% of the time, Pallas kernels for 0%

commit v1 on v0

v1 whole, which is shorter than its diff:
```python
import functools

import jax
import jax.numpy as jnp
from jax import lax
from jax.experimental import pallas as pl
from jax.experimental.pallas import tpu as pltpu
from jax.sharding import PartitionSpec as P

D = 1024
HEADS = 16
HEAD_SIZE = 64
KERNEL = 31
BACK_REACH = 64
FORE_REACH = 8
OFFSETS = 73
TABLE_ROWS = 128
SEQ = ("coarse", "fine")
VMEM_BYTES = 56 * 1024 * 1024

negative_fill = -1e30
bf16 = jnp.bfloat16
f32 = jnp.float32


def log2(size):
    return size.bit_length() - 1


def swapped(shard, axis, bit):
    peers = lax.axis_size(axis)
    return lax.ppermute(shard, axis, [(i, i ^ (1 << bit)) for i in range(peers)])


def passed_along(shard, axis, by):
    peers = lax.axis_size(axis)
    pairs = [(i, i + by) for i in range(peers) if 0 <= i + by < peers]
    return lax.ppermute(shard, axis, pairs)


def layer_norm(rows, scale, shift):
    middle = jnp.mean(rows, -1, keepdims=True)
    centered = rows - middle
    spread = jnp.mean(centered * centered, -1, keepdims=True)
    return centered * lax.rsqrt(spread + 1e-05) * scale + shift


def norm_back(rows, scale, shift, grad):
    unused, pull = jax.vjp(layer_norm, rows, scale, shift)
    return pull(grad)


def glu_gate(doubled):
    half = doubled.shape[-1] // 2
    return doubled[..., :half] * jax.nn.sigmoid(doubled[..., half:])


def post_norm(mixed, scale, shift):
    return jax.nn.silu(layer_norm(mixed, scale, shift))


def depthwise(extended, kernel):
    count = extended.shape[1] - kernel.shape[0] + 1
    return sum((kernel[tap] * extended[:, tap : tap + count] for tap in range(kernel.shape[0])))


def product(left, right):
    return jnp.dot(left, right, preferred_element_type=f32)


def weight_grad(left, right):
    return lax.dot_general(left, right, (((0,), (0,)), ((), ())), preferred_element_type=f32)


def product_t(left, right):
    return lax.dot_general(left, right, (((1,), (1,)), ((), ())), preferred_element_type=f32)


def column_sum(values):
    return jnp.sum(values.astype(f32), 0)


def gather_steps(reverse):
    coarse = [("coarse", b) for b in range(log2(lax.axis_size("coarse")))]
    fine = [("fine", b) for b in range(log2(lax.axis_size("fine")))]
    upper = [("clip", b) for b in range(1, log2(lax.axis_size("clip")))]
    return coarse + (upper + fine if reverse else fine + upper)


def place_table(steps):
    count = 1 << len(steps)
    index = jnp.arange(count, dtype=jnp.int32)
    at = {
        axis: jnp.full((count,), lax.axis_index(axis), jnp.int32)
        for axis in ("clip", "coarse", "fine")
    }
    core = at["clip"] & 1
    for step, (axis, bit) in enumerate(steps):
        at[axis] = at[axis] ^ (((index >> step) & 1) << bit)
    column = at["coarse"] * lax.axis_size("fine") + at["fine"]
    return jnp.stack([column, at["clip"] >> 1, core])


def place_kernel(splits, table, own_ref, other_ref, *outs):
    width = own_ref.shape[2]
    core = table[2, 0]

    def write(first, second):
        start = 0
        for out, rows in zip(outs, splits):
            out[:, :width] = first[0, start : start + rows, :]
            out[:, width:] = second[0, start : start + rows, :]
            start += rows

    @pl.when(core == 0)
    def own_first():
        write(own_ref, other_ref)

    @pl.when(core != 0)
    def own_second():
        write(other_ref, own_ref)


def place(own, other, table, splits):
    pieces, rows, width = own.shape
    columns = lax.axis_size(SEQ)
    uppers = lax.axis_size("clip") // 2
    total = 2 * pieces * rows * width
    return pl.pallas_call(
        functools.partial(place_kernel, splits),
        out_shape=[
            jax.ShapeDtypeStruct((columns * part, uppers * 2 * width), bf16) for part in splits
        ],
        grid_spec=pltpu.PrefetchScalarGridSpec(
            num_scalar_prefetch=1,
            grid=(pieces,),
            in_specs=[
                pl.BlockSpec((1, rows, width), lambda p, table: (p, 0, 0)),
                pl.BlockSpec((1, rows, width), lambda p, table: (p, 0, 0)),
            ],
            out_specs=[
                pl.BlockSpec((part, 2 * width), lambda p, table: (table[0, p], table[1, p]))
                for part in splits
            ],
        ),
        compiler_params=pltpu.CompilerParams(vmem_limit_bytes=VMEM_BYTES),
        cost_estimate=pl.CostEstimate(flops=0, bytes_accessed=4 * total, transcendentals=0),
        name="place",
    )(table, own, other)


def gather_group(shard, steps):
    held = shard[None]
    for axis, bit in steps:
        held = jnp.concatenate([held, swapped(held, axis, bit)], 0)
    return held, swapped(held, "clip", 0)


def reduce_group(pairs, reverse):
    clip_count = lax.axis_size("clip")
    uppers = clip_count // 2
    sizes = {"coarse": lax.axis_size("coarse"), "fine": lax.axis_size("fine")}
    me = lax.axis_index("clip")
    width = pairs[0][0].shape[1] // clip_count
    parts = []
    for left, right in pairs:

        def blocks(core):
            return [
                lax.dynamic_slice_in_dim(left, (me ^ (2 * upper + core)) * width, width, 1)
                for upper in range(uppers)
            ]

        away = weight_grad(right, jnp.concatenate(blocks(1), 1)).astype(bf16)
        arrived = swapped(away, "clip", 0)
        kept = weight_grad(right, jnp.concatenate(blocks(0), 1)) + arrived.astype(f32)
        per_block = right.shape[1] // (sizes["coarse"] * sizes["fine"])
        parts.append(
            kept.astype(bf16).reshape(
                sizes["coarse"], sizes["fine"], per_block, uppers * width
            )
        )
    held = parts[0] if len(parts) == 1 else jnp.concatenate(parts, 2)
    coarse = [("coarse", b) for b in range(log2(sizes["coarse"]))][::-1]
    fine = [("fine", b) for b in range(log2(sizes["fine"]))][::-1]
    upper = [("clip", b) for b in range(1, log2(clip_count))][::-1]
    steps = (fine + upper if reverse else upper + fine) + coarse
    for count, (axis, bit) in enumerate(steps):
        if axis == "clip":
            half = held.shape[3] // 2
            away, kept = held[..., half:], held[..., :half]
        else:
            dim = 0 if axis == "coarse" else 1
            split = held.shape[:dim] + (2, held.shape[dim] // 2) + held.shape[dim + 1 :]
            mine = (lax.axis_index(axis) >> bit) & 1
            both = held.reshape(split)
            away = lax.dynamic_index_in_dim(both, 1 - mine, dim, keepdims=False)
            kept = lax.dynamic_index_in_dim(both, mine, dim, keepdims=False)
        total = kept.astype(f32) + swapped(away, axis, bit).astype(f32)
        held = total if count == len(steps) - 1 else total.astype(bf16)
    return held.reshape(held.shape[2], held.shape[3])


def summed_everywhere(values):
    for axis in ("clip", "fine", "coarse"):
        for bit in range(log2(lax.axis_size(axis))):
            values = values + swapped(values, axis, bit)
    return values


def packed(parts):
    flat = jnp.concatenate([part.reshape(-1) for part in parts])
    rows = -(-flat.shape[0] // 8192) * 8
    return jnp.pad(flat, (0, rows * D - flat.shape[0])).reshape(rows, D)


def unpacked(rows, parts):
    flat = rows.reshape(-1)
    out, start = [], 0
    for part in parts:
        out.append(flat[start : start + part.size].reshape(part.shape))
        start += part.size
    return out


def head_rows(ref, start, width):
    return ref[:, 0, :, start : start + width].reshape(-1, width)


def attend_kernel(lengths, x_ref, table_ref, out_ref, probs_ref):
    blocks, unused, block, wide = x_ref.shape
    length = blocks * block
    width = wide // 3
    valid = lengths[pl.program_id(0)]
    table = table_ref[...]
    key_at = lax.broadcasted_iota(jnp.int32, (1, length), 1)
    masked = key_at >= valid
    row_at = lax.broadcasted_iota(jnp.int32, (block, 3 * block), 0)
    offset = lax.broadcasted_iota(jnp.int32, (block, 3 * block), 1) - block - row_at
    for head in range(width // HEAD_SIZE):
        at = head * HEAD_SIZE
        keys = head_rows(x_ref, width + at, HEAD_SIZE)
        values = head_rows(x_ref, 2 * width + at, HEAD_SIZE)
        for part in range(blocks):
            queries = x_ref[part, 0, :, at : at + HEAD_SIZE]
            relative = product_t(queries, table).astype(bf16).astype(f32)
            back = relative[:, :1]
            fore = relative[:, OFFSETS - 1 : OFFSETS]
            band = jnp.concatenate([relative, jnp.zeros((block, 2 * block), f32)], 1)
            band = pltpu.roll(band, block - BACK_REACH, 1, stride=1, stride_axis=0)
            band = jnp.where(offset <= -BACK_REACH, back, jnp.where(offset >= FORE_REACH, fore, band))
            bias = []
            if part > 1:
                bias.append(jnp.broadcast_to(back, (block, (part - 1) * block)))
            bias.append(
                band[:, (block if part == 0 else 0) : (2 * block if part == blocks - 1 else 3 * block)]
            )
            if part < blocks - 2:
                bias.append(jnp.broadcast_to(fore, (block, (blocks - 2 - part) * block)))
            scores = (product_t(queries, keys) + jnp.concatenate(bias, 1)) * HEAD_SIZE ** (-0.5)
            scores = jnp.where(masked, negative_fill, scores)
            shifted = jnp.exp(scores - jnp.max(scores, -1, keepdims=True))
            probs = (shifted * (1.0 / jnp.sum(shifted, -1, keepdims=True))).astype(bf16)
            probs_ref[0, head, part * block : (part + 1) * block, :] = probs
            out_ref[part, 0, :, at : at + HEAD_SIZE] = product(probs, values).astype(bf16)


def attend_back_kernel(x_ref, grad_ref, probs_ref, table_ref, out_ref, table_out, score_g, relative_g):
    blocks, unused, block, wide = x_ref.shape
    width = wide // 3
    table = table_ref[...]
    scale = HEAD_SIZE ** (-0.5)
    row_at = lax.broadcasted_iota(jnp.int32, (block, 3 * block), 0)
    offset = lax.broadcasted_iota(jnp.int32, (block, 3 * block), 1) - block - row_at
    row_two = lax.broadcasted_iota(jnp.int32, (block, 2 * block), 0)
    lane = lax.broadcasted_iota(jnp.int32, (block, TABLE_ROWS), 1)
    zeros = jnp.zeros((block, block), f32)
    table_total = jnp.zeros(table_out.shape[1:], f32)
    for head in range(width // HEAD_SIZE):
        at = head * HEAD_SIZE
        all_queries = head_rows(x_ref, at, HEAD_SIZE)
        keys = head_rows(x_ref, width + at, HEAD_SIZE)
        values = head_rows(x_ref, 2 * width + at, HEAD_SIZE)
        all_grads = head_rows(grad_ref, at, HEAD_SIZE)
        for part in range(blocks):
            rows = slice(part * block, (part + 1) * block)
            grads = grad_ref[part, 0, :, at : at + HEAD_SIZE]
            probs = probs_ref[0, head, rows, :].astype(f32)
            probs_g = product_t(grads, values)
            inner = jnp.sum(probs * probs_g, -1, keepdims=True)
            low = (probs * (probs_g - inner)).astype(bf16)
            score_g[rows, :] = low
            wide_low = low.astype(f32)
            first = (part - 1) * block
            pieces = []
            if part == 0:
                pieces.append(zeros)
            pieces.append(wide_low[:, max(first, 0) : first + 3 * block])
            if part == blocks - 1:
                pieces.append(zeros)
            window = jnp.concatenate(pieces, 1)
            back = jnp.sum(jnp.where(offset <= -BACK_REACH, window, 0.0), -1, keepdims=True)
            fore = jnp.sum(jnp.where(offset >= FORE_REACH, window, 0.0), -1, keepdims=True)
            if part > 1:
                back = back + jnp.sum(wide_low[:, :first], -1, keepdims=True)
            if part < blocks - 2:
                fore = fore + jnp.sum(wide_low[:, first + 3 * block :], -1, keepdims=True)
            band = pltpu.roll(window, 3 * block - (block - BACK_REACH), 1)[:, : 2 * block]
            for bit in range(log2(block)):
                rolled = pltpu.roll(band, 2 * block - (1 << bit), 1)
                band = jnp.where(((row_two >> bit) & 1) == 1, rolled, band)
            band = band[:, :TABLE_ROWS]
            band = jnp.where(lane == 0, back, jnp.where(lane == OFFSETS - 1, fore, band))
            band = jnp.where(lane < OFFSETS, band, 0.0)
            relative = (band * scale).astype(bf16)
            relative_g[rows, :] = relative
            query_g = product(low, keys) * scale + product(relative, table)
            out_ref[part, 0, :, at : at + HEAD_SIZE] = query_g.astype(bf16)
        key_g = (weight_grad(score_g[...], all_queries) * scale).astype(bf16)
        value_g = weight_grad(probs_ref[0, head], all_grads).astype(bf16)
        table_total = table_total + weight_grad(relative_g[...], all_queries)
        for part in range(blocks):
            rows = slice(part * block, (part + 1) * block)
            out_ref[part, 0, :, width + at : width + at + HEAD_SIZE] = key_g[rows]
            out_ref[part, 0, :, 2 * width + at : 2 * width + at + HEAD_SIZE] = value_g[rows]
    table_out[0] = table_total


def attend(x, lengths, table):
    blocks, clips, block, wide = x.shape
    length, heads = blocks * block, wide // 3 // HEAD_SIZE
    return pl.pallas_call(
        attend_kernel,
        out_shape=[
            jax.ShapeDtypeStruct((blocks, clips, block, wide // 3), bf16),
            jax.ShapeDtypeStruct((clips, heads, length, length), bf16),
        ],
        grid_spec=pltpu.PrefetchScalarGridSpec(
            num_scalar_prefetch=1,
            grid=(clips,),
            in_specs=[
                pl.BlockSpec((blocks, 1, block, wide), lambda c, lengths: (0, c, 0, 0)),
                pl.BlockSpec((TABLE_ROWS, HEAD_SIZE), lambda c, lengths: (0, 0)),
            ],
            out_specs=[
                pl.BlockSpec((blocks, 1, block, wide // 3), lambda c, lengths: (0, c, 0, 0)),
                pl.BlockSpec((1, heads, length, length), lambda c, lengths: (c, 0, 0, 0)),
            ],
        ),
        compiler_params=pltpu.CompilerParams(vmem_limit_bytes=VMEM_BYTES),
        cost_estimate=pl.CostEstimate(
            flops=16 * clips * heads * length * length * HEAD_SIZE,
            bytes_accessed=2 * clips * heads * length * length,
            transcendentals=clips * heads * length * length,
        ),
        name="attend",
    )(lengths, x, table)


def attend_back(x, grads, probs, table):
    blocks, clips, block, wide = x.shape
    length, heads = blocks * block, wide // 3 // HEAD_SIZE
    return pl.pallas_call(
        attend_back_kernel,
        out_shape=[
            jax.ShapeDtypeStruct(x.shape, bf16),
            jax.ShapeDtypeStruct((clips, TABLE_ROWS, HEAD_SIZE), f32),
        ],
        grid=(clips,),
        in_specs=[
            pl.BlockSpec((blocks, 1, block, wide), lambda c: (0, c, 0, 0)),
            pl.BlockSpec((blocks, 1, block, wide // 3), lambda c: (0, c, 0, 0)),
            pl.BlockSpec((1, heads, length, length), lambda c: (c, 0, 0, 0)),
            pl.BlockSpec((TABLE_ROWS, HEAD_SIZE), lambda c: (0, 0)),
        ],
        out_specs=[
            pl.BlockSpec((blocks, 1, block, wide), lambda c: (0, c, 0, 0)),
            pl.BlockSpec((1, TABLE_ROWS, HEAD_SIZE), lambda c: (c, 0, 0)),
        ],
        scratch_shapes=[
            pltpu.VMEM((length, length), bf16),
            pltpu.VMEM((length, TABLE_ROWS), bf16),
        ],
        compiler_params=pltpu.CompilerParams(vmem_limit_bytes=VMEM_BYTES),
        cost_estimate=pl.CostEstimate(
            flops=32 * clips * heads * length * length * HEAD_SIZE,
            bytes_accessed=2 * clips * heads * length * length,
            transcendentals=0,
        ),
        name="attend_back",
    )(x, grads, probs, table)


def exchanged(rows):
    return lax.all_to_all(rows, SEQ, 0, 0, tiled=True)


class HeadsSplit:
    def __init__(self, clips, frames, lengths, table_low):
        self.clips, self.frames, self.lengths = clips, frames, lengths
        self.peers = lax.axis_size(SEQ)
        self.table = jnp.pad(table_low, ((0, TABLE_ROWS - OFFSETS), (0, 0)))

    def to_heads(self, rows):
        wide = rows.shape[1] // self.peers
        split = rows.reshape(self.clips * self.frames, self.peers, wide).transpose(1, 0, 2)
        return exchanged(split.reshape(self.peers, self.clips, self.frames, wide))

    def to_rows(self, blocks):
        wide = blocks.shape[3]
        back = exchanged(blocks).reshape(self.peers, self.clips * self.frames, wide)
        return back.transpose(1, 0, 2).reshape(self.clips * self.frames, self.peers * wide)

    def forward(self, rows):
        self.x = self.to_heads(rows)
        mixed, self.probs = attend(self.x, self.lengths, self.table)
        return self.to_rows(mixed)

    def backward(self, mixed_grad):
        grads, table_g = attend_back(self.x, self.to_heads(mixed_grad), self.probs, self.table)
        return self.to_rows(grads), jnp.sum(table_g, 0)[:OFFSETS]


class KeysGathered:
    def __init__(self, clips, frames, lengths, table_low):
        self.clips, self.frames, self.table = clips, frames, table_low
        self.peers = lax.axis_size(SEQ)
        length = frames * self.peers
        query_pos = lax.axis_index(SEQ) * frames + jnp.arange(frames, dtype=jnp.int32)
        key_pos = jnp.arange(length, dtype=jnp.int32)
        offset = jnp.clip(key_pos[None, :] - query_pos[:, None], -BACK_REACH, FORE_REACH)
        self.onehot = (
            (offset + BACK_REACH)[None] == jnp.arange(OFFSETS, dtype=jnp.int32)[:, None, None]
        ).astype(bf16)
        self.key_valid = key_pos[None, :] < lengths[:, None]

    def heads(self, rows):
        return rows.reshape(rows.shape[0], rows.shape[1], HEADS, HEAD_SIZE)

    def scores(self):
        dotted = jnp.einsum("cihd,cjhd->chij", self.queries, self.keys, preferred_element_type=f32)
        bias = jnp.einsum("chir,rij->chij", self.relative, self.onehot, preferred_element_type=f32)
        scaled = (dotted + bias) * HEAD_SIZE ** (-0.5)
        return jnp.where(self.key_valid[:, None, None, :], scaled, negative_fill)

    def forward(self, rows):
        split = rows.reshape(self.clips, self.frames, self.peers, 3, -1)
        flat = [split[:, :, :, which].reshape(self.clips, self.frames, D) for which in range(3)]
        self.queries = self.heads(flat[0])
        self.keys = self.heads(lax.all_gather(flat[1], SEQ, axis=1, tiled=True))
        self.values = self.heads(lax.all_gather(flat[2], SEQ, axis=1, tiled=True))
        self.relative = jnp.einsum(
            "cihd,rd->chir", self.queries, self.table, preferred_element_type=f32
        ).astype(bf16)
        scores = self.scores()
        top = jnp.max(scores, -1, keepdims=True)
        self.log_total = jnp.log(jnp.sum(jnp.exp(scores - top), -1, keepdims=True)) + top
        probs = jnp.exp(scores - self.log_total).astype(bf16)
        mixed = jnp.einsum("chij,cjhd->cihd", probs, self.values, preferred_element_type=f32)
        return mixed.astype(bf16).reshape(self.clips * self.frames, D)

    def backward(self, mixed_grad):
        scale = HEAD_SIZE ** (-0.5)
        grads = self.heads(mixed_grad.reshape(self.clips, self.frames, D))
        probs = jnp.exp(self.scores() - self.log_total)
        probs_g = jnp.einsum("cihd,cjhd->chij", grads, self.values, preferred_element_type=f32)
        inner = jnp.sum(probs * probs_g, -1, keepdims=True)
        scores_g = (probs * (probs_g - inner)).astype(bf16)
        relative_g = (
            jnp.einsum("chij,rij->chir", scores_g, self.onehot, preferred_element_type=f32) * scale
        ).astype(bf16)
        query_g = jnp.einsum(
            "chij,cjhd->cihd", scores_g, self.keys, preferred_element_type=f32
        ) * scale + jnp.einsum("chir,rd->cihd", relative_g, self.table, preferred_element_type=f32)
        table_g = jnp.einsum(
            "chir,cihd->rd", relative_g, self.queries, preferred_element_type=f32
        )
        key_g = (
            jnp.einsum("chij,cihd->cjhd", scores_g, self.queries, preferred_element_type=f32) * scale
        )
        value_g = jnp.einsum(
            "chij,cihd->cjhd", probs.astype(bf16), grads, preferred_element_type=f32
        )
        length = self.frames * self.peers
        both = [
            lax.psum_scatter(
                terms.reshape(self.clips, length, D).astype(bf16),
                SEQ,
                scatter_dimension=1,
                tiled=True,
            )
            for terms in (key_g, value_g)
        ]
        rows = self.clips * self.frames
        parts = [query_g.astype(bf16)] + both
        joined = jnp.stack([part.reshape(rows, self.peers, -1) for part in parts], 2)
        return joined.reshape(rows, 3 * D), table_g


def feed_forward(hidden, scale, shift, w_in, b_in, w_out, b_out):
    normed = layer_norm(hidden, scale, shift).astype(bf16)
    upper = product_t(normed, w_in) + b_in
    acted = jax.nn.silu(upper).astype(bf16)
    return (product_t(acted, w_out) + b_out, (normed, upper, acted))


def feed_back(grad, hidden, scale, shift, w_in, w_out, saved):
    normed, upper, acted = saved
    grad_low = grad.astype(bf16)
    unused, silu_pull = jax.vjp(jax.nn.silu, upper)
    upper_grad = silu_pull(product(grad_low, w_out))[0].astype(bf16)
    hidden_grad, scale_grad, shift_grad = norm_back(
        hidden, scale, shift, product(upper_grad, w_in)
    )
    return (
        hidden_grad,
        (normed, upper_grad),
        (acted, grad_low),
        scale_grad,
        shift_grad,
        column_sum(upper_grad),
        column_sum(grad_low),
    )


def per_device(
    frames_in,
    clip_lengths,
    out_grad,
    first_up,
    first_down,
    query_weight,
    key_weight,
    value_weight,
    output_weight,
    pointwise_in,
    pointwise_out,
    second_up,
    second_down,
    norm_scales,
    norm_shifts,
    hidden_biases,
    width_biases,
    value_bias,
    relative_table,
    depth_kernel,
):
    clips, frames, unused = frames_in.shape
    rows = clips * frames
    peers = lax.axis_size(SEQ)

    orders = [gather_steps(False), gather_steps(True)]
    tables = [place_table(steps) for steps in orders]
    groups = (
        ([first_up],),
        ([first_down],),
        ([query_weight, key_weight, value_weight], [output_weight]),
        ([pointwise_in], [pointwise_out]),
        ([second_up],),
        ([second_down],),
    )
    placed = []
    for number, group in enumerate(groups):
        shards = [shard.astype(bf16).T for part in group for shard in part]
        splits = tuple(sum(shard.shape[1] for shard in part) for part in group)
        order = number % 2
        own, other = gather_group(jnp.concatenate(shards, 0), orders[order])
        placed.extend(place(own, other, tables[order], splits))
    (
        up_first,
        down_first,
        inputs_full,
        output_full,
        inner_full,
        outer_full,
        up_second,
        down_second,
    ) = placed

    base = lax.axis_index(SEQ) * frames
    table_low = relative_table.astype(bf16)
    query_pos = base + jnp.arange(frames, dtype=jnp.int32)
    frame_valid = (query_pos[None, :] < clip_lengths[:, None]).reshape(rows, 1)
    share = D // peers
    inputs_bias = jnp.stack(
        [
            width_biases[1].reshape(peers, share),
            jnp.zeros((peers, share), f32),
            value_bias.reshape(peers, share),
        ],
        1,
    ).reshape(3 * D)

    start_rows = frames_in.astype(f32).reshape(rows, D)
    branch_one, first_saved = feed_forward(
        start_rows,
        norm_scales[0],
        norm_shifts[0],
        up_first,
        hidden_biases[0],
        down_first,
        width_biases[0],
    )
    after_first = start_rows + 0.5 * branch_one
    att_normed = layer_norm(after_first, norm_scales[1], norm_shifts[1]).astype(bf16)
    attention_rows = (product_t(att_normed, inputs_full) + inputs_bias).astype(bf16)
    split_heads = HEADS % peers == 0 and (D // peers) % 128 == 0
    attention = (HeadsSplit if split_heads else KeysGathered)(
        clips, frames, clip_lengths, table_low
    )
    mixed = attention.forward(attention_rows)
    after_attention = after_first + product_t(mixed, output_full) + width_biases[2]
    conv_normed = jnp.where(
        frame_valid, layer_norm(after_attention, norm_scales[2], norm_shifts[2]), 0.0
    ).astype(bf16)
    doubled = product_t(conv_normed, inner_full)
    gated = glu_gate(doubled).astype(bf16).reshape(clips, frames, D)
    carried = passed_along(gated[:, frames - KERNEL + 1 :], SEQ, 1)
    extended = jnp.concatenate([carried, gated], 1).astype(f32)
    mixed_conv = depthwise(extended, depth_kernel).reshape(rows, D)
    conv_acted = post_norm(mixed_conv, norm_scales[3], norm_shifts[3]).astype(bf16)
    after_conv = after_attention + product_t(conv_acted, outer_full)
    branch_two, second_saved = feed_forward(
        after_conv,
        norm_scales[4],
        norm_shifts[4],
        up_second,
        hidden_biases[1],
        down_second,
        width_biases[3],
    )
    after_second = after_conv + 0.5 * branch_two
    layer_out = (
        layer_norm(after_second, norm_scales[5], norm_shifts[5])
        .astype(bf16)
        .reshape(clips, frames, D)
    )

    final_grad, final_scale, final_shift = norm_back(
        after_second, norm_scales[5], norm_shifts[5], out_grad.astype(f32).reshape(rows, D)
    )
    (
        second_in,
        second_up_pair,
        second_down_pair,
        second_scale,
        second_shift,
        second_hidden,
        second_width,
    ) = feed_back(
        0.5 * final_grad,
        after_conv,
        norm_scales[4],
        norm_shifts[4],
        up_second,
        down_second,
        second_saved,
    )
    second_down_g = reduce_group([second_down_pair], False)
    second_up_g = reduce_group([second_up_pair], True)
    grad_conv = final_grad + second_in
    conv_low = grad_conv.astype(bf16)
    unused, post_pull = jax.vjp(post_norm, mixed_conv, norm_scales[3], norm_shifts[3])
    mixed_g, depth_scale, depth_shift = post_pull(product(conv_low, outer_full))
    unused, depth_pull = jax.vjp(depthwise, extended, depth_kernel)
    extended_g, kernel_g = depth_pull(mixed_g.reshape(clips, frames, D))
    returned = passed_along(extended_g[:, : KERNEL - 1].astype(bf16), SEQ, -1).astype(f32)
    own_g = extended_g[:, KERNEL - 1 :]
    gated_g = jnp.concatenate(
        [own_g[:, : frames - KERNEL + 1], own_g[:, frames - KERNEL + 1 :] + returned], 1
    ).reshape(rows, D)
    unused, glu_pull = jax.vjp(glu_gate, doubled)
    doubled_g = glu_pull(gated_g)[0].astype(bf16)
    normed_g = jnp.where(frame_valid, product(doubled_g, inner_full), 0.0)
    conv_in_g, conv_scale, conv_shift = norm_back(
        after_attention, norm_scales[2], norm_shifts[2], normed_g
    )
    grad_att = grad_conv + conv_in_g
    att_low = grad_att.astype(bf16)
    middle_g = reduce_group(
        [(conv_normed, doubled_g), (conv_acted, conv_low), (mixed, att_low)], False
    )
    mixed_grad = product(att_low, output_full).astype(bf16)
    attention_g, table_g = attention.backward(mixed_grad)
    inputs_g = reduce_group([(att_normed, attention_g)], True)
    att_in_g, att_scale, att_shift = norm_back(
        after_first, norm_scales[1], norm_shifts[1], product(attention_g, inputs_full)
    )
    grad_first = grad_att + att_in_g
    (
        first_in,
        first_up_pair,
        first_down_pair,
        first_scale,
        first_shift,
        first_hidden,
        first_width,
    ) = feed_back(
        0.5 * grad_first,
        start_rows,
        norm_scales[0],
        norm_shifts[0],
        up_first,
        down_first,
        first_saved,
    )
    first_down_g = reduce_group([first_down_pair], False)
    first_up_g = reduce_group([first_up_pair], True)
    in_grad = (grad_first + first_in).astype(bf16).reshape(clips, frames, D)

    attention_sums = column_sum(attention_g).reshape(peers, 3, share)
    early = [
        jnp.stack([att_scale, conv_scale, depth_scale, second_scale, final_scale]),
        jnp.stack([att_shift, conv_shift, depth_shift, second_shift, final_shift]),
        second_hidden[None],
        jnp.stack([attention_sums[:, 0].reshape(D), column_sum(att_low), second_width]),
        attention_sums[:, 2].reshape(D),
        table_g,
        kernel_g,
    ]
    late = [first_scale[None], first_shift[None], first_hidden[None], first_width[None]]
    early = unpacked(summed_everywhere(packed(early)), early)
    late = unpacked(summed_everywhere(packed(late)), late)

    inner_n = 2 * D // peers
    outer_n = D // peers
    return (
        layer_out,
        in_grad,
        first_up_g.T,
        first_down_g.T,
        inputs_g[:share].T,
        inputs_g[share : 2 * share].T,
        inputs_g[2 * share :].T,
        middle_g[inner_n + outer_n :].T,
        middle_g[:inner_n].T,
        middle_g[inner_n : inner_n + outer_n].T,
        second_up_g.T,
        second_down_g.T,
        jnp.concatenate([late[0], early[0]], 0),
        jnp.concatenate([late[1], early[1]], 0),
        jnp.concatenate([late[2], early[2]], 0),
        jnp.concatenate([late[3], early[3]], 0),
        early[4],
        early[5],
        early[6],
    )


def solution(mesh):
    block = P("clip", ("coarse", "fine"))
    rows = P("clip", ("coarse", "fine"), None)
    in_specs = (rows, P("clip"), rows) + (block,) * 10 + (P(),) * 7
    out_specs = (rows, rows) + (block,) * 10 + (P(),) * 7
    return jax.shard_map(
        per_device, mesh=mesh, in_specs=in_specs, out_specs=out_specs, check_vma=False
    )
```

time: 2990 us -> 1040 us (0.35)
  waiting for transfers between devices: 2020 us -> 348 us
  matrix products: 459 us -> 143 us
  Pallas kernels: 0 us -> 173 us
  blocking collectives: 145 us -> 0 us
  starting transfers between devices: 18.9 us -> 93.9 us
  local copies, waits for them, and re-layouts: 199 us -> 131 us
    unnamed x62 -> x0, waiting for transfers between devices: 643 us -> none
    all_gather x21 -> x0, waiting for transfers between devices: 596 us -> none  [the longest x3 128 us: per_device(): lax.all_gather(value_rows.reshape(CLIPS_MB, frames, D), ('coarse', 'fine'...]
    reduce_scatter x13 -> x0, waiting for transfers between devices: 517 us -> none  [the longest x1 74.2 us: per_device(): lax.psum_scatter(totals[9].astype(jnp.bfloat16), 'clip', scatter_dimensio...]
    ppermute x0 -> x72, waiting for transfers between devices: none -> 340 us  [swapped(): return lax.ppermute(shard, axis, [(i, i ^ 1 << bit) for i in range(peers)])]
    psum x2 -> x0, waiting for transfers between devices: 256 us -> none  [per_device(): lax.psum((scale_total, shift_total, hidden_total, width_total, value_tota...]
    dot_general x93 -> x16, matrix products: 303 us -> 82.3 us  [the longest x8 42 us: product_t(): lax.dot_general(left, right, (((1,), (1,)), ((), ())), preferred_element_...]
    pallas_call x0 -> x8, Pallas kernels: none -> 173 us  [the longest x6 75.7 us: place(): pl.pallas_call(functools.partial(place_kernel, splits), out_shape=[jax.Sh...]
    all_gather x5 -> x0, blocking collectives: 145 us -> none  [the longest x1 30.4 us: per_device(): lax.all_gather(pointwise_out.astype(jnp.bfloat16), ('coarse', 'fine'), ax...]
  transfers between devices with their start and end apart: 55 -> 78, of which waited for: 42 -> 37; matrix products, arithmetic and copies ran while one was open for 21% -> 28% of each run, Pallas kernels for 0% -> 17%
where the time goes in v1:
time: 1040 us; the launch traced here: 1030 us
  waiting for transfers between devices  348 us (33%)
  Pallas kernels  173 us (17%)
  matrix products  143 us (14%)
  other arithmetic  133 us (13%)
  local copies, waits for them, and re-layouts  131 us (13%)
  starting transfers between devices  93.9 us (9%)
    ppermute x72, waiting for transfers between devices, swapped(): return lax.ppermute(shard, axis, [(i, i ^ 1 << bit) for i in range(peers)])  340 us
    pallas_call x6, Pallas kernels, place(): pl.pallas_call(functools.partial(place_kernel, splits), out_shape=[jax.Sh...  75.7 us
    pallas_call x1, Pallas kernels, attend_back(): pl.pallas_call(attend_back_kernel, out_shape=[jax.ShapeDtypeStruct(x.shap...  68 us
    ppermute x72, starting transfers between devices, swapped(): return lax.ppermute(shard, axis, [(i, i ^ 1 << bit) for i in range(peers)])  66.2 us
    dot_general x16, matrix products, weight_grad(): lax.dot_general(left, right, (((0,), (0,)), ((), ())), preferred_element_...  60.6 us
    unnamed x520, local copies, waits for them, and re-layouts  54.1 us
    dot_general x8, matrix products, product_t(): lax.dot_general(left, right, (((1,), (1,)), ((), ())), preferred_element_...  42 us
    dot_general x8, matrix products, product(): return jnp.dot(left, right, preferred_element_type=f32)  40.3 us
  transfers between devices with their start and end apart: 78, of which 37 were waited for; matrix products, arithmetic and copies ran while one was open for 28% of the time, Pallas kernels for 17%

profile of v1, /device:TPU:0, one launch (start us, length us, event | category | flops | bytes accessed | tf_op | source)
XLA Modules:
  0.0 1026.6 jit_solution(839351863410251570)
XLA Ops:
  6.2 5.9 collective-permute-done
  15.2 6.6 collective-permute-done.5
  22.0 28.6 %collective-permute-done.1 = bf16[2,512,256]{2,1,0:T(8,128)(2,1)S(1)} collective-permute-done((bf16[2,512,256]{2,1,0:T(8,128)(2,1)S(1)}, bf16[2,512,256]{2,1,0:T(8,128)(2,1)S(1)}, u32[]{:S(2)}, u32[]{:S(2)}) %collective-permute-start.1) | collective-permute-done | bytes 524320 | tf_op jit(solution)/shard_map/ppermute | solution.py:32
  53.5 5.6 collective-permute-done.6
  75.5 11.1 %collective-permute-done.7 = bf16[4,128,1024]{2,1,0:T(8,128)(2,1)} collective-permute-done((bf16[4,128,1024]{2,1,0:T(8,128)(2,1)}, bf16[4,128,1024]{2,1,0:T(8,128)(2,1)}, u32[]{:S(2)}, u32[]{:S(2)}) %collective-permute-start.7) | collective-permute-done | bytes 1048608 | tf_op jit(solution)/shard_map/ppermute | solution.py:32
  97.3 13.7 %collective-permute-done.11 = bf16[2,512,256]{2,1,0:T(8,128)(2,1)S(1)} collective-permute-done((bf16[2,512,256]{2,1,0:T(8,128)(2,1)}, bf16[2,512,256]{2,1,0:T(8,128)(2,1)S(1)}, u32[]{:S(2)}, u32[]{:S(2)}) %collective-permute-start.11) | collective-permute-done | bytes 524320 | tf_op jit(solution)/shard_map/ppermute | solution.py:32
  119.1 8.9 collective-permute-done.3
  131.1 7.3 collective-permute-done.8
  142.7 9.9 collective-permute-done.12
  164.1 25.7 %collective-permute-done.27 = bf16[2,128,1024]{2,1,0:T(8,128)(2,1)S(1)} collective-permute-done((bf16[2,128,1024]{2,1,0:T(8,128)(2,1)S(1)}, bf16[2,128,1024]{2,1,0:T(8,128)(2,1)S(1)}, u32[]{:S(2)}, u32[]{:S(2)}) %collective-permute-start.27) | collective-permute-done | bytes 524320 | tf_op jit(solution)/shard_map/ppermute | solution.py:32
  192.0 5.8 collective-permute-done.22
  210.1 11.0 %collective-permute-done.28 = bf16[4,128,1024]{2,1,0:T(8,128)(2,1)S(1)} collective-permute-done((bf16[4,128,1024]{2,1,0:T(8,128)(2,1)}, bf16[4,128,1024]{2,1,0:T(8,128)(2,1)S(1)}, u32[]{:S(2)}, u32[]{:S(2)}) %collective-permute-start.28) | collective-permute-done | bytes 1048608 | tf_op jit(solution)/shard_map/ppermute | solution.py:32
  228.4 12.9 %place.6 = bf16[4096,1024]{1,0:T(8,128)(2,1)} custom-call(s32[3,16]{1,0:T(4,128)} %get-tuple-element.276.table, bf16[16,512,256]{2,1,0:T(8,128)(2,1)} %constant_dynamic-update-slice_fusion.own_ref, bf16[16,512,256]{2,1,0:T(8,128)(2,1)} %collective-permute-done.4.other_ref), custom_call_target="tpu_custom_call" | custom-call | bytes 16777216 | tf_op jit(solution)/shard_map/place/pallas_call | solution.py:129
  241.2 12.7 %place.7 = bf16[1024,4096]{1,0:T(8,128)(2,1)} custom-call(s32[3,16]{1,0:T(4,128)} %get-tuple-element.275.table, bf16[16,128,1024]{2,1,0:T(8,128)(2,1)} %constant_dynamic-update-slice_fusion.5.own_ref, bf16[16,128,1024]{2,1,0:T(8,128)(2,1)} %collective-permute-done.9.other_ref), custom_call_target="tpu_custom_call" | custom-call | bytes 16777216 | tf_op jit(solution)/shard_map/place/pallas_call | solution.py:129
  254.0 11.5 %multiply_convert_fusion.1 = (bf16[384,4096]{1,0:T(8,128)(2,1)S(1)}, f32[384,4096]{1,0:T(8,128)}) fusion(f32[4096]{0:T(1024)S(1)} %bitcast.612, bf16[384,1024]{1,0:T(8,128)(2,1)S(1)} %fusion.43, bf16[4096,1024]{1,0:T(8,128)(2,1)} %place.6), kind=kOutput, calls=%fused_computation.17 | convolution fusion | flops 3230662656 | bytes 18628608 | tf_op jit(solution)/shard_map/dot_general | solution.py:76
  270.2 12.8 %place.8 = (bf16[3072,1024]{1,0:T(8,128)(2,1)}, bf16[1024,1024]{1,0:T(8,128)(2,1)}) custom-call(s32[3,16]{1,0:T(4,128)} %get-tuple-element.276.table, bf16[16,512,256]{2,1,0:T(8,128)(2,1)} %constant_dynamic-update-slice_fusion.10.own_ref, bf16[16,512,256]{2,1,0:T(8,128)(2,1)} %collective-permute-done.14.other_ref), custom_call_target="tpu_custom_call" | custom-call | bytes 16777216 | tf_op jit(solution)/shard_map/place/pallas_call | solution.py:129
  283.0 7.3 add_convert_fusion.5
  291.9 6.5 all-to-all-start
  306.2 11.0 %collective-permute-done.17 = bf16[4,384,256]{2,1,0:T(8,128)(2,1)S(1)} collective-permute-done((bf16[4,384,256]{2,1,0:T(8,128)(2,1)S(1)}, bf16[4,384,256]{2,1,0:T(8,128)(2,1)S(1)}, u32[]{:S(2)}, u32[]{:S(2)}) %collective-permute-start.17) | collective-permute-done | bytes 786464 | tf_op jit(solution)/shard_map/ppermute | solution.py:32
  336.1 27.1 %collective-permute-done.18 = bf16[8,384,256]{2,1,0:T(8,128)(2,1)S(1)} collective-permute-done((bf16[8,384,256]{2,1,0:T(8,128)(2,1)S(1)}, bf16[8,384,256]{2,1,0:T(8,128)(2,1)S(1)}, u32[]{:S(2)}, u32[]{:S(2)}) %collective-permute-start.18) | collective-permute-done | bytes 1572896 | tf_op jit(solution)/shard_map/ppermute | solution.py:32
  365.2 29.6 %attend.1 = (bf16[8,3,128,128]{3,2,1,0:T(8,128)(2,1)}, bf16[3,2,1024,1024]{3,2,1,0:T(8,128)(2,1)}) custom-call(s32[3]{0:T(128)} %lengths.1, bf16[8,3,128,384]{3,2,1,0:T(8,128)(2,1)} %all-to-all-done.x_ref, bf16[128,64]{1,0:T(8,128)(2,1)} %pad.204.table_ref), custom_call_target="tpu_custom_call" | custom-call | flops 6442450944 | bytes 12582912 | tf_op jit(solution)/shard_map/attend/pallas_call | solution.py:332
  394.8 5.8 all-to-all-start.1
  401.9 12.1 %place.9 = (bf16[2048,1024]{1,0:T(8,128)(2,1)}, bf16[1024,1024]{1,0:T(8,128)(2,1)}) custom-call(s32[3,16]{1,0:T(4,128)} %get-tuple-element.275.table, bf16[16,384,256]{2,1,0:T(8,128)(2,1)} %constant_dynamic-update-slice_fusion.15.own_ref, bf16[16,384,256]{2,1,0:T(8,128)(2,1)} %collective-permute-done.19.other_ref), custom_call_target="tpu_custom_call" | custom-call | bytes 12582912 | tf_op jit(solution)/shard_map/place/pallas_call | solution.py:129
  414.0 12.6 %place.10 = bf16[4096,1024]{1,0:T(8,128)(2,1)} custom-call(s32[3,16]{1,0:T(4,128)} %get-tuple-element.276.table, bf16[16,512,256]{2,1,0:T(8,128)(2,1)} %constant_dynamic-update-slice_fusion.20.own_ref, bf16[16,512,256]{2,1,0:T(8,128)(2,1)} %collective-permute-done.25.other_ref), custom_call_target="tpu_custom_call" | custom-call | bytes 16777216 | tf_op jit(solution)/shard_map/place/pallas_call | solution.py:129
  426.6 12.7 %place.11 = bf16[1024,4096]{1,0:T(8,128)(2,1)} custom-call(s32[3,16]{1,0:T(4,128)} %get-tuple-element.275.table, bf16[16,128,1024]{2,1,0:T(8,128)(2,1)} %constant_dynamic-update-slice_fusion.25.own_ref, bf16[16,128,1024]{2,1,0:T(8,128)(2,1)} %collective-permute-done.30.other_ref), custom_call_target="tpu_custom_call" | custom-call | bytes 16777216 | tf_op jit(solution)/shard_map/place/pallas_call | solution.py:129
  455.7 7.4 fusion.147
  468.7 6.7 multiply_convert_fusion
  475.4 7.0 fusion.159
  486.7 10.7 %convert_reduce_fusion = (f32[4096]{0:T(1024)}, bf16[384,4096]{1,0:T(8,128)(2,1)S(1)}) fusion(f32[384,4096]{1,0:T(8,128)} %get-tuple-element.286, f32[4096]{0:T(1024)S(1)} %bitcast.615, bf16[384,1024]{1,0:T(8,128)(2,1)S(1)} %get-tuple-element.129, bf16[1024,4096]{1,0:T(8,128)(2,1)} %place.11), kind=kOutput, calls=%fused_computation.12 | convolution fusion | flops 3241668608 | bytes 18644992 | tf_op jit(solution)/shard_map/dot_general | solution.py:68
  517.6 9.7 broadcast_multiply_fusion
  527.3 16.1 %pad_add_fusion = f32[3,158,1024]{2,1,0:T(8,128)S(1)} fusion(f32[3,128,1024]{2,1,0:T(8,128)S(1)} %get-tuple-element.155, f32[3,128,1024]{2,1,0:T(8,128)S(1)} %get-tuple-element.156, f32[3,128,1024]{2,1,0:T(8,128)S(1)} %get-tuple-element.157, f32[3,128,1024]{2,1,0:T(8,128)} %get-tuple-element.158, f32[3,128,1024]{2,1,0:T(8,128)} %get-tuple-element.159, ...), kind=kLoop, calls=%fused_computation.62 | loop fusion | flops 14561280 | bytes 50700288 | tf_op jit(solution)/shard_map/transpose(jvp())/add_any | solution.py:64
  572.4 5.7 all-to-all-start.2
  578.2 6.1 convolution_convert_fusion.3
  599.5 68.0 %attend_back.1 = (bf16[8,3,128,384]{3,2,1,0:T(8,128)(2,1)}, f32[3,128,64]{2,1,0:T(8,128)}) custom-call(bf16[8,3,128,384]{3,2,1,0:T(8,128)(2,1)} %all-to-all-done.x_ref, bf16[8,3,128,128]{3,2,1,0:T(8,128)(2,1)} %all-to-all-done.2.grad_ref, bf16[3,2,1024,1024]{3,2,1,0:T(8,128)(2,1)} %get-tuple-element.32.probs_ref, bf16[128,64]{1,0:T(8,128)(2,1)} %pad.204.table_ref), custom_call_target="tpu_custom_call" | custom-call | flops 12884901888 | bytes 12582912 | tf_op jit(solution)/shard_map/attend_back/pallas_call | solution.py:363
  705.3 18.4 %collective-permute-done.51 = bf16[4,1,512,256]{3,2,1,0:T(8,128)(2,1)S(1)} collective-permute-done((bf16[4,1,512,256]{3,2,1,0:T(8,128)(2,1)S(1)}, bf16[4,1,512,256]{3,2,1,0:T(8,128)(2,1)S(1)}, u32[]{:S(2)}, u32[]{:S(2)}) %collective-permute-start.51) | collective-permute-done | bytes 1048608 | tf_op jit(solution)/shard_map/ppermute | solution.py:32
  734.1 5.1 multiply_reduce_fusion.34
  742.8 10.9 %convert_reduce_fusion.1 = (f32[4096]{0:T(1024)S(1)}, bf16[384,4096]{1,0:T(8,128)(2,1)S(1)}) fusion(f32[384,4096]{1,0:T(8,128)} %get-tuple-element.278, f32[4096]{0:T(1024)S(1)} %bitcast.613, bf16[384,1024]{1,0:T(8,128)(2,1)S(1)} %get-tuple-element.124, bf16[1024,4096]{1,0:T(8,128)(2,1)} %place.7), kind=kOutput, calls=%fused_computation.13 | convolution fusion | flops 3241668608 | bytes 18644992 | tf_op jit(solution)/shard_map/dot_general | solution.py:68
  767.9 6.4 convolution_convert_fusion.1
  793.9 5.8 collective-permute-done.70
  804.1 5.1 collective-permute-done.71
  813.8 5.0 collective-permute-done.72
  824.2 8.7 collective-permute-done.73
  836.7 6.8 collective-permute-done.56
  878.3 14.7 %collective-permute-done.43 = bf16[4,1,384,512]{3,2,0,1:T(8,128)(2,1)} collective-permute-done((bf16[4,1,384,512]{3,2,0,1:T(8,128)(2,1)}, bf16[4,1,384,512]{3,2,0,1:T(8,128)(2,1)}, u32[]{:S(2)}, u32[]{:S(2)}) %collective-permute-start.43) | collective-permute-done | bytes 1572896 | tf_op jit(solution)/shard_map/ppermute | solution.py:32
  906.0 28.0 %collective-permute-done.44 = bf16[4,1,384,256]{3,2,0,1:T(8,128)(2,1)} collective-permute-done((bf16[4,1,384,256]{3,2,0,1:T(8,128)(2,1)}, bf16[4,1,384,256]{3,2,0,1:T(8,128)(2,1)}, u32[]{:S(2)}, u32[]{:S(2)}) %collective-permute-start.44) | collective-permute-done | bytes 786464 | tf_op jit(solution)/shard_map/ppermute | solution.py:32
  956.4 9.4 collective-permute-done.34
  975.6 27.6 %collective-permute-done.35 = bf16[2,1,512,256]{2,3,1,0:T(8,128)(2,1)} collective-permute-done((bf16[2,1,512,256]{2,3,1,0:T(8,128)(2,1)}, bf16[2,1,512,256]{2,3,1,0:T(8,128)(2,1)}, u32[]{:S(2)}, u32[]{:S(2)}) %collective-permute-start.35) | collective-permute-done | bytes 524320 | tf_op jit(solution)/shard_map/ppermute | solution.py:32
  1004.5 9.8 collective-permute-done.40
  (890 shorter events, 408.3 us)
Async XLA Ops:
  12.1 38.5 %collective-permute-start.1 = (bf16[2,512,256]{2,1,0:T(8,128)(2,1)S(1)}, bf16[2,512,256]{2,1,0:T(8,128)(2,1)S(1)}, u32[]{:S(2)}, u32[]{:S(2)}) collective-permute-start(bf16[2,512,256]{2,1,0:T(8,128)(2,1)S(1)} %pad_maximum_fusion.14), channel_id=1, source_target_pairs={{0,4},{2,6},{4,0},{6,2},{1,5},{3,7},{5,1},{7,3},{8,12},{10,14},{12... | collective-permute-start | bytes 1572872 | tf_op jit(solution)/shard_map/ppermute | solution.py:32
  21.9 37.2 %collective-permute-start.6 = (bf16[2,128,1024]{2,1,0:T(8,128)(2,1)S(1)}, bf16[2,128,1024]{2,1,0:T(8,128)(2,1)S(1)}, u32[]{:S(2)}, u32[]{:S(2)}) collective-permute-start(bf16[2,128,1024]{2,1,0:T(8,128)(2,1)S(1)} %pad_maximum_fusion.15), channel_id=1, source_target_pairs={{0,4},{2,6},{4,0},{6,2},{1,5},{3,7},{5,1},{7,3},{8,12},{10,14},{12... | collective-permute-start | bytes 1572872 | tf_op jit(solution)/shard_map/ppermute | solution.py:32
  60.2 26.4 %collective-permute-start.7 = (bf16[4,128,1024]{2,1,0:T(8,128)(2,1)}, bf16[4,128,1024]{2,1,0:T(8,128)(2,1)}, u32[]{:S(2)}, u32[]{:S(2)}) collective-permute-start(bf16[4,128,1024]{2,1,0:T(8,128)(2,1)} %pad_maximum_fusion.9), channel_id=1, source_target_pairs={{0,16},{8,24},{16,0},{24,8},{1,17},{9,25},{17,1},{25,9},{2,18},{10... | collective-permute-start | bytes 3145736 | tf_op jit(solution)/shard_map/ppermute | solution.py:32
  61.8 94.8 %collective-permute-start.26 = (bf16[1,128,1024]{2,1,0:T(8,128)(2,1)S(1)}, bf16[1,128,1024]{2,1,0:T(8,128)(2,1)}, u32[]{:S(2)}, u32[]{:S(2)}) collective-permute-start(bf16[1,128,1024]{2,1,0:T(8,128)(2,1)S(1)} %bitcast.423), channel_id=1, source_target_pairs={{0,2},{2,0},{4,6},{6,4},{1,3},{3,1},{5,7},{7,5},{8,10},{10,8},{12,... | collective-permute-start | bytes 786440 | tf_op jit(solution)/shard_map/ppermute | solution.py:32
  63.8 93.9 %collective-permute-start.21 = (bf16[1,512,256]{2,1,0:T(8,128)(2,1)S(1)}, bf16[1,512,256]{2,1,0:T(8,128)(2,1)}, u32[]{:S(2)}, u32[]{:S(2)}) collective-permute-start(bf16[1,512,256]{2,1,0:T(8,128)(2,1)S(1)} %bitcast.427), channel_id=1, source_target_pairs={{0,2},{2,0},{4,6},{6,4},{1,3},{3,1},{5,7},{7,5},{8,10},{10,8},{12,... | collective-permute-start | bytes 786440 | tf_op jit(solution)/shard_map/ppermute | solution.py:32
  74.6 53.4 %collective-permute-start.3 = (bf16[8,512,256]{2,1,0:T(8,128)(2,1)}, bf16[8,512,256]{2,1,0:T(8,128)(2,1)}, u32[]{:S(2)}, u32[]{:S(2)}) collective-permute-start(bf16[8,512,256]{2,1,0:T(8,128)(2,1)} %pad_maximum_fusion.1), channel_id=1, source_target_pairs={{0,16},{8,24},{16,0},{24,8},{1,17},{9,25},{17,1},{25,9},{2,18},{10... | collective-permute-start | bytes 6291464 | tf_op jit(solution)/shard_map/ppermute | solution.py:32
  89.5 48.9 %collective-permute-start.8 = (bf16[8,128,1024]{2,1,0:T(8,128)(2,1)}, bf16[8,128,1024]{2,1,0:T(8,128)(2,1)}, u32[]{:S(2)}, u32[]{:S(2)}) collective-permute-start(bf16[8,128,1024]{2,1,0:T(8,128)(2,1)} %pad_maximum_fusion.2), channel_id=1, source_target_pairs={{0,1},{1,0},{2,3},{3,2},{4,5},{5,4},{6,7},{7,6},{8,9},{9,8},{10,11... | collective-permute-start | bytes 6291464 | tf_op jit(solution)/shard_map/ppermute | solution.py:32
  111.1 41.5 %collective-permute-start.12 = (bf16[4,512,256]{2,1,0:T(8,128)(2,1)S(1)}, bf16[4,512,256]{2,1,0:T(8,128)(2,1)S(1)}, u32[]{:S(2)}, u32[]{:S(2)}) collective-permute-start(bf16[4,512,256]{2,1,0:T(8,128)(2,1)S(1)} %pad_maximum_fusion.10), channel_id=1, source_target_pairs={{0,1},{1,0},{2,3},{3,2},{4,5},{5,4},{6,7},{7,6},{8,9},{9,8},{10,11... | collective-permute-start | bytes 3145736 | tf_op jit(solution)/shard_map/ppermute | solution.py:32
  131.1 96.7 %collective-permute-start.4 = (bf16[16,512,256]{2,1,0:T(8,128)(2,1)}, bf16[16,512,256]{2,1,0:T(8,128)(2,1)}, u32[]{:S(2)}, u32[]{:S(2)}) collective-permute-start(bf16[16,512,256]{2,1,0:T(8,128)(2,1)} %constant_dynamic-update-slice_fusion.own_ref), channel_id=1, source_target_pairs={{0,8},{8,0},{16,24},{24,16},{1,9},{9,1},{17,25},{25,17},{2,10},{10... | collective-permute-start | bytes 12582920 | tf_op jit(solution)/shard_map/ppermute | solution.py:32
  141.4 99.8 %collective-permute-start.9 = (bf16[16,128,1024]{2,1,0:T(8,128)(2,1)}, bf16[16,128,1024]{2,1,0:T(8,128)(2,1)}, u32[]{:S(2)}, u32[]{:S(2)}) collective-permute-start(bf16[16,128,1024]{2,1,0:T(8,128)(2,1)} %constant_dynamic-update-slice_fusion.5.own_ref), channel_id=1, source_target_pairs={{0,8},{8,0},{16,24},{24,16},{1,9},{9,1},{17,25},{25,17},{2,10},{10... | collective-permute-start | bytes 12582920 | tf_op jit(solution)/shard_map/ppermute | solution.py:32
  154.2 47.4 %collective-permute-start.13 = (bf16[8,512,256]{2,1,0:T(8,128)(2,1)}, bf16[8,512,256]{2,1,0:T(8,128)(2,1)}, u32[]{:S(2)}, u32[]{:S(2)}) collective-permute-start(bf16[8,512,256]{2,1,0:T(8,128)(2,1)} %pad_maximum_fusion.3), channel_id=1, source_target_pairs={{0,16},{8,24},{16,0},{24,8},{1,17},{9,25},{17,1},{25,9},{2,18},{10... | collective-permute-start | bytes 6291464 | tf_op jit(solution)/shard_map/ppermute | solution.py:32
  157.6 32.2 %collective-permute-start.27 = (bf16[2,128,1024]{2,1,0:T(8,128)(2,1)S(1)}, bf16[2,128,1024]{2,1,0:T(8,128)(2,1)S(1)}, u32[]{:S(2)}, u32[]{:S(2)}) collective-permute-start(bf16[2,128,1024]{2,1,0:T(8,128)(2,1)S(1)} %pad_maximum_fusion.18), channel_id=1, source_target_pairs={{0,4},{2,6},{4,0},{6,2},{1,5},{3,7},{5,1},{7,3},{8,12},{10,14},{12... | collective-permute-start | bytes 1572872 | tf_op jit(solution)/shard_map/ppermute | solution.py:32
  158.7 39.1 %collective-permute-start.22 = (bf16[2,512,256]{2,1,0:T(8,128)(2,1)S(1)}, bf16[2,512,256]{2,1,0:T(8,128)(2,1)S(1)}, u32[]{:S(2)}, u32[]{:S(2)}) collective-permute-start(bf16[2,512,256]{2,1,0:T(8,128)(2,1)S(1)} %pad_maximum_fusion.17), channel_id=1, source_target_pairs={{0,4},{2,6},{4,0},{6,2},{1,5},{3,7},{5,1},{7,3},{8,12},{10,14},{12... | collective-permute-start | bytes 1572872 | tf_op jit(solution)/shard_map/ppermute | solution.py:32
  205.8 64.4 %collective-permute-start.14 = (bf16[16,512,256]{2,1,0:T(8,128)(2,1)}, bf16[16,512,256]{2,1,0:T(8,128)(2,1)}, u32[]{:S(2)}, u32[]{:S(2)}) collective-permute-start(bf16[16,512,256]{2,1,0:T(8,128)(2,1)} %constant_dynamic-update-slice_fusion.10.own_ref), channel_id=1, source_target_pairs={{0,8},{8,0},{16,24},{24,16},{1,9},{9,1},{17,25},{25,17},{2,10},{10... | collective-permute-start | bytes 12582920 | tf_op jit(solution)/shard_map/ppermute | solution.py:32
  221.1 77.4 %collective-permute-start.16 = (bf16[2,384,256]{2,1,0:T(8,128)(2,1)}, bf16[2,384,256]{2,1,0:T(8,128)(2,1)}, u32[]{:S(2)}, u32[]{:S(2)}) collective-permute-start(bf16[2,384,256]{2,1,0:T(8,128)(2,1)} %pad_maximum_fusion.19), channel_id=1, source_target_pairs={{0,4},{2,6},{4,0},{6,2},{1,5},{3,7},{5,1},{7,3},{8,12},{10,14},{12... | collective-permute-start | bytes 1179656 | tf_op jit(solution)/shard_map/ppermute | solution.py:32
  224.9 102.5 %collective-permute-start.29 = (bf16[8,128,1024]{2,1,0:T(8,128)(2,1)}, bf16[8,128,1024]{2,1,0:T(8,128)(2,1)}, u32[]{:S(2)}, u32[]{:S(2)}) collective-permute-start(bf16[8,128,1024]{2,1,0:T(8,128)(2,1)} %pad_maximum_fusion.5), channel_id=1, source_target_pairs={{0,1},{1,0},{2,3},{3,2},{4,5},{5,4},{6,7},{7,6},{8,9},{9,8},{10,11... | collective-permute-start | bytes 6291464 | tf_op jit(solution)/shard_map/ppermute | solution.py:32
  227.8 96.5 %collective-permute-start.24 = (bf16[8,512,256]{2,1,0:T(8,128)(2,1)}, bf16[8,512,256]{2,1,0:T(8,128)(2,1)}, u32[]{:S(2)}, u32[]{:S(2)}) collective-permute-start(bf16[8,512,256]{2,1,0:T(8,128)(2,1)} %pad_maximum_fusion.4), channel_id=1, source_target_pairs={{0,16},{8,24},{16,0},{24,8},{1,17},{9,25},{17,1},{25,9},{2,18},{10... | collective-permute-start | bytes 6291464 | tf_op jit(solution)/shard_map/ppermute | solution.py:32
  291.9 73.3 %all-to-all-start = ((bf16[8,3,128,384]{3,2,1,0:T(8,128)(2,1)}), bf16[8,3,128,384]{3,2,1,0:T(8,128)(2,1)}, u32[]{:S(2)}, u32[]{:S(2)}) async-start(bf16[8,3,128,384]{3,2,1,0:T(8,128)(2,1)} %bitcast.418), calls=%async_computation | async-start | bytes 4718592 | tf_op jit(solution)/shard_map/all_to_all | solution.py:395
  318.4 44.7 %collective-permute-start.18 = (bf16[8,384,256]{2,1,0:T(8,128)(2,1)S(1)}, bf16[8,384,256]{2,1,0:T(8,128)(2,1)S(1)}, u32[]{:S(2)}, u32[]{:S(2)}) collective-permute-start(bf16[8,384,256]{2,1,0:T(8,128)(2,1)S(1)} %pad_maximum_fusion.6), channel_id=1, source_target_pairs={{0,1},{1,0},{2,3},{3,2},{4,5},{5,4},{6,7},{7,6},{8,9},{9,8},{10,11... | collective-permute-start | bytes 4718600 | tf_op jit(solution)/shard_map/ppermute | solution.py:32
  327.4 86.6 %collective-permute-start.25 = (bf16[16,512,256]{2,1,0:T(8,128)(2,1)}, bf16[16,512,256]{2,1,0:T(8,128)(2,1)}, u32[]{:S(2)}, u32[]{:S(2)}) collective-permute-start(bf16[16,512,256]{2,1,0:T(8,128)(2,1)} %constant_dynamic-update-slice_fusion.20.own_ref), channel_id=1, source_target_pairs={{0,8},{8,0},{16,24},{24,16},{1,9},{9,1},{17,25},{25,17},{2,10},{10... | collective-permute-start | bytes 12582920 | tf_op jit(solution)/shard_map/ppermute | solution.py:32
  330.5 96.1 %collective-permute-start.30 = (bf16[16,128,1024]{2,1,0:T(8,128)(2,1)}, bf16[16,128,1024]{2,1,0:T(8,128)(2,1)}, u32[]{:S(2)}, u32[]{:S(2)}) collective-permute-start(bf16[16,128,1024]{2,1,0:T(8,128)(2,1)} %constant_dynamic-update-slice_fusion.25.own_ref), channel_id=1, source_target_pairs={{0,8},{8,0},{16,24},{24,16},{1,9},{9,1},{17,25},{25,17},{2,10},{10... | collective-permute-start | bytes 12582920 | tf_op jit(solution)/shard_map/ppermute | solution.py:32
  364.4 37.4 %collective-permute-start.19 = (bf16[16,384,256]{2,1,0:T(8,128)(2,1)}, bf16[16,384,256]{2,1,0:T(8,128)(2,1)}, u32[]{:S(2)}, u32[]{:S(2)}) collective-permute-start(bf16[16,384,256]{2,1,0:T(8,128)(2,1)} %constant_dynamic-update-slice_fusion.15.own_ref), channel_id=1, source_target_pairs={{0,8},{8,0},{16,24},{24,16},{1,9},{9,1},{17,25},{25,17},{2,10},{10... | collective-permute-start | bytes 9437192 | tf_op jit(solution)/shard_map/ppermute | solution.py:32
  394.8 44.4 %all-to-all-start.1 = ((bf16[8,3,128,128]{3,2,1,0:T(8,128)(2,1)}), bf16[8,3,128,128]{3,2,1,0:T(8,128)(2,1)S(1)}, u32[]{:S(2)}, u32[]{:S(2)}) async-start(bf16[8,3,128,128]{3,2,1,0:T(8,128)(2,1)} %get-tuple-element.28), calls=%async_computation.1 | async-start | bytes 1572864 | tf_op jit(solution)/shard_map/all_to_all | solution.py:395
  546.1 38.9 %collective-permute-start.48 = (bf16[1024,512]{1,0:T(8,128)(2,1)}, bf16[1024,512]{1,0:T(8,128)(2,1)}, u32[]{:S(2)}, u32[]{:S(2)}) collective-permute-start(bf16[1024,512]{1,0:T(8,128)(2,1)} %convolution_convert_fusion.7), channel_id=1, source_target_pairs={{0,8},{8,0},{16,24},{24,16},{1,9},{9,1},{17,25},{25,17},{2,10},{10... | collective-permute-start | bytes 3145736 | tf_op jit(solution)/shard_map/ppermute | solution.py:32
  551.8 136.5 %collective-permute-start.54 = (bf16[4096,512]{1,0:T(8,128)(2,1)}, bf16[4096,512]{1,0:T(8,128)(2,1)}, u32[]{:S(2)}, u32[]{:S(2)}) collective-permute-start(bf16[4096,512]{1,0:T(8,128)(2,1)} %convolution_convert_fusion), channel_id=1, source_target_pairs={{0,8},{8,0},{16,24},{24,16},{1,9},{9,1},{17,25},{25,17},{2,10},{10... | collective-permute-start | bytes 12582920 | tf_op jit(solution)/shard_map/ppermute | solution.py:32
  572.4 27.1 %all-to-all-start.2 = ((bf16[8,3,128,128]{3,2,1,0:T(8,128)(2,1)}), bf16[8,3,128,128]{3,2,1,0:T(8,128)(2,1)}, u32[]{:S(2)}, u32[]{:S(2)}) async-start(bf16[8,3,128,128]{3,2,1,0:T(8,128)(2,1)} %bitcast.463), calls=%async_computation.2 | async-start | bytes 1572864 | tf_op jit(solution)/shard_map/all_to_all | solution.py:395
  584.3 112.4 %collective-permute-start.59 = (bf16[1024,2048]{1,0:T(8,128)(2,1)}, bf16[1024,2048]{1,0:T(8,128)(2,1)}, u32[]{:S(2)}, u32[]{:S(2)}) collective-permute-start(bf16[1024,2048]{1,0:T(8,128)(2,1)} %convolution_convert_fusion.3), channel_id=1, source_target_pairs={{0,8},{8,0},{16,24},{24,16},{1,9},{9,1},{17,25},{25,17},{2,10},{10... | collective-permute-start | bytes 12582920 | tf_op jit(solution)/shard_map/ppermute | solution.py:32
  595.3 88.0 %collective-permute-start.50 = (bf16[4,2,512,256]{3,2,1,0:T(8,128)(2,1)}, bf16[4,2,512,256]{3,2,1,0:T(8,128)(2,1)}, u32[]{:S(2)}, u32[]{:S(2)}) collective-permute-start(bf16[4,2,512,256]{3,2,1,0:T(8,128)(2,1)} %slice.634), channel_id=1, source_target_pairs={{0,16},{8,24},{16,0},{24,8},{1,17},{9,25},{17,1},{25,9},{2,18},{10... | collective-permute-start | bytes 6291464 | tf_op jit(solution)/shard_map/ppermute | solution.py:32
  667.5 62.2 %all-to-all-start.3 = ((bf16[8,3,128,384]{3,2,1,0:T(8,128)(2,1)}), bf16[8,3,128,384]{3,2,1,0:T(8,128)(2,1)}, u32[]{:S(2)}, u32[]{:S(2)}) async-start(bf16[8,3,128,384]{3,2,1,0:T(8,128)(2,1)} %get-tuple-element.33), calls=%async_computation.3 | async-start | bytes 4718592 | tf_op jit(solution)/shard_map/all_to_all | solution.py:395
  686.3 37.4 %collective-permute-start.51 = (bf16[4,1,512,256]{3,2,1,0:T(8,128)(2,1)S(1)}, bf16[4,1,512,256]{3,2,1,0:T(8,128)(2,1)S(1)}, u32[]{:S(2)}, u32[]{:S(2)}) collective-permute-start(bf16[4,1,512,256]{3,2,1,0:T(8,128)(2,1)S(1)} %constant_dynamic-slice_fusion.12), channel_id=1, source_target_pairs={{0,1},{1,0},{2,3},{3,2},{4,5},{5,4},{6,7},{7,6},{8,9},{9,8},{10,11... | collective-permute-start | bytes 3145736 | tf_op jit(solution)/shard_map/ppermute | solution.py:32
  695.8 114.8 %collective-permute-start.55 = (bf16[4,1,512,512]{3,2,0,1:T(8,128)(2,1)}, bf16[4,1,512,512]{3,2,0,1:T(8,128)(2,1)}, u32[]{:S(2)}, u32[]{:S(2)}) collective-permute-start(bf16[4,1,512,512]{3,2,0,1:T(8,128)(2,1)} %dynamic-slice_bitcast_fusion), channel_id=1, source_target_pairs={{0,1},{1,0},{2,3},{3,2},{4,5},{5,4},{6,7},{7,6},{8,9},{9,8},{10,11... | collective-permute-start | bytes 6291464 | tf_op jit(solution)/shard_map/ppermute | solution.py:32
  703.9 116.2 %collective-permute-start.60 = (bf16[4,2,128,1024]{3,2,1,0:T(8,128)(2,1)}, bf16[4,2,128,1024]{3,2,1,0:T(8,128)(2,1)}, u32[]{:S(2)}, u32[]{:S(2)}) collective-permute-start(bf16[4,2,128,1024]{3,2,1,0:T(8,128)(2,1)} %slice.641), channel_id=1, source_target_pairs={{0,16},{8,24},{16,0},{24,8},{1,17},{9,25},{17,1},{25,9},{2,18},{10... | collective-permute-start | bytes 6291464 | tf_op jit(solution)/shard_map/ppermute | solution.py:32
  725.4 67.0 %collective-permute-start.52 = (bf16[2,1,512,256]{2,3,1,0:T(8,128)(2,1)}, bf16[2,1,512,256]{2,3,1,0:T(8,128)(2,1)}, u32[]{:S(2)}, u32[]{:S(2)}) collective-permute-start(bf16[2,1,512,256]{2,3,1,0:T(8,128)(2,1)} %dynamic-slice_bitcast_fusion.5), channel_id=1, source_target_pairs={{0,4},{2,6},{4,0},{6,2},{1,5},{3,7},{5,1},{7,3},{8,12},{10,14},{12... | collective-permute-start | bytes 1572872 | tf_op jit(solution)/shard_map/ppermute | solution.py:32
  766.0 25.6 %collective-permute-start.69 = (f32[56,1024]{1,0:T(8,128)}, f32[56,1024]{1,0:T(8,128)S(1)}, u32[]{:S(2)}, u32[]{:S(2)}) collective-permute-start(f32[56,1024]{1,0:T(8,128)} %reshape.946), channel_id=1, source_target_pairs={{0,8},{8,0},{16,24},{24,16},{1,9},{9,1},{17,25},{25,17},{2,10},{10... | collective-permute-start | bytes 688136 | tf_op jit(solution)/shard_map/ppermute | solution.py:32
  791.6 63.9 %collective-permute-start.32 = (bf16[4096,512]{1,0:T(8,128)(2,1)}, bf16[4096,512]{1,0:T(8,128)(2,1)}, u32[]{:S(2)}, u32[]{:S(2)}) collective-permute-start(bf16[4096,512]{1,0:T(8,128)(2,1)} %convolution_convert_fusion.1), channel_id=1, source_target_pairs={{0,8},{8,0},{16,24},{24,16},{1,9},{9,1},{17,25},{25,17},{2,10},{10... | collective-permute-start | bytes 12582920 | tf_op jit(solution)/shard_map/ppermute | solution.py:32
  799.7 47.7 %collective-permute-start.42 = (bf16[3072,512]{1,0:T(8,128)(2,1)}, bf16[3072,512]{1,0:T(8,128)(2,1)}, u32[]{:S(2)}, u32[]{:S(2)}) collective-permute-start(bf16[3072,512]{1,0:T(8,128)(2,1)} %convolution_convert_fusion.2), channel_id=1, source_target_pairs={{0,8},{8,0},{16,24},{24,16},{1,9},{9,1},{17,25},{25,17},{2,10},{10... | collective-permute-start | bytes 9437192 | tf_op jit(solution)/shard_map/ppermute | solution.py:32
  809.2 54.1 %collective-permute-start.37 = (bf16[1024,2048]{1,0:T(8,128)(2,1)}, bf16[1024,2048]{1,0:T(8,128)(2,1)}, u32[]{:S(2)}, u32[]{:S(2)}) collective-permute-start(bf16[1024,2048]{1,0:T(8,128)(2,1)} %convolution_convert_fusion.4), channel_id=1, source_target_pairs={{0,8},{8,0},{16,24},{24,16},{1,9},{9,1},{17,25},{25,17},{2,10},{10... | collective-permute-start | bytes 12582920 | tf_op jit(solution)/shard_map/ppermute | solution.py:32
  833.0 39.2 %collective-permute-start.61 = (bf16[4,1,128,1024]{3,2,1,0:T(8,128)(2,1)}, bf16[4,1,128,1024]{3,2,1,0:T(8,128)(2,1)}, u32[]{:S(2)}, u32[]{:S(2)}) collective-permute-start(bf16[4,1,128,1024]{3,2,1,0:T(8,128)(2,1)} %constant_dynamic-slice_fusion.1), channel_id=1, source_target_pairs={{0,1},{1,0},{2,3},{3,2},{4,5},{5,4},{6,7},{7,6},{8,9},{9,8},{10,11... | collective-permute-start | bytes 3145736 | tf_op jit(solution)/shard_map/ppermute | solution.py:32
  847.2 52.7 %collective-permute-start.57 = (bf16[2,1,512,256]{2,3,1,0:T(8,128)(2,1)}, bf16[2,1,512,256]{2,3,1,0:T(8,128)(2,1)}, u32[]{:S(2)}, u32[]{:S(2)}) collective-permute-start(bf16[2,1,512,256]{2,3,1,0:T(8,128)(2,1)} %dynamic-slice_bitcast_fusion.4), channel_id=1, source_target_pairs={{0,4},{2,6},{4,0},{6,2},{1,5},{3,7},{5,1},{7,3},{8,12},{10,14},{12... | collective-permute-start | bytes 1572872 | tf_op jit(solution)/shard_map/ppermute | solution.py:32
  853.7 39.3 %collective-permute-start.43 = (bf16[4,1,384,512]{3,2,0,1:T(8,128)(2,1)}, bf16[4,1,384,512]{3,2,0,1:T(8,128)(2,1)}, u32[]{:S(2)}, u32[]{:S(2)}) collective-permute-start(bf16[4,1,384,512]{3,2,0,1:T(8,128)(2,1)} %dynamic-slice_bitcast_fusion.2), channel_id=1, source_target_pairs={{0,1},{1,0},{2,3},{3,2},{4,5},{5,4},{6,7},{7,6},{8,9},{9,8},{10,11... | collective-permute-start | bytes 4718600 | tf_op jit(solution)/shard_map/ppermute | solution.py:32
  863.0 77.4 %collective-permute-start.33 = (bf16[4,1,512,512]{3,2,0,1:T(8,128)(2,1)}, bf16[4,1,512,512]{3,2,0,1:T(8,128)(2,1)}, u32[]{:S(2)}, u32[]{:S(2)}) collective-permute-start(bf16[4,1,512,512]{3,2,0,1:T(8,128)(2,1)} %dynamic-slice_bitcast_fusion.1), channel_id=1, source_target_pairs={{0,1},{1,0},{2,3},{3,2},{4,5},{5,4},{6,7},{7,6},{8,9},{9,8},{10,11... | collective-permute-start | bytes 6291464 | tf_op jit(solution)/shard_map/ppermute | solution.py:32
  870.8 74.1 %collective-permute-start.38 = (bf16[4,2,128,1024]{3,2,1,0:T(8,128)(2,1)}, bf16[4,2,128,1024]{3,2,1,0:T(8,128)(2,1)}, u32[]{:S(2)}, u32[]{:S(2)}) collective-permute-start(bf16[4,2,128,1024]{3,2,1,0:T(8,128)(2,1)} %slice.627), channel_id=1, source_target_pairs={{0,16},{8,24},{16,0},{24,8},{1,17},{9,25},{17,1},{25,9},{2,18},{10... | collective-permute-start | bytes 6291464 | tf_op jit(solution)/shard_map/ppermute | solution.py:32
  875.6 26.3 %collective-permute-start.62 = (bf16[2,1,128,1024]{2,3,1,0:T(8,128)(2,1)}, bf16[2,1,128,1024]{2,3,1,0:T(8,128)(2,1)}, u32[]{:S(2)}, u32[]{:S(2)}) collective-permute-start(bf16[2,1,128,1024]{2,3,1,0:T(8,128)(2,1)} %dynamic-slice_bitcast_fusion.3), channel_id=1, source_target_pairs={{0,4},{2,6},{4,0},{6,2},{1,5},{3,7},{5,1},{7,3},{8,12},{10,14},{12... | collective-permute-start | bytes 1572872 | tf_op jit(solution)/shard_map/ppermute | solution.py:32
  896.3 37.6 %collective-permute-start.44 = (bf16[4,1,384,256]{3,2,0,1:T(8,128)(2,1)}, bf16[4,1,384,256]{3,2,0,1:T(8,128)(2,1)}, u32[]{:S(2)}, u32[]{:S(2)}) collective-permute-start(bf16[4,1,384,256]{3,2,0,1:T(8,128)(2,1)} %slice.629), channel_id=1, source_target_pairs={{0,16},{8,24},{16,0},{24,8},{1,17},{9,25},{17,1},{25,9},{2,18},{10... | collective-permute-start | bytes 2359304 | tf_op jit(solution)/shard_map/ppermute | solution.py:32
  901.9 48.0 %collective-permute-start.58 = (bf16[1,1,512,256]{2,3,1,0:T(8,128)(2,1)}, bf16[1,1,512,256]{2,3,1,0:T(8,128)(2,1)}, u32[]{:S(2)}, u32[]{:S(2)}) collective-permute-start(bf16[1,1,512,256]{2,3,1,0:T(8,128)(2,1)} %constant_dynamic-slice_fusion.6), channel_id=1, source_target_pairs={{0,2},{2,0},{4,6},{6,4},{1,3},{3,1},{5,7},{7,5},{8,10},{10,8},{12,... | collective-permute-start | bytes 786440 | tf_op jit(solution)/shard_map/ppermute | solution.py:32
  904.0 47.8 %collective-permute-start.63 = (bf16[1,1,128,1024]{2,3,1,0:T(8,128)(2,1)}, bf16[1,1,128,1024]{2,3,1,0:T(8,128)(2,1)}, u32[]{:S(2)}, u32[]{:S(2)}) collective-permute-start(bf16[1,1,128,1024]{2,3,1,0:T(8,128)(2,1)} %constant_dynamic-slice_fusion), channel_id=1, source_target_pairs={{0,2},{2,0},{4,6},{6,4},{1,3},{3,1},{5,7},{7,5},{8,10},{10,8},{12,... | collective-permute-start | bytes 786440 | tf_op jit(solution)/shard_map/ppermute | solution.py:32
  969.3 34.0 %collective-permute-start.35 = (bf16[2,1,512,256]{2,3,1,0:T(8,128)(2,1)}, bf16[2,1,512,256]{2,3,1,0:T(8,128)(2,1)}, u32[]{:S(2)}, u32[]{:S(2)}) collective-permute-start(bf16[2,1,512,256]{2,3,1,0:T(8,128)(2,1)} %dynamic-slice_bitcast_fusion.7), channel_id=1, source_target_pairs={{0,4},{2,6},{4,0},{6,2},{1,5},{3,7},{5,1},{7,3},{8,12},{10,14},{12... | collective-permute-start | bytes 1572872 | tf_op jit(solution)/shard_map/ppermute | solution.py:32
  973.2 41.2 %collective-permute-start.40 = (bf16[2,1,128,1024]{2,3,1,0:T(8,128)(2,1)S(1)}, bf16[2,1,128,1024]{2,3,1,0:T(8,128)(2,1)S(1)}, u32[]{:S(2)}, u32[]{:S(2)}) collective-permute-start(bf16[2,1,128,1024]{2,3,1,0:T(8,128)(2,1)S(1)} %dynamic-slice_bitcast_fusion.6), channel_id=1, source_target_pairs={{0,4},{2,6},{4,0},{6,2},{1,5},{3,7},{5,1},{7,3},{8,12},{10,14},{12... | collective-permute-start | bytes 1572872 | tf_op jit(solution)/shard_map/ppermute | solution.py:32
  (271 other events, 3562.8 us)

commit v2 on v1

--- a/solution.py
+++ b/solution.py
@@ -4,6 +4,7 @@
 import jax.numpy as jnp
 from jax import lax
 from jax.experimental import pallas as pl
+from jax.experimental.layout import Layout, with_layout_constraint
 from jax.experimental.pallas import tpu as pltpu
 from jax.sharding import PartitionSpec as P
 
@@ -87,70 +88,60 @@
     return coarse + (upper + fine if reverse else fine + upper)
 
 
-def place_table(steps):
-    count = 1 << len(steps)
-    index = jnp.arange(count, dtype=jnp.int32)
-    at = {
-        axis: jnp.full((count,), lax.axis_index(axis), jnp.int32)
-        for axis in ("clip", "coarse", "fine")
-    }
-    core = at["clip"] & 1
-    for step, (axis, bit) in enumerate(steps):
-        at[axis] = at[axis] ^ (((index >> step) & 1) << bit)
-    column = at["coarse"] * lax.axis_size("fine") + at["fine"]
-    return jnp.stack([column, at["clip"] >> 1, core])
-
-
-def place_kernel(splits, table, own_ref, other_ref, *outs):
-    width = own_ref.shape[2]
-    core = table[2, 0]
-
-    def write(first, second):
-        start = 0
-        for out, rows in zip(outs, splits):
-            out[:, :width] = first[0, start : start + rows, :]
-            out[:, width:] = second[0, start : start + rows, :]
-            start += rows
-
-    @pl.when(core == 0)
-    def own_first():
-        write(own_ref, other_ref)
-
-    @pl.when(core != 0)
-    def own_second():
-        write(other_ref, own_ref)
-
-
-def place(own, other, table, splits):
+def place_whole_kernel(splits, reverse, across, deep, uppers, here, own_ref, other_ref, *outs):
+    width = own_ref.shape[-1]
+    for left in range(across):
+        for upper in range(uppers):
+            for core, ref in enumerate((own_ref, other_ref)):
+                piece = ref.at[left, upper, 0] if reverse else ref.at[upper, left, 0]
+                lanes = pl.ds(
+                    pl.multiple_of(((here[2] ^ upper) * 2 + (here[3] ^ core)) * width, 128), width
+                )
+                start = 0
+                for out, rows in zip(outs, splits):
+                    at = pl.multiple_of((here[1] ^ left) * rows, 16)
+                    out[pl.ds(at, rows), lanes] = piece[start : start + rows, :]
+                    start += rows
+
+
+def place_whole(own, other, reverse, splits):
     pieces, rows, width = own.shape
-    columns = lax.axis_size(SEQ)
+    across, deep = lax.axis_size("fine"), lax.axis_size("coarse")
     uppers = lax.axis_size("clip") // 2
-    total = 2 * pieces * rows * width
+    lead = (across, uppers) if reverse else (uppers, across)
+    me = lax.axis_index("clip")
+    here = jnp.stack(
+        [lax.axis_index("coarse"), lax.axis_index("fine"), me >> 1, me & 1]
+    ).astype(jnp.int32)
+    spec = pl.BlockSpec((*lead, 1, rows, width), lambda z, here: (0, 0, z, 0, 0))
+    shape = (*lead, deep, rows, width)
     return pl.pallas_call(
-        functools.partial(place_kernel, splits),
+        functools.partial(place_whole_kernel, splits, reverse, across, deep, uppers),
         out_shape=[
-            jax.ShapeDtypeStruct((columns * part, uppers * 2 * width), bf16) for part in splits
+            jax.ShapeDtypeStruct((deep * across * part, uppers * 2 * width), bf16)
+            for part in splits
         ],
         grid_spec=pltpu.PrefetchScalarGridSpec(
             num_scalar_prefetch=1,
-            grid=(pieces,),
-            in_specs=[
-                pl.BlockSpec((1, rows, width), lambda p, table: (p, 0, 0)),
-                pl.BlockSpec((1, rows, width), lambda p, table: (p, 0, 0)),
-            ],
+            grid=(deep,),
+            in_specs=[spec, spec],
             out_specs=[
-                pl.BlockSpec((part, 2 * width), lambda p, table: (table[0, p], table[1, p]))
+                pl.BlockSpec(
+                    (across * part, uppers * 2 * width), lambda z, here: (here[0] ^ z, 0)
+                )
                 for part in splits
             ],
         ),
         compiler_params=pltpu.CompilerParams(vmem_limit_bytes=VMEM_BYTES),
-        cost_estimate=pl.CostEstimate(flops=0, bytes_accessed=4 * total, transcendentals=0),
+        cost_estimate=pl.CostEstimate(
+            flops=0, bytes_accessed=8 * pieces * rows * width, transcendentals=0
+        ),
         name="place",
-    )(table, own, other)
+    )(here, own.reshape(shape), other.reshape(shape))
 
 
 def gather_group(shard, steps):
-    held = shard[None]
+    held = with_layout_constraint(shard[None], Layout((0, 1, 2)))
     for axis, bit in steps:
         held = jnp.concatenate([held, swapped(held, axis, bit)], 0)
     return held, swapped(held, "clip", 0)
@@ -550,7 +541,6 @@
     peers = lax.axis_size(SEQ)
 
     orders = [gather_steps(False), gather_steps(True)]
-    tables = [place_table(steps) for steps in orders]
     groups = (
         ([first_up],),
         ([first_down],),
@@ -565,7 +555,7 @@
         splits = tuple(sum(shard.shape[1] for shard in part) for part in group)
         order = number % 2
         own, other = gather_group(jnp.concatenate(shards, 0), orders[order])
-        placed.extend(place(own, other, tables[order], splits))
+        placed.extend(place_whole(own, other, order == 1, splits))
     (
         up_first,
         down_first,

time: 1040 us -> 1010 us (0.971)
  Pallas kernels: 173 us -> 144 us
  waiting for transfers between devices: 348 us -> 361 us
  other arithmetic: 133 us -> 122 us
    pallas_call x6, Pallas kernels: 75.7 us -> 46.6 us  [place_whole(): pl.pallas_call(functools.partial(place_whole_kernel, splits, reverse, acr...]
    ppermute x72, waiting for transfers between devices: 340 us -> 353 us  [swapped(): return lax.ppermute(shard, axis, [(i, i ^ 1 << bit) for i in range(peers)])]
    concatenate x18, other arithmetic: 26.6 us -> 15.2 us  [gather_group(): held = jnp.concatenate([held, swapped(held, axis, bit)], 0)]
    unnamed x520 -> x548, local copies, waits for them, and re-layouts: 54.1 us -> 49.7 us
  transfers between devices with their start and end apart: 78 -> 78, of which waited for: 37 -> 38; matrix products, arithmetic and copies ran while one was open for 28% -> 27% of each run, Pallas kernels for 17% -> 14%
where the time goes in v2:
time: 1010 us; the launch traced here: 997 us
  waiting for transfers between devices  361 us (36%)
  Pallas kernels  144 us (14%)
  matrix products  143 us (14%)
  local copies, waits for them, and re-layouts  123 us (12%)
  other arithmetic  122 us (12%)
  starting transfers between devices  98.6 us (10%)
    ppermute x72, waiting for transfers between devices, swapped(): return lax.ppermute(shard, axis, [(i, i ^ 1 << bit) for i in range(peers)])  353 us
    ppermute x72, starting transfers between devices, swapped(): return lax.ppermute(shard, axis, [(i, i ^ 1 << bit) for i in range(peers)])  71.9 us
    pallas_call x1, Pallas kernels, attend_back(): pl.pallas_call(attend_back_kernel, out_shape=[jax.ShapeDtypeStruct(x.shap...  68 us
    dot_general x16, matrix products, weight_grad(): lax.dot_general(left, right, (((0,), (0,)), ((), ())), preferred_element_...  60.5 us
    unnamed x548, local copies, waits for them, and re-layouts  49.7 us
    pallas_call x6, Pallas kernels, place_whole(): pl.pallas_call(functools.partial(place_whole_kernel, splits, reverse, acr...  46.6 us
    dot_general x8, matrix products, product_t(): lax.dot_general(left, right, (((1,), (1,)), ((), ())), preferred_element_...  41.8 us
    dot_general x8, matrix products, product(): return jnp.dot(left, right, preferred_element_type=f32)  40.4 us
  transfers between devices with their start and end apart: 78, of which 38 were waited for; matrix products, arithmetic and copies ran while one was open for 27% of the time, Pallas kernels for 14%

profile of v2, /device:TPU:0, one launch (start us, length us, event | category | flops | bytes accessed | tf_op | source)
XLA Modules:
  0.0 997.0 jit_solution(5152268320680290344)
XLA Ops:
  6.2 5.9 collective-permute-done
  15.2 6.6 collective-permute-done.5
  22.0 28.6 %collective-permute-done.1 = bf16[2,512,256]{2,1,0:T(8,128)(2,1)S(1)} collective-permute-done((bf16[2,512,256]{2,1,0:T(8,128)(2,1)S(1)}, bf16[2,512,256]{2,1,0:T(8,128)(2,1)S(1)}, u32[]{:S(2)}, u32[]{:S(2)}) %collective-permute-start.1) | collective-permute-done | bytes 524320 | tf_op jit(solution)/shard_map/ppermute | solution.py:33
  52.6 6.6 collective-permute-done.6
  60.6 9.9 collective-permute-done.2
  73.2 12.2 %collective-permute-done.7 = bf16[4,128,1024]{2,1,0:T(8,128)(2,1)S(1)} collective-permute-done((bf16[4,128,1024]{2,1,0:T(8,128)(2,1)S(1)}, bf16[4,128,1024]{2,1,0:T(8,128)(2,1)S(1)}, u32[]{:S(2)}, u32[]{:S(2)}) %collective-permute-start.7) | collective-permute-done | bytes 1048608 | tf_op jit(solution)/shard_map/ppermute | solution.py:33
  93.3 7.4 collective-permute-done.10
  108.2 9.3 collective-permute-done.11
  129.9 6.1 collective-permute-done.8
  140.6 9.6 collective-permute-done.12
  164.6 24.2 %collective-permute-done.27 = bf16[2,128,1024]{2,1,0:T(8,128)(2,1)S(1)} collective-permute-done((bf16[2,128,1024]{2,1,0:T(8,128)(2,1)}, bf16[2,128,1024]{2,1,0:T(8,128)(2,1)S(1)}, u32[]{:S(2)}, u32[]{:S(2)}) %collective-permute-start.27) | collective-permute-done | bytes 524320 | tf_op jit(solution)/shard_map/ppermute | solution.py:33
  190.1 6.8 collective-permute-done.22
  207.4 12.5 %collective-permute-done.28 = bf16[4,128,1024]{2,1,0:T(8,128)(2,1)S(1)} collective-permute-done((bf16[4,128,1024]{2,1,0:T(8,128)(2,1)S(1)}, bf16[4,128,1024]{2,1,0:T(8,128)(2,1)S(1)}, u32[]{:S(2)}, u32[]{:S(2)}) %collective-permute-start.28) | collective-permute-done | bytes 1048608 | tf_op jit(solution)/shard_map/ppermute | solution.py:33
  226.0 8.5 place.6
  234.5 7.8 place.7
  242.3 11.4 %multiply_convert_fusion.1 = (bf16[384,4096]{1,0:T(8,128)(2,1)S(1)}, f32[384,4096]{1,0:T(8,128)}) fusion(f32[4096]{0:T(1024)S(1)} %bitcast.629, bf16[384,1024]{1,0:T(8,128)(2,1)S(1)} %copy-done.62, bf16[4096,1024]{1,0:T(8,128)(2,1)} %place.6), kind=kOutput, calls=%fused_computation.17 | convolution fusion | flops 3230662656 | bytes 18628608 | tf_op jit(solution)/shard_map/dot_general | solution.py:77
  259.8 8.0 place.8
  268.5 7.2 add_convert_fusion.5
  277.5 5.6 all-to-all-start
  289.8 12.1 %collective-permute-done.17 = bf16[4,384,256]{2,1,0:T(8,128)(2,1)S(1)} collective-permute-done((bf16[4,384,256]{2,1,0:T(8,128)(2,1)S(1)}, bf16[4,384,256]{2,1,0:T(8,128)(2,1)S(1)}, u32[]{:S(2)}, u32[]{:S(2)}) %collective-permute-start.17) | collective-permute-done | bytes 786464 | tf_op jit(solution)/shard_map/ppermute | solution.py:33
  318.7 29.1 %collective-permute-done.18 = bf16[8,384,256]{2,1,0:T(8,128)(2,1)S(1)} collective-permute-done((bf16[8,384,256]{2,1,0:T(8,128)(2,1)S(1)}, bf16[8,384,256]{2,1,0:T(8,128)(2,1)S(1)}, u32[]{:S(2)}, u32[]{:S(2)}) %collective-permute-start.18) | collective-permute-done | bytes 1572896 | tf_op jit(solution)/shard_map/ppermute | solution.py:33
  349.8 29.6 %attend.1 = (bf16[8,3,128,128]{3,2,1,0:T(8,128)(2,1)}, bf16[3,2,1024,1024]{3,2,1,0:T(8,128)(2,1)}) custom-call(s32[3]{0:T(128)} %lengths.1, bf16[8,3,128,384]{3,2,1,0:T(8,128)(2,1)} %all-to-all-done.x_ref, bf16[128,64]{1,0:T(8,128)(2,1)} %pad.204.table_ref), custom_call_target="tpu_custom_call" | custom-call | flops 6442450944 | bytes 12582912 | tf_op jit(solution)/shard_map/attend/pallas_call | solution.py:323
  379.4 5.5 all-to-all-start.1
  385.5 6.7 place.9
  392.2 7.9 place.10
  400.1 7.7 place.11
  423.7 7.5 fusion.147
  436.1 6.7 multiply_convert_fusion
  442.8 7.0 fusion.159
  454.5 10.9 %convert_reduce_fusion = (f32[4096]{0:T(1024)}, bf16[384,4096]{1,0:T(8,128)(2,1)S(1)}) fusion(f32[384,4096]{1,0:T(8,128)} %get-tuple-element.284, f32[4096]{0:T(1024)S(1)} %bitcast.632, bf16[384,1024]{1,0:T(8,128)(2,1)S(1)} %get-tuple-element.129, bf16[1024,4096]{1,0:T(8,128)(2,1)} %place.11), kind=kOutput, calls=%fused_computation.12 | convolution fusion | flops 3241668608 | bytes 18644992 | tf_op jit(solution)/shard_map/dot_general | solution.py:69
  485.5 9.8 broadcast_multiply_fusion
  495.3 16.1 %pad_add_fusion = f32[3,158,1024]{2,1,0:T(8,128)S(1)} fusion(f32[3,128,1024]{2,1,0:T(8,128)S(1)} %get-tuple-element.155, f32[3,128,1024]{2,1,0:T(8,128)S(1)} %get-tuple-element.156, f32[3,128,1024]{2,1,0:T(8,128)S(1)} %get-tuple-element.157, f32[3,128,1024]{2,1,0:T(8,128)} %get-tuple-element.158, f32[3,128,1024]{2,1,0:T(8,128)} %get-tuple-element.159, ...), kind=kLoop, calls=%fused_computation.62 | loop fusion | flops 14561280 | bytes 50700288 | tf_op jit(solution)/shard_map/transpose(jvp())/add_any | solution.py:65
  542.0 5.9 all-to-all-start.2
  547.9 6.3 convolution_convert_fusion.3
  568.8 68.0 %attend_back.1 = (bf16[8,3,128,384]{3,2,1,0:T(8,128)(2,1)}, f32[3,128,64]{2,1,0:T(8,128)}) custom-call(bf16[8,3,128,384]{3,2,1,0:T(8,128)(2,1)} %all-to-all-done.x_ref, bf16[8,3,128,128]{3,2,1,0:T(8,128)(2,1)} %all-to-all-done.2.grad_ref, bf16[3,2,1024,1024]{3,2,1,0:T(8,128)(2,1)} %get-tuple-element.32.probs_ref, bf16[128,64]{1,0:T(8,128)(2,1)} %pad.204.table_ref), custom_call_target="tpu_custom_call" | custom-call | flops 12884901888 | bytes 12582912 | tf_op jit(solution)/shard_map/attend_back/pallas_call | solution.py:354
  671.7 20.2 %collective-permute-done.51 = bf16[4,1,512,256]{3,2,1,0:T(8,128)(2,1)S(1)} collective-permute-done((bf16[4,1,512,256]{3,2,1,0:T(8,128)(2,1)S(1)}, bf16[4,1,512,256]{3,2,1,0:T(8,128)(2,1)S(1)}, u32[]{:S(2)}, u32[]{:S(2)}) %collective-permute-start.51) | collective-permute-done | bytes 1048608 | tf_op jit(solution)/shard_map/ppermute | solution.py:33
  700.6 5.1 multiply_reduce_fusion.34
  709.3 10.3 %convert_reduce_fusion.1 = (f32[4096]{0:T(1024)S(1)}, bf16[384,4096]{1,0:T(8,128)(2,1)S(1)}) fusion(f32[384,4096]{1,0:T(8,128)} %get-tuple-element.276, f32[4096]{0:T(1024)S(1)} %bitcast.630, bf16[384,1024]{1,0:T(8,128)(2,1)S(1)} %get-tuple-element.124, bf16[1024,4096]{1,0:T(8,128)(2,1)} %place.7), kind=kOutput, calls=%fused_computation.13 | convolution fusion | flops 3241668608 | bytes 18644992 | tf_op jit(solution)/shard_map/dot_general | solution.py:69
  732.9 6.3 convolution_convert_fusion.1
  749.0 5.3 collective-permute-start.67
  774.3 5.4 collective-permute-done.71
  794.5 8.9 collective-permute-done.73
  806.6 7.5 collective-permute-done.56
  848.6 14.9 %collective-permute-done.43 = bf16[4,1,384,512]{3,2,0,1:T(8,128)(2,1)} collective-permute-done((bf16[4,1,384,512]{3,2,0,1:T(8,128)(2,1)}, bf16[4,1,384,512]{3,2,0,1:T(8,128)(2,1)}, u32[]{:S(2)}, u32[]{:S(2)}) %collective-permute-start.43) | collective-permute-done | bytes 1572896 | tf_op jit(solution)/shard_map/ppermute | solution.py:33
  876.3 28.0 %collective-permute-done.44 = bf16[4,1,384,256]{3,2,0,1:T(8,128)(2,1)} collective-permute-done((bf16[4,1,384,256]{3,2,0,1:T(8,128)(2,1)}, bf16[4,1,384,256]{3,2,0,1:T(8,128)(2,1)}, u32[]{:S(2)}, u32[]{:S(2)}) %collective-permute-start.44) | collective-permute-done | bytes 786464 | tf_op jit(solution)/shard_map/ppermute | solution.py:33
  927.4 8.7 collective-permute-done.34
  946.0 28.6 %collective-permute-done.35 = bf16[2,1,512,256]{2,3,1,0:T(8,128)(2,1)} collective-permute-done((bf16[2,1,512,256]{2,3,1,0:T(8,128)(2,1)}, bf16[2,1,512,256]{2,3,1,0:T(8,128)(2,1)}, u32[]{:S(2)}, u32[]{:S(2)}) %collective-permute-start.35) | collective-permute-done | bytes 524320 | tf_op jit(solution)/shard_map/ppermute | solution.py:33
  975.9 8.9 collective-permute-done.40
  (911 shorter events, 403.3 us)
Async XLA Ops:
  12.1 38.5 %collective-permute-start.1 = (bf16[2,512,256]{2,1,0:T(8,128)(2,1)S(1)}, bf16[2,512,256]{2,1,0:T(8,128)(2,1)S(1)}, u32[]{:S(2)}, u32[]{:S(2)}) collective-permute-start(bf16[2,512,256]{2,1,0:T(8,128)(2,1)S(1)} %pad_maximum_fusion.14), channel_id=1, source_target_pairs={{0,4},{2,6},{4,0},{6,2},{1,5},{3,7},{5,1},{7,3},{8,12},{10,14},{12... | collective-permute-start | bytes 1572872 | tf_op jit(solution)/shard_map/ppermute | solution.py:33
  21.9 37.2 %collective-permute-start.6 = (bf16[2,128,1024]{2,1,0:T(8,128)(2,1)S(1)}, bf16[2,128,1024]{2,1,0:T(8,128)(2,1)S(1)}, u32[]{:S(2)}, u32[]{:S(2)}) collective-permute-start(bf16[2,128,1024]{2,1,0:T(8,128)(2,1)S(1)} %pad_maximum_fusion.15), channel_id=1, source_target_pairs={{0,4},{2,6},{4,0},{6,2},{1,5},{3,7},{5,1},{7,3},{8,12},{10,14},{12... | collective-permute-start | bytes 1572872 | tf_op jit(solution)/shard_map/ppermute | solution.py:33
  59.2 26.2 %collective-permute-start.7 = (bf16[4,128,1024]{2,1,0:T(8,128)(2,1)S(1)}, bf16[4,128,1024]{2,1,0:T(8,128)(2,1)S(1)}, u32[]{:S(2)}, u32[]{:S(2)}) collective-permute-start(bf16[4,128,1024]{2,1,0:T(8,128)(2,1)S(1)} %pad_maximum_fusion.9), channel_id=1, source_target_pairs={{0,16},{8,24},{16,0},{24,8},{1,17},{9,25},{17,1},{25,9},{2,18},{10... | collective-permute-start | bytes 3145736 | tf_op jit(solution)/shard_map/ppermute | solution.py:33
  72.3 54.6 %collective-permute-start.3 = (bf16[8,512,256]{2,1,0:T(8,128)(2,1)}, bf16[8,512,256]{2,1,0:T(8,128)(2,1)}, u32[]{:S(2)}, u32[]{:S(2)}) collective-permute-start(bf16[8,512,256]{2,1,0:T(8,128)(2,1)} %pad_maximum_fusion.1), channel_id=1, source_target_pairs={{0,16},{8,24},{16,0},{24,8},{1,17},{9,25},{17,1},{25,9},{2,18},{10... | collective-permute-start | bytes 6291464 | tf_op jit(solution)/shard_map/ppermute | solution.py:33
  87.1 48.9 %collective-permute-start.8 = (bf16[8,128,1024]{2,1,0:T(8,128)(2,1)}, bf16[8,128,1024]{2,1,0:T(8,128)(2,1)}, u32[]{:S(2)}, u32[]{:S(2)}) collective-permute-start(bf16[8,128,1024]{2,1,0:T(8,128)(2,1)} %pad_maximum_fusion.2), channel_id=1, source_target_pairs={{0,1},{1,0},{2,3},{3,2},{4,5},{5,4},{6,7},{7,6},{8,9},{9,8},{10,11... | collective-permute-start | bytes 6291464 | tf_op jit(solution)/shard_map/ppermute | solution.py:33
  90.0 65.6 %collective-permute-start.26 = (bf16[1,128,1024]{2,1,0:T(8,128)(2,1)S(1)}, bf16[1,128,1024]{2,1,0:T(8,128)(2,1)S(1)}, u32[]{:S(2)}, u32[]{:S(2)}) collective-permute-start(bf16[1,128,1024]{2,1,0:T(8,128)(2,1)S(1)} %bitcast.438), channel_id=1, source_target_pairs={{0,2},{2,0},{4,6},{6,4},{1,3},{3,1},{5,7},{7,5},{8,10},{10,8},{12,... | collective-permute-start | bytes 786440 | tf_op jit(solution)/shard_map/ppermute | solution.py:33
  92.5 64.0 %collective-permute-start.21 = (bf16[1,512,256]{2,1,0:T(8,128)(2,1)S(1)}, bf16[1,512,256]{2,1,0:T(8,128)(2,1)S(1)}, u32[]{:S(2)}, u32[]{:S(2)}) collective-permute-start(bf16[1,512,256]{2,1,0:T(8,128)(2,1)S(1)} %bitcast.442), channel_id=1, source_target_pairs={{0,2},{2,0},{4,6},{6,4},{1,3},{3,1},{5,7},{7,5},{8,10},{10,8},{12,... | collective-permute-start | bytes 786440 | tf_op jit(solution)/shard_map/ppermute | solution.py:33
  117.6 32.6 %collective-permute-start.12 = (bf16[4,512,256]{2,1,0:T(8,128)(2,1)S(1)}, bf16[4,512,256]{2,1,0:T(8,128)(2,1)S(1)}, u32[]{:S(2)}, u32[]{:S(2)}) collective-permute-start(bf16[4,512,256]{2,1,0:T(8,128)(2,1)S(1)} %pad_maximum_fusion.10), channel_id=1, source_target_pairs={{0,1},{1,0},{2,3},{3,2},{4,5},{5,4},{6,7},{7,6},{8,9},{9,8},{10,11... | collective-permute-start | bytes 3145736 | tf_op jit(solution)/shard_map/ppermute | solution.py:33
  129.9 95.8 %collective-permute-start.4 = (bf16[16,512,256]{2,1,0:T(8,128)(2,1)}, bf16[16,512,256]{2,1,0:T(8,128)(2,1)}, u32[]{:S(2)}, u32[]{:S(2)}) collective-permute-start(bf16[16,512,256]{2,1,0:T(8,128)(2,1)} %constant_dynamic-update-slice_fusion), channel_id=1, source_target_pairs={{0,8},{8,0},{16,24},{24,16},{1,9},{9,1},{17,25},{25,17},{2,10},{10... | collective-permute-start | bytes 12582920 | tf_op jit(solution)/shard_map/ppermute | solution.py:33
  139.1 95.4 %collective-permute-start.9 = (bf16[16,128,1024]{2,1,0:T(8,128)(2,1)}, bf16[16,128,1024]{2,1,0:T(8,128)(2,1)}, u32[]{:S(2)}, u32[]{:S(2)}) collective-permute-start(bf16[16,128,1024]{2,1,0:T(8,128)(2,1)} %constant_dynamic-update-slice_fusion.5), channel_id=1, source_target_pairs={{0,8},{8,0},{16,24},{24,16},{1,9},{9,1},{17,25},{25,17},{2,10},{10... | collective-permute-start | bytes 12582920 | tf_op jit(solution)/shard_map/ppermute | solution.py:33
  151.9 48.7 %collective-permute-start.13 = (bf16[8,512,256]{2,1,0:T(8,128)(2,1)}, bf16[8,512,256]{2,1,0:T(8,128)(2,1)}, u32[]{:S(2)}, u32[]{:S(2)}) collective-permute-start(bf16[8,512,256]{2,1,0:T(8,128)(2,1)} %pad_maximum_fusion.3), channel_id=1, source_target_pairs={{0,16},{8,24},{16,0},{24,8},{1,17},{9,25},{17,1},{25,9},{2,18},{10... | collective-permute-start | bytes 6291464 | tf_op jit(solution)/shard_map/ppermute | solution.py:33
  156.5 32.3 %collective-permute-start.27 = (bf16[2,128,1024]{2,1,0:T(8,128)(2,1)}, bf16[2,128,1024]{2,1,0:T(8,128)(2,1)S(1)}, u32[]{:S(2)}, u32[]{:S(2)}) collective-permute-start(bf16[2,128,1024]{2,1,0:T(8,128)(2,1)} %pad_maximum_fusion.18), channel_id=1, source_target_pairs={{0,4},{2,6},{4,0},{6,2},{1,5},{3,7},{5,1},{7,3},{8,12},{10,14},{12... | collective-permute-start | bytes 1572872 | tf_op jit(solution)/shard_map/ppermute | solution.py:33
  158.1 38.8 %collective-permute-start.22 = (bf16[2,512,256]{2,1,0:T(8,128)(2,1)}, bf16[2,512,256]{2,1,0:T(8,128)(2,1)S(1)}, u32[]{:S(2)}, u32[]{:S(2)}) collective-permute-start(bf16[2,512,256]{2,1,0:T(8,128)(2,1)} %pad_maximum_fusion.17), channel_id=1, source_target_pairs={{0,4},{2,6},{4,0},{6,2},{1,5},{3,7},{5,1},{7,3},{8,12},{10,14},{12... | collective-permute-start | bytes 1572872 | tf_op jit(solution)/shard_map/ppermute | solution.py:33
  204.0 53.8 %collective-permute-start.14 = (bf16[16,512,256]{2,1,0:T(8,128)(2,1)}, bf16[16,512,256]{2,1,0:T(8,128)(2,1)S(1)}, u32[]{:S(2)}, u32[]{:S(2)}) collective-permute-start(bf16[16,512,256]{2,1,0:T(8,128)(2,1)} %constant_dynamic-update-slice_fusion.10), channel_id=1, source_target_pairs={{0,8},{8,0},{16,24},{24,16},{1,9},{9,1},{17,25},{25,17},{2,10},{10... | collective-permute-start | bytes 12582920 | tf_op jit(solution)/shard_map/ppermute | solution.py:33
  219.9 63.2 %collective-permute-start.16 = (bf16[2,384,256]{2,1,0:T(8,128)(2,1)}, bf16[2,384,256]{2,1,0:T(8,128)(2,1)}, u32[]{:S(2)}, u32[]{:S(2)}) collective-permute-start(bf16[2,384,256]{2,1,0:T(8,128)(2,1)} %pad_maximum_fusion.19), channel_id=1, source_target_pairs={{0,4},{2,6},{4,0},{6,2},{1,5},{3,7},{5,1},{7,3},{8,12},{10,14},{12... | collective-permute-start | bytes 1179656 | tf_op jit(solution)/shard_map/ppermute | solution.py:33
  223.8 87.1 %collective-permute-start.29 = (bf16[8,128,1024]{2,1,0:T(8,128)(2,1)}, bf16[8,128,1024]{2,1,0:T(8,128)(2,1)}, u32[]{:S(2)}, u32[]{:S(2)}) collective-permute-start(bf16[8,128,1024]{2,1,0:T(8,128)(2,1)} %pad_maximum_fusion.5), channel_id=1, source_target_pairs={{0,1},{1,0},{2,3},{3,2},{4,5},{5,4},{6,7},{7,6},{8,9},{9,8},{10,11... | collective-permute-start | bytes 6291464 | tf_op jit(solution)/shard_map/ppermute | solution.py:33
  225.6 82.3 %collective-permute-start.24 = (bf16[8,512,256]{2,1,0:T(8,128)(2,1)}, bf16[8,512,256]{2,1,0:T(8,128)(2,1)}, u32[]{:S(2)}, u32[]{:S(2)}) collective-permute-start(bf16[8,512,256]{2,1,0:T(8,128)(2,1)} %pad_maximum_fusion.4), channel_id=1, source_target_pairs={{0,16},{8,24},{16,0},{24,8},{1,17},{9,25},{17,1},{25,9},{2,18},{10... | collective-permute-start | bytes 6291464 | tf_op jit(solution)/shard_map/ppermute | solution.py:33
  277.5 72.4 %all-to-all-start = ((bf16[8,3,128,384]{3,2,1,0:T(8,128)(2,1)}), bf16[8,3,128,384]{3,2,1,0:T(8,128)(2,1)}, u32[]{:S(2)}, u32[]{:S(2)}) async-start(bf16[8,3,128,384]{3,2,1,0:T(8,128)(2,1)} %bitcast.433), calls=%async_computation | async-start | bytes 4718592 | tf_op jit(solution)/shard_map/all_to_all | solution.py:386
  303.1 44.7 %collective-permute-start.18 = (bf16[8,384,256]{2,1,0:T(8,128)(2,1)S(1)}, bf16[8,384,256]{2,1,0:T(8,128)(2,1)S(1)}, u32[]{:S(2)}, u32[]{:S(2)}) collective-permute-start(bf16[8,384,256]{2,1,0:T(8,128)(2,1)S(1)} %pad_maximum_fusion.6), channel_id=1, source_target_pairs={{0,1},{1,0},{2,3},{3,2},{4,5},{5,4},{6,7},{7,6},{8,9},{9,8},{10,11... | collective-permute-start | bytes 4718600 | tf_op jit(solution)/shard_map/ppermute | solution.py:33
  310.9 81.3 %collective-permute-start.25 = (bf16[16,512,256]{2,1,0:T(8,128)(2,1)}, bf16[16,512,256]{2,1,0:T(8,128)(2,1)}, u32[]{:S(2)}, u32[]{:S(2)}) collective-permute-start(bf16[16,512,256]{2,1,0:T(8,128)(2,1)} %constant_dynamic-update-slice_fusion.20), channel_id=1, source_target_pairs={{0,8},{8,0},{16,24},{24,16},{1,9},{9,1},{17,25},{25,17},{2,10},{10... | collective-permute-start | bytes 12582920 | tf_op jit(solution)/shard_map/ppermute | solution.py:33
  314.1 86.0 %collective-permute-start.30 = (bf16[16,128,1024]{2,1,0:T(8,128)(2,1)}, bf16[16,128,1024]{2,1,0:T(8,128)(2,1)}, u32[]{:S(2)}, u32[]{:S(2)}) collective-permute-start(bf16[16,128,1024]{2,1,0:T(8,128)(2,1)} %constant_dynamic-update-slice_fusion.25), channel_id=1, source_target_pairs={{0,8},{8,0},{16,24},{24,16},{1,9},{9,1},{17,25},{25,17},{2,10},{10... | collective-permute-start | bytes 12582920 | tf_op jit(solution)/shard_map/ppermute | solution.py:33
  349.1 36.4 %collective-permute-start.19 = (bf16[16,384,256]{2,1,0:T(8,128)(2,1)}, bf16[16,384,256]{2,1,0:T(8,128)(2,1)}, u32[]{:S(2)}, u32[]{:S(2)}) collective-permute-start(bf16[16,384,256]{2,1,0:T(8,128)(2,1)} %constant_dynamic-update-slice_fusion.15), channel_id=1, source_target_pairs={{0,8},{8,0},{16,24},{24,16},{1,9},{9,1},{17,25},{25,17},{2,10},{10... | collective-permute-start | bytes 9437192 | tf_op jit(solution)/shard_map/ppermute | solution.py:33
  379.4 28.4 %all-to-all-start.1 = ((bf16[8,3,128,128]{3,2,1,0:T(8,128)(2,1)}), bf16[8,3,128,128]{3,2,1,0:T(8,128)(2,1)S(1)}, u32[]{:S(2)}, u32[]{:S(2)}) async-start(bf16[8,3,128,128]{3,2,1,0:T(8,128)(2,1)} %get-tuple-element.28), calls=%async_computation.1 | async-start | bytes 1572864 | tf_op jit(solution)/shard_map/all_to_all | solution.py:386
  514.0 40.3 %collective-permute-start.48 = (bf16[1024,512]{1,0:T(8,128)(2,1)}, bf16[1024,512]{1,0:T(8,128)(2,1)}, u32[]{:S(2)}, u32[]{:S(2)}) collective-permute-start(bf16[1024,512]{1,0:T(8,128)(2,1)} %convolution_convert_fusion.7), channel_id=1, source_target_pairs={{0,8},{8,0},{16,24},{24,16},{1,9},{9,1},{17,25},{25,17},{2,10},{10... | collective-permute-start | bytes 3145736 | tf_op jit(solution)/shard_map/ppermute | solution.py:33
  519.8 135.0 %collective-permute-start.54 = (bf16[4096,512]{1,0:T(8,128)(2,1)}, bf16[4096,512]{1,0:T(8,128)(2,1)}, u32[]{:S(2)}, u32[]{:S(2)}) collective-permute-start(bf16[4096,512]{1,0:T(8,128)(2,1)} %convolution_convert_fusion), channel_id=1, source_target_pairs={{0,8},{8,0},{16,24},{24,16},{1,9},{9,1},{17,25},{25,17},{2,10},{10... | collective-permute-start | bytes 12582920 | tf_op jit(solution)/shard_map/ppermute | solution.py:33
  542.0 26.8 %all-to-all-start.2 = ((bf16[8,3,128,128]{3,2,1,0:T(8,128)(2,1)}), bf16[8,3,128,128]{3,2,1,0:T(8,128)(2,1)}, u32[]{:S(2)}, u32[]{:S(2)}) async-start(bf16[8,3,128,128]{3,2,1,0:T(8,128)(2,1)} %bitcast.480), calls=%async_computation.2 | async-start | bytes 1572864 | tf_op jit(solution)/shard_map/all_to_all | solution.py:386
  554.2 109.1 %collective-permute-start.59 = (bf16[1024,2048]{1,0:T(8,128)(2,1)}, bf16[1024,2048]{1,0:T(8,128)(2,1)}, u32[]{:S(2)}, u32[]{:S(2)}) collective-permute-start(bf16[1024,2048]{1,0:T(8,128)(2,1)} %convolution_convert_fusion.3), channel_id=1, source_target_pairs={{0,8},{8,0},{16,24},{24,16},{1,9},{9,1},{17,25},{25,17},{2,10},{10... | collective-permute-start | bytes 12582920 | tf_op jit(solution)/shard_map/ppermute | solution.py:33
  564.8 85.1 %collective-permute-start.50 = (bf16[4,2,512,256]{3,2,1,0:T(8,128)(2,1)}, bf16[4,2,512,256]{3,2,1,0:T(8,128)(2,1)}, u32[]{:S(2)}, u32[]{:S(2)}) collective-permute-start(bf16[4,2,512,256]{3,2,1,0:T(8,128)(2,1)} %slice.634), channel_id=1, source_target_pairs={{0,16},{8,24},{16,0},{24,8},{1,17},{9,25},{17,1},{25,9},{2,18},{10... | collective-permute-start | bytes 6291464 | tf_op jit(solution)/shard_map/ppermute | solution.py:33
  636.8 59.4 %all-to-all-start.3 = ((bf16[8,3,128,384]{3,2,1,0:T(8,128)(2,1)}), bf16[8,3,128,384]{3,2,1,0:T(8,128)(2,1)}, u32[]{:S(2)}, u32[]{:S(2)}) async-start(bf16[8,3,128,384]{3,2,1,0:T(8,128)(2,1)} %get-tuple-element.33), calls=%async_computation.3 | async-start | bytes 4718592 | tf_op jit(solution)/shard_map/all_to_all | solution.py:386
  652.9 39.1 %collective-permute-start.51 = (bf16[4,1,512,256]{3,2,1,0:T(8,128)(2,1)S(1)}, bf16[4,1,512,256]{3,2,1,0:T(8,128)(2,1)S(1)}, u32[]{:S(2)}, u32[]{:S(2)}) collective-permute-start(bf16[4,1,512,256]{3,2,1,0:T(8,128)(2,1)S(1)} %constant_dynamic-slice_fusion.12), channel_id=1, source_target_pairs={{0,1},{1,0},{2,3},{3,2},{4,5},{5,4},{6,7},{7,6},{8,9},{9,8},{10,11... | collective-permute-start | bytes 3145736 | tf_op jit(solution)/shard_map/ppermute | solution.py:33
  662.4 118.8 %collective-permute-start.55 = (bf16[4,1,512,512]{3,2,0,1:T(8,128)(2,1)}, bf16[4,1,512,512]{3,2,0,1:T(8,128)(2,1)}, u32[]{:S(2)}, u32[]{:S(2)}) collective-permute-start(bf16[4,1,512,512]{3,2,0,1:T(8,128)(2,1)} %dynamic-slice_bitcast_fusion), channel_id=1, source_target_pairs={{0,1},{1,0},{2,3},{3,2},{4,5},{5,4},{6,7},{7,6},{8,9},{9,8},{10,11... | collective-permute-start | bytes 6291464 | tf_op jit(solution)/shard_map/ppermute | solution.py:33
  670.5 120.1 %collective-permute-start.60 = (bf16[4,2,128,1024]{3,2,1,0:T(8,128)(2,1)}, bf16[4,2,128,1024]{3,2,1,0:T(8,128)(2,1)}, u32[]{:S(2)}, u32[]{:S(2)}) collective-permute-start(bf16[4,2,128,1024]{3,2,1,0:T(8,128)(2,1)} %slice.641), channel_id=1, source_target_pairs={{0,16},{8,24},{16,0},{24,8},{1,17},{9,25},{17,1},{25,9},{2,18},{10... | collective-permute-start | bytes 6291464 | tf_op jit(solution)/shard_map/ppermute | solution.py:33
  693.7 68.2 %collective-permute-start.52 = (bf16[2,1,512,256]{2,3,1,0:T(8,128)(2,1)}, bf16[2,1,512,256]{2,3,1,0:T(8,128)(2,1)}, u32[]{:S(2)}, u32[]{:S(2)}) collective-permute-start(bf16[2,1,512,256]{2,3,1,0:T(8,128)(2,1)} %dynamic-slice_bitcast_fusion.5), channel_id=1, source_target_pairs={{0,4},{2,6},{4,0},{6,2},{1,5},{3,7},{5,1},{7,3},{8,12},{10,14},{12... | collective-permute-start | bytes 1572872 | tf_op jit(solution)/shard_map/ppermute | solution.py:33
  732.4 28.6 %collective-permute-start.69 = (f32[56,1024]{1,0:T(8,128)}, f32[56,1024]{1,0:T(8,128)S(1)}, u32[]{:S(2)}, u32[]{:S(2)}) collective-permute-start(f32[56,1024]{1,0:T(8,128)} %reshape.903), channel_id=1, source_target_pairs={{0,8},{8,0},{16,24},{24,16},{1,9},{9,1},{17,25},{25,17},{2,10},{10... | collective-permute-start | bytes 688136 | tf_op jit(solution)/shard_map/ppermute | solution.py:33
  761.0 64.6 %collective-permute-start.32 = (bf16[4096,512]{1,0:T(8,128)(2,1)}, bf16[4096,512]{1,0:T(8,128)(2,1)}, u32[]{:S(2)}, u32[]{:S(2)}) collective-permute-start(bf16[4096,512]{1,0:T(8,128)(2,1)} %convolution_convert_fusion.1), channel_id=1, source_target_pairs={{0,8},{8,0},{16,24},{24,16},{1,9},{9,1},{17,25},{25,17},{2,10},{10... | collective-permute-start | bytes 12582920 | tf_op jit(solution)/shard_map/ppermute | solution.py:33
  769.2 48.6 %collective-permute-start.42 = (bf16[3072,512]{1,0:T(8,128)(2,1)}, bf16[3072,512]{1,0:T(8,128)(2,1)}, u32[]{:S(2)}, u32[]{:S(2)}) collective-permute-start(bf16[3072,512]{1,0:T(8,128)(2,1)} %convolution_convert_fusion.2), channel_id=1, source_target_pairs={{0,8},{8,0},{16,24},{24,16},{1,9},{9,1},{17,25},{25,17},{2,10},{10... | collective-permute-start | bytes 9437192 | tf_op jit(solution)/shard_map/ppermute | solution.py:33
  779.7 53.8 %collective-permute-start.37 = (bf16[1024,2048]{1,0:T(8,128)(2,1)}, bf16[1024,2048]{1,0:T(8,128)(2,1)}, u32[]{:S(2)}, u32[]{:S(2)}) collective-permute-start(bf16[1024,2048]{1,0:T(8,128)(2,1)} %convolution_convert_fusion.4), channel_id=1, source_target_pairs={{0,8},{8,0},{16,24},{24,16},{1,9},{9,1},{17,25},{25,17},{2,10},{10... | collective-permute-start | bytes 12582920 | tf_op jit(solution)/shard_map/ppermute | solution.py:33
  803.4 38.9 %collective-permute-start.61 = (bf16[4,1,128,1024]{3,2,1,0:T(8,128)(2,1)}, bf16[4,1,128,1024]{3,2,1,0:T(8,128)(2,1)}, u32[]{:S(2)}, u32[]{:S(2)}) collective-permute-start(bf16[4,1,128,1024]{3,2,1,0:T(8,128)(2,1)} %constant_dynamic-slice_fusion.1), channel_id=1, source_target_pairs={{0,1},{1,0},{2,3},{3,2},{4,5},{5,4},{6,7},{7,6},{8,9},{9,8},{10,11... | collective-permute-start | bytes 3145736 | tf_op jit(solution)/shard_map/ppermute | solution.py:33
  817.7 52.6 %collective-permute-start.57 = (bf16[2,1,512,256]{2,3,1,0:T(8,128)(2,1)}, bf16[2,1,512,256]{2,3,1,0:T(8,128)(2,1)}, u32[]{:S(2)}, u32[]{:S(2)}) collective-permute-start(bf16[2,1,512,256]{2,3,1,0:T(8,128)(2,1)} %dynamic-slice_bitcast_fusion.4), channel_id=1, source_target_pairs={{0,4},{2,6},{4,0},{6,2},{1,5},{3,7},{5,1},{7,3},{8,12},{10,14},{12... | collective-permute-start | bytes 1572872 | tf_op jit(solution)/shard_map/ppermute | solution.py:33
  823.9 39.6 %collective-permute-start.43 = (bf16[4,1,384,512]{3,2,0,1:T(8,128)(2,1)}, bf16[4,1,384,512]{3,2,0,1:T(8,128)(2,1)}, u32[]{:S(2)}, u32[]{:S(2)}) collective-permute-start(bf16[4,1,384,512]{3,2,0,1:T(8,128)(2,1)} %dynamic-slice_bitcast_fusion.2), channel_id=1, source_target_pairs={{0,1},{1,0},{2,3},{3,2},{4,5},{5,4},{6,7},{7,6},{8,9},{9,8},{10,11... | collective-permute-start | bytes 4718600 | tf_op jit(solution)/shard_map/ppermute | solution.py:33
  833.2 77.6 %collective-permute-start.33 = (bf16[4,1,512,512]{3,2,0,1:T(8,128)(2,1)}, bf16[4,1,512,512]{3,2,0,1:T(8,128)(2,1)}, u32[]{:S(2)}, u32[]{:S(2)}) collective-permute-start(bf16[4,1,512,512]{3,2,0,1:T(8,128)(2,1)} %dynamic-slice_bitcast_fusion.1), channel_id=1, source_target_pairs={{0,1},{1,0},{2,3},{3,2},{4,5},{5,4},{6,7},{7,6},{8,9},{9,8},{10,11... | collective-permute-start | bytes 6291464 | tf_op jit(solution)/shard_map/ppermute | solution.py:33
  841.0 74.2 %collective-permute-start.38 = (bf16[4,2,128,1024]{3,2,1,0:T(8,128)(2,1)}, bf16[4,2,128,1024]{3,2,1,0:T(8,128)(2,1)}, u32[]{:S(2)}, u32[]{:S(2)}) collective-permute-start(bf16[4,2,128,1024]{3,2,1,0:T(8,128)(2,1)} %slice.627), channel_id=1, source_target_pairs={{0,16},{8,24},{16,0},{24,8},{1,17},{9,25},{17,1},{25,9},{2,18},{10... | collective-permute-start | bytes 6291464 | tf_op jit(solution)/shard_map/ppermute | solution.py:33
  845.7 26.8 %collective-permute-start.62 = (bf16[2,1,128,1024]{2,3,1,0:T(8,128)(2,1)}, bf16[2,1,128,1024]{2,3,1,0:T(8,128)(2,1)}, u32[]{:S(2)}, u32[]{:S(2)}) collective-permute-start(bf16[2,1,128,1024]{2,3,1,0:T(8,128)(2,1)} %dynamic-slice_bitcast_fusion.3), channel_id=1, source_target_pairs={{0,4},{2,6},{4,0},{6,2},{1,5},{3,7},{5,1},{7,3},{8,12},{10,14},{12... | collective-permute-start | bytes 1572872 | tf_op jit(solution)/shard_map/ppermute | solution.py:33
  866.9 37.4 %collective-permute-start.44 = (bf16[4,1,384,256]{3,2,0,1:T(8,128)(2,1)}, bf16[4,1,384,256]{3,2,0,1:T(8,128)(2,1)}, u32[]{:S(2)}, u32[]{:S(2)}) collective-permute-start(bf16[4,1,384,256]{3,2,0,1:T(8,128)(2,1)} %slice.629), channel_id=1, source_target_pairs={{0,16},{8,24},{16,0},{24,8},{1,17},{9,25},{17,1},{25,9},{2,18},{10... | collective-permute-start | bytes 2359304 | tf_op jit(solution)/shard_map/ppermute | solution.py:33
  872.2 48.0 %collective-permute-start.58 = (bf16[1,1,512,256]{2,3,1,0:T(8,128)(2,1)}, bf16[1,1,512,256]{2,3,1,0:T(8,128)(2,1)}, u32[]{:S(2)}, u32[]{:S(2)}) collective-permute-start(bf16[1,1,512,256]{2,3,1,0:T(8,128)(2,1)} %constant_dynamic-slice_fusion.6), channel_id=1, source_target_pairs={{0,2},{2,0},{4,6},{6,4},{1,3},{3,1},{5,7},{7,5},{8,10},{10,8},{12,... | collective-permute-start | bytes 786440 | tf_op jit(solution)/shard_map/ppermute | solution.py:33
  874.5 47.5 %collective-permute-start.63 = (bf16[1,1,128,1024]{2,3,1,0:T(8,128)(2,1)}, bf16[1,1,128,1024]{2,3,1,0:T(8,128)(2,1)}, u32[]{:S(2)}, u32[]{:S(2)}) collective-permute-start(bf16[1,1,128,1024]{2,3,1,0:T(8,128)(2,1)} %constant_dynamic-slice_fusion), channel_id=1, source_target_pairs={{0,2},{2,0},{4,6},{6,4},{1,3},{3,1},{5,7},{7,5},{8,10},{10,8},{12,... | collective-permute-start | bytes 786440 | tf_op jit(solution)/shard_map/ppermute | solution.py:33
  939.7 34.9 %collective-permute-start.35 = (bf16[2,1,512,256]{2,3,1,0:T(8,128)(2,1)}, bf16[2,1,512,256]{2,3,1,0:T(8,128)(2,1)}, u32[]{:S(2)}, u32[]{:S(2)}) collective-permute-start(bf16[2,1,512,256]{2,3,1,0:T(8,128)(2,1)} %dynamic-slice_bitcast_fusion.7), channel_id=1, source_target_pairs={{0,4},{2,6},{4,0},{6,2},{1,5},{3,7},{5,1},{7,3},{8,12},{10,14},{12... | collective-permute-start | bytes 1572872 | tf_op jit(solution)/shard_map/ppermute | solution.py:33
  943.5 41.3 %collective-permute-start.40 = (bf16[2,1,128,1024]{2,3,1,0:T(8,128)(2,1)S(1)}, bf16[2,1,128,1024]{2,3,1,0:T(8,128)(2,1)S(1)}, u32[]{:S(2)}, u32[]{:S(2)}) collective-permute-start(bf16[2,1,128,1024]{2,3,1,0:T(8,128)(2,1)S(1)} %dynamic-slice_bitcast_fusion.6), channel_id=1, source_target_pairs={{0,4},{2,6},{4,0},{6,2},{1,5},{3,7},{5,1},{7,3},{8,12},{10,14},{12... | collective-permute-start | bytes 1572872 | tf_op jit(solution)/shard_map/ppermute | solution.py:33
  (285 other events, 3352.3 us)

commit v3 on v2

--- a/solution.py
+++ b/solution.py
@@ -147,7 +147,7 @@
     return held, swapped(held, "clip", 0)
 
 
-def reduce_group(pairs, reverse):
+def reduce_group(pairs, reverse, begun=None):
     clip_count = lax.axis_size("clip")
     uppers = clip_count // 2
     sizes = {"coarse": lax.axis_size("coarse"), "fine": lax.axis_size("fine")}
@@ -172,6 +172,8 @@
             )
         )
     held = parts[0] if len(parts) == 1 else jnp.concatenate(parts, 2)
+    if begun is not None:
+        begun.append(held)
     coarse = [("coarse", b) for b in range(log2(sizes["coarse"]))][::-1]
     fine = [("fine", b) for b in range(log2(sizes["fine"]))][::-1]
     upper = [("clip", b) for b in range(1, log2(clip_count))][::-1]
@@ -193,7 +195,7 @@
 
 
 def summed_everywhere(values):
-    for axis in ("clip", "fine", "coarse"):
+    for axis in ("coarse", "clip", "fine"):
         for bit in range(log2(lax.axis_size(axis))):
             values = values + swapped(values, axis, bit)
     return values
@@ -672,7 +674,8 @@
     )
     mixed_grad = product(att_low, output_full).astype(bf16)
     attention_g, table_g = attention.backward(mixed_grad)
-    inputs_g = reduce_group([(att_normed, attention_g)], True)
+    begun = []
+    inputs_g = reduce_group([(att_normed, attention_g)], True, begun)
     att_in_g, att_scale, att_shift = norm_back(
         after_first, norm_scales[1], norm_shifts[1], product(attention_g, inputs_full)
     )
@@ -694,23 +697,24 @@
         down_first,
         first_saved,
     )
-    first_down_g = reduce_group([first_down_pair], False)
-    first_up_g = reduce_group([first_up_pair], True)
+    first_down_g = reduce_group([first_down_pair], False, begun)
+    first_up_g = reduce_group([first_up_pair], True, begun)
     in_grad = (grad_first + first_in).astype(bf16).reshape(clips, frames, D)
 
     attention_sums = column_sum(attention_g).reshape(peers, 3, share)
-    early = [
-        jnp.stack([att_scale, conv_scale, depth_scale, second_scale, final_scale]),
-        jnp.stack([att_shift, conv_shift, depth_shift, second_shift, final_shift]),
-        second_hidden[None],
-        jnp.stack([attention_sums[:, 0].reshape(D), column_sum(att_low), second_width]),
+    small = [
+        jnp.stack([first_scale, att_scale, conv_scale, depth_scale, second_scale, final_scale]),
+        jnp.stack([first_shift, att_shift, conv_shift, depth_shift, second_shift, final_shift]),
+        jnp.stack([first_hidden, second_hidden]),
+        jnp.stack(
+            [first_width, attention_sums[:, 0].reshape(D), column_sum(att_low), second_width]
+        ),
         attention_sums[:, 2].reshape(D),
         table_g,
         kernel_g,
     ]
-    late = [first_scale[None], first_shift[None], first_hidden[None], first_width[None]]
-    early = unpacked(summed_everywhere(packed(early)), early)
-    late = unpacked(summed_everywhere(packed(late)), late)
+    values, unused = lax.optimization_barrier((packed(small), begun))
+    small = unpacked(summed_everywhere(values), small)
 
     inner_n = 2 * D // peers
     outer_n = D // peers
@@ -727,13 +731,7 @@
         middle_g[inner_n : inner_n + outer_n].T,
         second_up_g.T,
         second_down_g.T,
-        jnp.concatenate([late[0], early[0]], 0),
-        jnp.concatenate([late[1], early[1]], 0),
-        jnp.concatenate([late[2], early[2]], 0),
-        jnp.concatenate([late[3], early[3]], 0),
-        early[4],
-        early[5],
-        early[6],
+        *small,
     )
 
 

time: 1010 us -> 989 us (0.979)
  waiting for transfers between devices: 361 us -> 346 us
    ppermute x72 -> x67, waiting for transfers between devices: 353 us -> 338 us  [swapped(): return lax.ppermute(shard, axis, [(i, i ^ 1 << bit) for i in range(peers)])]
    ppermute x72 -> x67, starting transfers between devices: 71.9 us -> 69 us  [swapped(): return lax.ppermute(shard, axis, [(i, i ^ 1 << bit) for i in range(peers)])]
    unnamed x548 -> x536, local copies, waits for them, and re-layouts: 49.7 us -> 47.8 us
  transfers between devices with their start and end apart: 78 -> 73, of which waited for: 38 -> 33; matrix products, arithmetic and copies ran while one was open for 27% -> 28% of each run, Pallas kernels for 14% -> 15%
where the time goes in v3:
time: 989 us; the launch traced here: 981 us
  waiting for transfers between devices  346 us (35%)
  Pallas kernels  144 us (15%)
  matrix products  144 us (15%)
  local copies, waits for them, and re-layouts  126 us (13%)
  other arithmetic  120 us (12%)
  starting transfers between devices  96.2 us (10%)
    ppermute x67, waiting for transfers between devices, swapped(): return lax.ppermute(shard, axis, [(i, i ^ 1 << bit) for i in range(peers)])  338 us
    ppermute x67, starting transfers between devices, swapped(): return lax.ppermute(shard, axis, [(i, i ^ 1 << bit) for i in range(peers)])  69 us
    pallas_call x1, Pallas kernels, attend_back(): pl.pallas_call(attend_back_kernel, out_shape=[jax.ShapeDtypeStruct(x.shap...  67.9 us
    dot_general x16, matrix products, weight_grad(): lax.dot_general(left, right, (((0,), (0,)), ((), ())), preferred_element_...  60.9 us
    unnamed x536, local copies, waits for them, and re-layouts  47.8 us
    pallas_call x6, Pallas kernels, place_whole(): pl.pallas_call(functools.partial(place_whole_kernel, splits, reverse, acr...  46.3 us
    dot_general x8, matrix products, product_t(): lax.dot_general(left, right, (((1,), (1,)), ((), ())), preferred_element_...  41.6 us
    dot_general x8, matrix products, product(): return jnp.dot(left, right, preferred_element_type=f32)  41.2 us
  transfers between devices with their start and end apart: 73, of which 33 were waited for; matrix products, arithmetic and copies ran while one was open for 28% of the time, Pallas kernels for 15%

profile of v3, /device:TPU:0, one launch (start us, length us, event | category | flops | bytes accessed | tf_op | source)
XLA Modules:
  0.0 981.0 jit_solution(11432263071612588453)
XLA Ops:
  6.2 5.9 collective-permute-done
  15.2 6.6 collective-permute-done.5
  22.0 28.6 %collective-permute-done.1 = bf16[2,512,256]{2,1,0:T(8,128)(2,1)S(1)} collective-permute-done((bf16[2,512,256]{2,1,0:T(8,128)(2,1)S(1)}, bf16[2,512,256]{2,1,0:T(8,128)(2,1)S(1)}, u32[]{:S(2)}, u32[]{:S(2)}) %collective-permute-start.1) | collective-permute-done | bytes 524320 | tf_op jit(solution)/shard_map/ppermute | solution.py:33
  52.6 6.6 collective-permute-done.6
  60.6 9.9 %collective-permute-done.2 = bf16[4,512,256]{2,1,0:T(8,128)(2,1)S(1)} collective-permute-done((bf16[4,512,256]{2,1,0:T(8,128)(2,1)S(1)}, bf16[4,512,256]{2,1,0:T(8,128)(2,1)S(1)}, u32[]{:S(2)}, u32[]{:S(2)}) %collective-permute-start.2) | collective-permute-done | bytes 1048608 | tf_op jit(solution)/shard_map/ppermute | solution.py:33
  73.2 12.2 %collective-permute-done.7 = bf16[4,128,1024]{2,1,0:T(8,128)(2,1)S(1)} collective-permute-done((bf16[4,128,1024]{2,1,0:T(8,128)(2,1)S(1)}, bf16[4,128,1024]{2,1,0:T(8,128)(2,1)S(1)}, u32[]{:S(2)}, u32[]{:S(2)}) %collective-permute-start.7) | collective-permute-done | bytes 1048608 | tf_op jit(solution)/shard_map/ppermute | solution.py:33
  93.3 7.4 collective-permute-done.10
  108.2 9.3 collective-permute-done.11
  129.9 6.1 collective-permute-done.8
  140.6 9.6 collective-permute-done.12
  164.6 24.2 %collective-permute-done.27 = bf16[2,128,1024]{2,1,0:T(8,128)(2,1)S(1)} collective-permute-done((bf16[2,128,1024]{2,1,0:T(8,128)(2,1)}, bf16[2,128,1024]{2,1,0:T(8,128)(2,1)S(1)}, u32[]{:S(2)}, u32[]{:S(2)}) %collective-permute-start.27) | collective-permute-done | bytes 524320 | tf_op jit(solution)/shard_map/ppermute | solution.py:33
  190.1 6.8 collective-permute-done.22
  207.3 12.6 %collective-permute-done.28 = bf16[4,128,1024]{2,1,0:T(8,128)(2,1)S(1)} collective-permute-done((bf16[4,128,1024]{2,1,0:T(8,128)(2,1)S(1)}, bf16[4,128,1024]{2,1,0:T(8,128)(2,1)S(1)}, u32[]{:S(2)}, u32[]{:S(2)}) %collective-permute-start.28) | collective-permute-done | bytes 1048608 | tf_op jit(solution)/shard_map/ppermute | solution.py:33
  226.1 8.2 place.6
  234.3 7.8 place.7
  242.1 11.4 %multiply_convert_fusion.1 = (bf16[384,4096]{1,0:T(8,128)(2,1)S(1)}, f32[384,4096]{1,0:T(8,128)}) fusion(f32[4096]{0:T(1024)S(1)} %bitcast.635, bf16[384,1024]{1,0:T(8,128)(2,1)S(1)} %copy-done.60, bf16[4096,1024]{1,0:T(8,128)(2,1)} %place.6), kind=kOutput, calls=%fused_computation.17 | convolution fusion | flops 3230662656 | bytes 18628608 | tf_op jit(solution)/shard_map/dot_general | solution.py:77
  259.6 8.0 place.8
  268.3 7.2 add_convert_fusion.5
  277.2 5.5 all-to-all-start
  289.5 12.1 %collective-permute-done.17 = bf16[4,384,256]{2,1,0:T(8,128)(2,1)S(1)} collective-permute-done((bf16[4,384,256]{2,1,0:T(8,128)(2,1)S(1)}, bf16[4,384,256]{2,1,0:T(8,128)(2,1)S(1)}, u32[]{:S(2)}, u32[]{:S(2)}) %collective-permute-start.17) | collective-permute-done | bytes 786464 | tf_op jit(solution)/shard_map/ppermute | solution.py:33
  318.4 29.1 %collective-permute-done.18 = bf16[8,384,256]{2,1,0:T(8,128)(2,1)S(1)} collective-permute-done((bf16[8,384,256]{2,1,0:T(8,128)(2,1)S(1)}, bf16[8,384,256]{2,1,0:T(8,128)(2,1)S(1)}, u32[]{:S(2)}, u32[]{:S(2)}) %collective-permute-start.18) | collective-permute-done | bytes 1572896 | tf_op jit(solution)/shard_map/ppermute | solution.py:33
  349.6 29.6 %attend.1 = (bf16[8,3,128,128]{3,2,1,0:T(8,128)(2,1)}, bf16[3,2,1024,1024]{3,2,1,0:T(8,128)(2,1)}) custom-call(s32[3]{0:T(128)} %lengths.1, bf16[8,3,128,384]{3,2,1,0:T(8,128)(2,1)} %all-to-all-done.x_ref, bf16[128,64]{1,0:T(8,128)(2,1)} %pad.200.table_ref), custom_call_target="tpu_custom_call" | custom-call | flops 6442450944 | bytes 12582912 | tf_op jit(solution)/shard_map/attend/pallas_call | solution.py:325
  379.1 5.7 all-to-all-start.1
  385.4 6.7 place.9
  392.1 7.9 place.10
  400.1 7.7 place.11
  423.7 7.4 fusion.148
  435.9 6.5 multiply_convert_fusion
  442.5 7.0 fusion.159
  454.3 10.7 %convert_reduce_fusion = (f32[4096]{0:T(1024)}, bf16[384,4096]{1,0:T(8,128)(2,1)S(1)}) fusion(f32[384,4096]{1,0:T(8,128)} %get-tuple-element.284, f32[4096]{0:T(1024)S(1)} %bitcast.639, bf16[384,1024]{1,0:T(8,128)(2,1)S(1)} %get-tuple-element.130, bf16[1024,4096]{1,0:T(8,128)(2,1)} %place.11), kind=kOutput, calls=%fused_computation.12 | convolution fusion | flops 3241668608 | bytes 18644992 | tf_op jit(solution)/shard_map/dot_general | solution.py:69
  485.1 10.0 %broadcast_multiply_fusion = (f32[3,128,1024]{2,1,0:T(8,128)}, f32[3,128,1024]{2,1,0:T(8,128)}, f32[3,128,1024]{2,1,0:T(8,128)}, f32[3,128,1024]{2,1,0:T(8,128)}...) fusion(f32[3,128,1024]{2,1,0:T(8,128)S(1)} %bitcast.433, ...), kind=kLoop, calls=%fused_computation.204 | loop fusion | flops 7077888 | bytes 29958144 | tf_op jit(solution)/shard_map/transpose(jvp())/mul | solution.py:65
  495.1 16.1 %pad_add_fusion = f32[3,158,1024]{2,1,0:T(8,128)S(1)} fusion(f32[3,128,1024]{2,1,0:T(8,128)S(1)} %get-tuple-element.158, f32[3,128,1024]{2,1,0:T(8,128)S(1)} %get-tuple-element.159, f32[3,128,1024]{2,1,0:T(8,128)S(1)} %get-tuple-element.160, f32[3,128,1024]{2,1,0:T(8,128)} %get-tuple-element.161, f32[3,128,1024]{2,1,0:T(8,128)} %get-tuple-element.162, ...), kind=kLoop, calls=%fused_computation.62 | loop fusion | flops 14561280 | bytes 50700288 | tf_op jit(solution)/shard_map/transpose(jvp())/add_any | solution.py:65
  541.8 6.1 all-to-all-start.2
  547.9 6.3 convolution_convert_fusion.3
  568.8 67.9 %attend_back.1 = (bf16[8,3,128,384]{3,2,1,0:T(8,128)(2,1)}, f32[3,128,64]{2,1,0:T(8,128)}) custom-call(bf16[8,3,128,384]{3,2,1,0:T(8,128)(2,1)} %all-to-all-done.x_ref, bf16[8,3,128,128]{3,2,1,0:T(8,128)(2,1)} %all-to-all-done.2.grad_ref, bf16[3,2,1024,1024]{3,2,1,0:T(8,128)(2,1)} %get-tuple-element.33.probs_ref, bf16[128,64]{1,0:T(8,128)(2,1)} %pad.200.table_ref), custom_call_target="tpu_custom_call" | custom-call | flops 12884901888 | bytes 12582912 | tf_op jit(solution)/shard_map/attend_back/pallas_call | solution.py:356
  671.7 20.1 %collective-permute-done.51 = bf16[4,1,512,256]{3,2,1,0:T(8,128)(2,1)S(1)} collective-permute-done((bf16[4,1,512,256]{3,2,1,0:T(8,128)(2,1)S(1)}, bf16[4,1,512,256]{3,2,1,0:T(8,128)(2,1)S(1)}, u32[]{:S(2)}, u32[]{:S(2)}) %collective-permute-start.51) | collective-permute-done | bytes 1048608 | tf_op jit(solution)/shard_map/ppermute | solution.py:33
  700.6 5.9 multiply_reduce_fusion.34
  709.9 10.6 %convert_reduce_fusion.1 = (f32[4096]{0:T(1024)S(1)}, bf16[384,4096]{1,0:T(8,128)(2,1)S(1)}) fusion(f32[384,4096]{1,0:T(8,128)} %get-tuple-element.276, f32[4096]{0:T(1024)S(1)} %bitcast.636, bf16[384,1024]{1,0:T(8,128)(2,1)S(1)} %get-tuple-element.125, bf16[1024,4096]{1,0:T(8,128)(2,1)} %place.7), kind=kOutput, calls=%fused_computation.13 | convolution fusion | flops 3241668608 | bytes 18644992 | tf_op jit(solution)/shard_map/dot_general | solution.py:69
  739.7 4.8 concatenate.201
  751.2 5.7 collective-permute-start.53
  771.3 16.6 %collective-permute-done.56 = bf16[4,1,512,256]{3,2,0,1:T(8,128)(2,1)S(1)} collective-permute-done((bf16[4,1,512,256]{3,2,0,1:T(8,128)(2,1)S(1)}, bf16[4,1,512,256]{3,2,0,1:T(8,128)(2,1)S(1)}, u32[]{:S(2)}, u32[]{:S(2)}) %collective-permute-start.56) | collective-permute-done | bytes 1048608 | tf_op jit(solution)/shard_map/ppermute | solution.py:33
  807.4 6.8 add_convert_fusion.2
  825.7 9.7 collective-permute-done.43
  841.6 16.0 %collective-permute-done.65 = f32[64,1024]{1,0:T(8,128)S(1)} collective-permute-done((f32[64,1024]{1,0:T(8,128)S(1)}, f32[64,1024]{1,0:T(8,128)S(1)}, u32[]{:S(2)}, u32[]{:S(2)}) %collective-permute-start.65) | collective-permute-done | bytes 262176 | tf_op jit(solution)/shard_map/ppermute | solution.py:33
  860.8 5.8 collective-permute-done.58
  867.7 21.4 %collective-permute-done.67 = f32[64,1024]{1,0:T(8,128)S(1)} collective-permute-done((f32[64,1024]{1,0:T(8,128)S(1)}, f32[64,1024]{1,0:T(8,128)S(1)}, u32[]{:S(2)}, u32[]{:S(2)}) %collective-permute-start.67) | collective-permute-done | bytes 262176 | tf_op jit(solution)/shard_map/ppermute | solution.py:33
  931.0 27.5 %collective-permute-done.35 = bf16[2,1,512,256]{2,3,1,0:T(8,128)(2,1)} collective-permute-done((bf16[2,1,512,256]{2,3,1,0:T(8,128)(2,1)}, bf16[2,1,512,256]{2,3,1,0:T(8,128)(2,1)}, u32[]{:S(2)}, u32[]{:S(2)}) %collective-permute-start.35) | collective-permute-done | bytes 524320 | tf_op jit(solution)/shard_map/ppermute | solution.py:33
  959.8 8.8 collective-permute-done.40
  (880 shorter events, 385.9 us)
Async XLA Ops:
  12.1 38.5 %collective-permute-start.1 = (bf16[2,512,256]{2,1,0:T(8,128)(2,1)S(1)}, bf16[2,512,256]{2,1,0:T(8,128)(2,1)S(1)}, u32[]{:S(2)}, u32[]{:S(2)}) collective-permute-start(bf16[2,512,256]{2,1,0:T(8,128)(2,1)S(1)} %pad_maximum_fusion.14), channel_id=1, source_target_pairs={{0,4},{2,6},{4,0},{6,2},{1,5},{3,7},{5,1},{7,3},{8,12},{10,14},{12... | collective-permute-start | bytes 1572872 | tf_op jit(solution)/shard_map/ppermute | solution.py:33
  21.9 37.2 %collective-permute-start.6 = (bf16[2,128,1024]{2,1,0:T(8,128)(2,1)S(1)}, bf16[2,128,1024]{2,1,0:T(8,128)(2,1)S(1)}, u32[]{:S(2)}, u32[]{:S(2)}) collective-permute-start(bf16[2,128,1024]{2,1,0:T(8,128)(2,1)S(1)} %pad_maximum_fusion.15), channel_id=1, source_target_pairs={{0,4},{2,6},{4,0},{6,2},{1,5},{3,7},{5,1},{7,3},{8,12},{10,14},{12... | collective-permute-start | bytes 1572872 | tf_op jit(solution)/shard_map/ppermute | solution.py:33
  59.2 26.2 %collective-permute-start.7 = (bf16[4,128,1024]{2,1,0:T(8,128)(2,1)S(1)}, bf16[4,128,1024]{2,1,0:T(8,128)(2,1)S(1)}, u32[]{:S(2)}, u32[]{:S(2)}) collective-permute-start(bf16[4,128,1024]{2,1,0:T(8,128)(2,1)S(1)} %pad_maximum_fusion.9), channel_id=1, source_target_pairs={{0,16},{8,24},{16,0},{24,8},{1,17},{9,25},{17,1},{25,9},{2,18},{10... | collective-permute-start | bytes 3145736 | tf_op jit(solution)/shard_map/ppermute | solution.py:33
  72.2 54.6 %collective-permute-start.3 = (bf16[8,512,256]{2,1,0:T(8,128)(2,1)}, bf16[8,512,256]{2,1,0:T(8,128)(2,1)}, u32[]{:S(2)}, u32[]{:S(2)}) collective-permute-start(bf16[8,512,256]{2,1,0:T(8,128)(2,1)} %pad_maximum_fusion.1), channel_id=1, source_target_pairs={{0,16},{8,24},{16,0},{24,8},{1,17},{9,25},{17,1},{25,9},{2,18},{10... | collective-permute-start | bytes 6291464 | tf_op jit(solution)/shard_map/ppermute | solution.py:33
  87.1 48.9 %collective-permute-start.8 = (bf16[8,128,1024]{2,1,0:T(8,128)(2,1)}, bf16[8,128,1024]{2,1,0:T(8,128)(2,1)}, u32[]{:S(2)}, u32[]{:S(2)}) collective-permute-start(bf16[8,128,1024]{2,1,0:T(8,128)(2,1)} %pad_maximum_fusion.2), channel_id=1, source_target_pairs={{0,1},{1,0},{2,3},{3,2},{4,5},{5,4},{6,7},{7,6},{8,9},{9,8},{10,11... | collective-permute-start | bytes 6291464 | tf_op jit(solution)/shard_map/ppermute | solution.py:33
  90.0 65.6 %collective-permute-start.26 = (bf16[1,128,1024]{2,1,0:T(8,128)(2,1)S(1)}, bf16[1,128,1024]{2,1,0:T(8,128)(2,1)S(1)}, u32[]{:S(2)}, u32[]{:S(2)}) collective-permute-start(bf16[1,128,1024]{2,1,0:T(8,128)(2,1)S(1)} %bitcast.443), channel_id=1, source_target_pairs={{0,2},{2,0},{4,6},{6,4},{1,3},{3,1},{5,7},{7,5},{8,10},{10,8},{12,... | collective-permute-start | bytes 786440 | tf_op jit(solution)/shard_map/ppermute | solution.py:33
  92.5 64.0 %collective-permute-start.21 = (bf16[1,512,256]{2,1,0:T(8,128)(2,1)S(1)}, bf16[1,512,256]{2,1,0:T(8,128)(2,1)S(1)}, u32[]{:S(2)}, u32[]{:S(2)}) collective-permute-start(bf16[1,512,256]{2,1,0:T(8,128)(2,1)S(1)} %bitcast.447), channel_id=1, source_target_pairs={{0,2},{2,0},{4,6},{6,4},{1,3},{3,1},{5,7},{7,5},{8,10},{10,8},{12,... | collective-permute-start | bytes 786440 | tf_op jit(solution)/shard_map/ppermute | solution.py:33
  117.6 32.6 %collective-permute-start.12 = (bf16[4,512,256]{2,1,0:T(8,128)(2,1)S(1)}, bf16[4,512,256]{2,1,0:T(8,128)(2,1)S(1)}, u32[]{:S(2)}, u32[]{:S(2)}) collective-permute-start(bf16[4,512,256]{2,1,0:T(8,128)(2,1)S(1)} %pad_maximum_fusion.10), channel_id=1, source_target_pairs={{0,1},{1,0},{2,3},{3,2},{4,5},{5,4},{6,7},{7,6},{8,9},{9,8},{10,11... | collective-permute-start | bytes 3145736 | tf_op jit(solution)/shard_map/ppermute | solution.py:33
  129.9 95.8 %collective-permute-start.4 = (bf16[16,512,256]{2,1,0:T(8,128)(2,1)}, bf16[16,512,256]{2,1,0:T(8,128)(2,1)}, u32[]{:S(2)}, u32[]{:S(2)}) collective-permute-start(bf16[16,512,256]{2,1,0:T(8,128)(2,1)} %constant_dynamic-update-slice_fusion), channel_id=1, source_target_pairs={{0,8},{8,0},{16,24},{24,16},{1,9},{9,1},{17,25},{25,17},{2,10},{10... | collective-permute-start | bytes 12582920 | tf_op jit(solution)/shard_map/ppermute | solution.py:33
  139.1 95.2 %collective-permute-start.9 = (bf16[16,128,1024]{2,1,0:T(8,128)(2,1)}, bf16[16,128,1024]{2,1,0:T(8,128)(2,1)}, u32[]{:S(2)}, u32[]{:S(2)}) collective-permute-start(bf16[16,128,1024]{2,1,0:T(8,128)(2,1)} %constant_dynamic-update-slice_fusion.5), channel_id=1, source_target_pairs={{0,8},{8,0},{16,24},{24,16},{1,9},{9,1},{17,25},{25,17},{2,10},{10... | collective-permute-start | bytes 12582920 | tf_op jit(solution)/shard_map/ppermute | solution.py:33
  151.9 48.7 %collective-permute-start.13 = (bf16[8,512,256]{2,1,0:T(8,128)(2,1)}, bf16[8,512,256]{2,1,0:T(8,128)(2,1)}, u32[]{:S(2)}, u32[]{:S(2)}) collective-permute-start(bf16[8,512,256]{2,1,0:T(8,128)(2,1)} %pad_maximum_fusion.3), channel_id=1, source_target_pairs={{0,16},{8,24},{16,0},{24,8},{1,17},{9,25},{17,1},{25,9},{2,18},{10... | collective-permute-start | bytes 6291464 | tf_op jit(solution)/shard_map/ppermute | solution.py:33
  156.5 32.3 %collective-permute-start.27 = (bf16[2,128,1024]{2,1,0:T(8,128)(2,1)}, bf16[2,128,1024]{2,1,0:T(8,128)(2,1)S(1)}, u32[]{:S(2)}, u32[]{:S(2)}) collective-permute-start(bf16[2,128,1024]{2,1,0:T(8,128)(2,1)} %pad_maximum_fusion.18), channel_id=1, source_target_pairs={{0,4},{2,6},{4,0},{6,2},{1,5},{3,7},{5,1},{7,3},{8,12},{10,14},{12... | collective-permute-start | bytes 1572872 | tf_op jit(solution)/shard_map/ppermute | solution.py:33
  158.0 38.8 %collective-permute-start.22 = (bf16[2,512,256]{2,1,0:T(8,128)(2,1)}, bf16[2,512,256]{2,1,0:T(8,128)(2,1)S(1)}, u32[]{:S(2)}, u32[]{:S(2)}) collective-permute-start(bf16[2,512,256]{2,1,0:T(8,128)(2,1)} %pad_maximum_fusion.17), channel_id=1, source_target_pairs={{0,4},{2,6},{4,0},{6,2},{1,5},{3,7},{5,1},{7,3},{8,12},{10,14},{12... | collective-permute-start | bytes 1572872 | tf_op jit(solution)/shard_map/ppermute | solution.py:33
  204.0 53.5 %collective-permute-start.14 = (bf16[16,512,256]{2,1,0:T(8,128)(2,1)}, bf16[16,512,256]{2,1,0:T(8,128)(2,1)S(1)}, u32[]{:S(2)}, u32[]{:S(2)}) collective-permute-start(bf16[16,512,256]{2,1,0:T(8,128)(2,1)} %constant_dynamic-update-slice_fusion.10), channel_id=1, source_target_pairs={{0,8},{8,0},{16,24},{24,16},{1,9},{9,1},{17,25},{25,17},{2,10},{10... | collective-permute-start | bytes 12582920 | tf_op jit(solution)/shard_map/ppermute | solution.py:33
  219.9 62.9 %collective-permute-start.16 = (bf16[2,384,256]{2,1,0:T(8,128)(2,1)}, bf16[2,384,256]{2,1,0:T(8,128)(2,1)}, u32[]{:S(2)}, u32[]{:S(2)}) collective-permute-start(bf16[2,384,256]{2,1,0:T(8,128)(2,1)} %pad_maximum_fusion.19), channel_id=1, source_target_pairs={{0,4},{2,6},{4,0},{6,2},{1,5},{3,7},{5,1},{7,3},{8,12},{10,14},{12... | collective-permute-start | bytes 1179656 | tf_op jit(solution)/shard_map/ppermute | solution.py:33
  223.8 86.9 %collective-permute-start.29 = (bf16[8,128,1024]{2,1,0:T(8,128)(2,1)}, bf16[8,128,1024]{2,1,0:T(8,128)(2,1)}, u32[]{:S(2)}, u32[]{:S(2)}) collective-permute-start(bf16[8,128,1024]{2,1,0:T(8,128)(2,1)} %pad_maximum_fusion.5), channel_id=1, source_target_pairs={{0,1},{1,0},{2,3},{3,2},{4,5},{5,4},{6,7},{7,6},{8,9},{9,8},{10,11... | collective-permute-start | bytes 6291464 | tf_op jit(solution)/shard_map/ppermute | solution.py:33
  225.7 81.9 %collective-permute-start.24 = (bf16[8,512,256]{2,1,0:T(8,128)(2,1)}, bf16[8,512,256]{2,1,0:T(8,128)(2,1)}, u32[]{:S(2)}, u32[]{:S(2)}) collective-permute-start(bf16[8,512,256]{2,1,0:T(8,128)(2,1)} %pad_maximum_fusion.4), channel_id=1, source_target_pairs={{0,16},{8,24},{16,0},{24,8},{1,17},{9,25},{17,1},{25,9},{2,18},{10... | collective-permute-start | bytes 6291464 | tf_op jit(solution)/shard_map/ppermute | solution.py:33
  277.2 72.3 %all-to-all-start = ((bf16[8,3,128,384]{3,2,1,0:T(8,128)(2,1)}), bf16[8,3,128,384]{3,2,1,0:T(8,128)(2,1)}, u32[]{:S(2)}, u32[]{:S(2)}) async-start(bf16[8,3,128,384]{3,2,1,0:T(8,128)(2,1)} %bitcast.438), calls=%async_computation | async-start | bytes 4718592 | tf_op jit(solution)/shard_map/all_to_all | solution.py:388
  302.8 44.7 %collective-permute-start.18 = (bf16[8,384,256]{2,1,0:T(8,128)(2,1)S(1)}, bf16[8,384,256]{2,1,0:T(8,128)(2,1)S(1)}, u32[]{:S(2)}, u32[]{:S(2)}) collective-permute-start(bf16[8,384,256]{2,1,0:T(8,128)(2,1)S(1)} %pad_maximum_fusion.6), channel_id=1, source_target_pairs={{0,1},{1,0},{2,3},{3,2},{4,5},{5,4},{6,7},{7,6},{8,9},{9,8},{10,11... | collective-permute-start | bytes 4718600 | tf_op jit(solution)/shard_map/ppermute | solution.py:33
  310.6 81.5 %collective-permute-start.25 = (bf16[16,512,256]{2,1,0:T(8,128)(2,1)}, bf16[16,512,256]{2,1,0:T(8,128)(2,1)}, u32[]{:S(2)}, u32[]{:S(2)}) collective-permute-start(bf16[16,512,256]{2,1,0:T(8,128)(2,1)} %constant_dynamic-update-slice_fusion.20), channel_id=1, source_target_pairs={{0,8},{8,0},{16,24},{24,16},{1,9},{9,1},{17,25},{25,17},{2,10},{10... | collective-permute-start | bytes 12582920 | tf_op jit(solution)/shard_map/ppermute | solution.py:33
  313.8 86.2 %collective-permute-start.30 = (bf16[16,128,1024]{2,1,0:T(8,128)(2,1)}, bf16[16,128,1024]{2,1,0:T(8,128)(2,1)}, u32[]{:S(2)}, u32[]{:S(2)}) collective-permute-start(bf16[16,128,1024]{2,1,0:T(8,128)(2,1)} %constant_dynamic-update-slice_fusion.25), channel_id=1, source_target_pairs={{0,8},{8,0},{16,24},{24,16},{1,9},{9,1},{17,25},{25,17},{2,10},{10... | collective-permute-start | bytes 12582920 | tf_op jit(solution)/shard_map/ppermute | solution.py:33
  348.8 36.6 %collective-permute-start.19 = (bf16[16,384,256]{2,1,0:T(8,128)(2,1)}, bf16[16,384,256]{2,1,0:T(8,128)(2,1)}, u32[]{:S(2)}, u32[]{:S(2)}) collective-permute-start(bf16[16,384,256]{2,1,0:T(8,128)(2,1)} %constant_dynamic-update-slice_fusion.15), channel_id=1, source_target_pairs={{0,8},{8,0},{16,24},{24,16},{1,9},{9,1},{17,25},{25,17},{2,10},{10... | collective-permute-start | bytes 9437192 | tf_op jit(solution)/shard_map/ppermute | solution.py:33
  379.1 28.6 %all-to-all-start.1 = ((bf16[8,3,128,128]{3,2,1,0:T(8,128)(2,1)}), bf16[8,3,128,128]{3,2,1,0:T(8,128)(2,1)S(1)}, u32[]{:S(2)}, u32[]{:S(2)}) async-start(bf16[8,3,128,128]{3,2,1,0:T(8,128)(2,1)} %get-tuple-element.29), calls=%async_computation.1 | async-start | bytes 1572864 | tf_op jit(solution)/shard_map/all_to_all | solution.py:388
  513.8 40.6 %collective-permute-start.48 = (bf16[1024,512]{1,0:T(8,128)(2,1)}, bf16[1024,512]{1,0:T(8,128)(2,1)}, u32[]{:S(2)}, u32[]{:S(2)}) collective-permute-start(bf16[1024,512]{1,0:T(8,128)(2,1)} %convolution_convert_fusion.7), channel_id=1, source_target_pairs={{0,8},{8,0},{16,24},{24,16},{1,9},{9,1},{17,25},{25,17},{2,10},{10... | collective-permute-start | bytes 3145736 | tf_op jit(solution)/shard_map/ppermute | solution.py:33
  519.6 135.1 %collective-permute-start.54 = (bf16[4096,512]{1,0:T(8,128)(2,1)}, bf16[4096,512]{1,0:T(8,128)(2,1)}, u32[]{:S(2)}, u32[]{:S(2)}) collective-permute-start(bf16[4096,512]{1,0:T(8,128)(2,1)} %convolution_convert_fusion), channel_id=1, source_target_pairs={{0,8},{8,0},{16,24},{24,16},{1,9},{9,1},{17,25},{25,17},{2,10},{10... | collective-permute-start | bytes 12582920 | tf_op jit(solution)/shard_map/ppermute | solution.py:33
  533.5 25.3 %collective-permute-start.47 = (bf16[2048,512]{1,0:T(8,128)(2,1)}, bf16[2048,512]{1,0:T(8,128)(2,1)}, u32[]{:S(2)}, u32[]{:S(2)}) collective-permute-start(bf16[2048,512]{1,0:T(8,128)(2,1)} %convolution_convert_fusion.5), channel_id=1, source_target_pairs={{0,8},{8,0},{16,24},{24,16},{1,9},{9,1},{17,25},{25,17},{2,10},{10... | collective-permute-start | bytes 6291464 | tf_op jit(solution)/shard_map/ppermute | solution.py:33
  541.8 27.0 %all-to-all-start.2 = ((bf16[8,3,128,128]{3,2,1,0:T(8,128)(2,1)}), bf16[8,3,128,128]{3,2,1,0:T(8,128)(2,1)}, u32[]{:S(2)}, u32[]{:S(2)}) async-start(bf16[8,3,128,128]{3,2,1,0:T(8,128)(2,1)} %bitcast.485), calls=%async_computation.2 | async-start | bytes 1572864 | tf_op jit(solution)/shard_map/all_to_all | solution.py:388
  554.2 108.9 %collective-permute-start.59 = (bf16[1024,2048]{1,0:T(8,128)(2,1)}, bf16[1024,2048]{1,0:T(8,128)(2,1)}, u32[]{:S(2)}, u32[]{:S(2)}) collective-permute-start(bf16[1024,2048]{1,0:T(8,128)(2,1)} %convolution_convert_fusion.3), channel_id=1, source_target_pairs={{0,8},{8,0},{16,24},{24,16},{1,9},{9,1},{17,25},{25,17},{2,10},{10... | collective-permute-start | bytes 12582920 | tf_op jit(solution)/shard_map/ppermute | solution.py:33
  564.9 84.9 %collective-permute-start.50 = (bf16[4,2,512,256]{3,2,1,0:T(8,128)(2,1)}, bf16[4,2,512,256]{3,2,1,0:T(8,128)(2,1)}, u32[]{:S(2)}, u32[]{:S(2)}) collective-permute-start(bf16[4,2,512,256]{3,2,1,0:T(8,128)(2,1)} %slice.614), channel_id=1, source_target_pairs={{0,16},{8,24},{16,0},{24,8},{1,17},{9,25},{17,1},{25,9},{2,18},{10... | collective-permute-start | bytes 6291464 | tf_op jit(solution)/shard_map/ppermute | solution.py:33
  636.6 59.5 %all-to-all-start.3 = ((bf16[8,3,128,384]{3,2,1,0:T(8,128)(2,1)}), bf16[8,3,128,384]{3,2,1,0:T(8,128)(2,1)}, u32[]{:S(2)}, u32[]{:S(2)}) async-start(bf16[8,3,128,384]{3,2,1,0:T(8,128)(2,1)} %get-tuple-element.34), calls=%async_computation.3 | async-start | bytes 4718592 | tf_op jit(solution)/shard_map/all_to_all | solution.py:388
  652.7 39.1 %collective-permute-start.51 = (bf16[4,1,512,256]{3,2,1,0:T(8,128)(2,1)S(1)}, bf16[4,1,512,256]{3,2,1,0:T(8,128)(2,1)S(1)}, u32[]{:S(2)}, u32[]{:S(2)}) collective-permute-start(bf16[4,1,512,256]{3,2,1,0:T(8,128)(2,1)S(1)} %constant_dynamic-slice_fusion.12), channel_id=1, source_target_pairs={{0,1},{1,0},{2,3},{3,2},{4,5},{5,4},{6,7},{7,6},{8,9},{9,8},{10,11... | collective-permute-start | bytes 3145736 | tf_op jit(solution)/shard_map/ppermute | solution.py:33
  662.2 88.9 %collective-permute-start.55 = (bf16[4,1,512,512]{3,2,0,1:T(8,128)(2,1)}, bf16[4,1,512,512]{3,2,0,1:T(8,128)(2,1)}, u32[]{:S(2)}, u32[]{:S(2)}) collective-permute-start(bf16[4,1,512,512]{3,2,0,1:T(8,128)(2,1)} %dynamic-slice_bitcast_fusion), channel_id=1, source_target_pairs={{0,1},{1,0},{2,3},{3,2},{4,5},{5,4},{6,7},{7,6},{8,9},{9,8},{10,11... | collective-permute-start | bytes 6291464 | tf_op jit(solution)/shard_map/ppermute | solution.py:33
  670.3 95.9 %collective-permute-start.60 = (bf16[4,2,128,1024]{3,2,1,0:T(8,128)(2,1)}, bf16[4,2,128,1024]{3,2,1,0:T(8,128)(2,1)}, u32[]{:S(2)}, u32[]{:S(2)}) collective-permute-start(bf16[4,2,128,1024]{3,2,1,0:T(8,128)(2,1)} %slice.621), channel_id=1, source_target_pairs={{0,16},{8,24},{16,0},{24,8},{1,17},{9,25},{17,1},{25,9},{2,18},{10... | collective-permute-start | bytes 6291464 | tf_op jit(solution)/shard_map/ppermute | solution.py:33
  693.6 45.3 %collective-permute-start.52 = (bf16[2,1,512,256]{2,3,1,0:T(8,128)(2,1)}, bf16[2,1,512,256]{2,3,1,0:T(8,128)(2,1)}, u32[]{:S(2)}, u32[]{:S(2)}) collective-permute-start(bf16[2,1,512,256]{2,3,1,0:T(8,128)(2,1)} %dynamic-slice_bitcast_fusion.5), channel_id=1, source_target_pairs={{0,4},{2,6},{4,0},{6,2},{1,5},{3,7},{5,1},{7,3},{8,12},{10,14},{12... | collective-permute-start | bytes 1572872 | tf_op jit(solution)/shard_map/ppermute | solution.py:33
  727.8 63.7 %collective-permute-start.42 = (bf16[3072,512]{1,0:T(8,128)(2,1)}, bf16[3072,512]{1,0:T(8,128)(2,1)}, u32[]{:S(2)}, u32[]{:S(2)}) collective-permute-start(bf16[3072,512]{1,0:T(8,128)(2,1)} %convolution_convert_fusion.2), channel_id=1, source_target_pairs={{0,8},{8,0},{16,24},{24,16},{1,9},{9,1},{17,25},{25,17},{2,10},{10... | collective-permute-start | bytes 9437192 | tf_op jit(solution)/shard_map/ppermute | solution.py:33
  732.3 65.5 %collective-permute-start.32 = (bf16[4096,512]{1,0:T(8,128)(2,1)}, bf16[4096,512]{1,0:T(8,128)(2,1)}, u32[]{:S(2)}, u32[]{:S(2)}) collective-permute-start(bf16[4096,512]{1,0:T(8,128)(2,1)} %convolution_convert_fusion.1), channel_id=1, source_target_pairs={{0,8},{8,0},{16,24},{24,16},{1,9},{9,1},{17,25},{25,17},{2,10},{10... | collective-permute-start | bytes 12582920 | tf_op jit(solution)/shard_map/ppermute | solution.py:33
  738.9 68.4 %collective-permute-start.37 = (bf16[1024,2048]{1,0:T(8,128)(2,1)}, bf16[1024,2048]{1,0:T(8,128)(2,1)}, u32[]{:S(2)}, u32[]{:S(2)}) collective-permute-start(bf16[1024,2048]{1,0:T(8,128)(2,1)} %convolution_convert_fusion.4), channel_id=1, source_target_pairs={{0,8},{8,0},{16,24},{24,16},{1,9},{9,1},{17,25},{25,17},{2,10},{10... | collective-permute-start | bytes 12582920 | tf_op jit(solution)/shard_map/ppermute | solution.py:33
  771.3 44.4 %collective-permute-start.61 = (bf16[4,1,128,1024]{3,2,1,0:T(8,128)(2,1)}, bf16[4,1,128,1024]{3,2,1,0:T(8,128)(2,1)}, u32[]{:S(2)}, u32[]{:S(2)}) collective-permute-start(bf16[4,1,128,1024]{3,2,1,0:T(8,128)(2,1)} %constant_dynamic-slice_fusion.1), channel_id=1, source_target_pairs={{0,1},{1,0},{2,3},{3,2},{4,5},{5,4},{6,7},{7,6},{8,9},{9,8},{10,11... | collective-permute-start | bytes 3145736 | tf_op jit(solution)/shard_map/ppermute | solution.py:33
  791.4 48.7 %collective-permute-start.57 = (bf16[2,1,512,256]{2,3,1,0:T(8,128)(2,1)}, bf16[2,1,512,256]{2,3,1,0:T(8,128)(2,1)S(1)}, u32[]{:S(2)}, u32[]{:S(2)}) collective-permute-start(bf16[2,1,512,256]{2,3,1,0:T(8,128)(2,1)} %dynamic-slice_bitcast_fusion.4), channel_id=1, source_target_pairs={{0,4},{2,6},{4,0},{6,2},{1,5},{3,7},{5,1},{7,3},{8,12},{10,14},{12... | collective-permute-start | bytes 1572872 | tf_op jit(solution)/shard_map/ppermute | solution.py:33
  797.8 37.7 %collective-permute-start.43 = (bf16[4,1,384,512]{3,2,0,1:T(8,128)(2,1)}, bf16[4,1,384,512]{3,2,0,1:T(8,128)(2,1)}, u32[]{:S(2)}, u32[]{:S(2)}) collective-permute-start(bf16[4,1,384,512]{3,2,0,1:T(8,128)(2,1)} %dynamic-slice_bitcast_fusion.2), channel_id=1, source_target_pairs={{0,1},{1,0},{2,3},{3,2},{4,5},{5,4},{6,7},{7,6},{8,9},{9,8},{10,11... | collective-permute-start | bytes 4718600 | tf_op jit(solution)/shard_map/ppermute | solution.py:33
  805.3 89.2 %collective-permute-start.33 = (bf16[4,1,512,512]{3,2,0,1:T(8,128)(2,1)}, bf16[4,1,512,512]{3,2,0,1:T(8,128)(2,1)}, u32[]{:S(2)}, u32[]{:S(2)}) collective-permute-start(bf16[4,1,512,512]{3,2,0,1:T(8,128)(2,1)} %dynamic-slice_bitcast_fusion.1), channel_id=1, source_target_pairs={{0,1},{1,0},{2,3},{3,2},{4,5},{5,4},{6,7},{7,6},{8,9},{9,8},{10,11... | collective-permute-start | bytes 6291464 | tf_op jit(solution)/shard_map/ppermute | solution.py:33
  821.5 78.4 %collective-permute-start.38 = (bf16[4,2,128,1024]{3,2,1,0:T(8,128)(2,1)}, bf16[4,2,128,1024]{3,2,1,0:T(8,128)(2,1)}, u32[]{:S(2)}, u32[]{:S(2)}) collective-permute-start(bf16[4,2,128,1024]{3,2,1,0:T(8,128)(2,1)} %slice.607), channel_id=1, source_target_pairs={{0,16},{8,24},{16,0},{24,8},{1,17},{9,25},{17,1},{25,9},{2,18},{10... | collective-permute-start | bytes 6291464 | tf_op jit(solution)/shard_map/ppermute | solution.py:33
  822.9 34.8 %collective-permute-start.62 = (bf16[2,1,128,1024]{2,3,1,0:T(8,128)(2,1)S(1)}, bf16[2,1,128,1024]{2,3,1,0:T(8,128)(2,1)S(1)}, u32[]{:S(2)}, u32[]{:S(2)}) collective-permute-start(bf16[2,1,128,1024]{2,3,1,0:T(8,128)(2,1)S(1)} %dynamic-slice_bitcast_fusion.3), channel_id=1, source_target_pairs={{0,4},{2,6},{4,0},{6,2},{1,5},{3,7},{5,1},{7,3},{8,12},{10,14},{12... | collective-permute-start | bytes 1572872 | tf_op jit(solution)/shard_map/ppermute | solution.py:33
  840.1 50.4 %collective-permute-start.44 = (bf16[4,1,384,256]{3,2,0,1:T(8,128)(2,1)S(1)}, bf16[4,1,384,256]{3,2,0,1:T(8,128)(2,1)S(1)}, u32[]{:S(2)}, u32[]{:S(2)}) collective-permute-start(bf16[4,1,384,256]{3,2,0,1:T(8,128)(2,1)S(1)} %slice.609), channel_id=1, source_target_pairs={{0,16},{8,24},{16,0},{24,8},{1,17},{9,25},{17,1},{25,9},{2,18},{10... | collective-permute-start | bytes 2359304 | tf_op jit(solution)/shard_map/ppermute | solution.py:33
  859.3 29.8 %collective-permute-start.67 = (f32[64,1024]{1,0:T(8,128)S(1)}, f32[64,1024]{1,0:T(8,128)S(1)}, u32[]{:S(2)}, u32[]{:S(2)}) collective-permute-start(f32[64,1024]{1,0:T(8,128)S(1)} %add.836), channel_id=1, source_target_pairs={{0,16},{8,24},{16,0},{24,8},{1,17},{9,25},{17,1},{25,9},{2,18},{10... | collective-permute-start | bytes 786440 | tf_op jit(solution)/shard_map/ppermute | solution.py:33
  866.5 38.7 %collective-permute-start.63 = (bf16[1,1,128,1024]{2,3,1,0:T(8,128)(2,1)}, bf16[1,1,128,1024]{2,3,1,0:T(8,128)(2,1)}, u32[]{:S(2)}, u32[]{:S(2)}) collective-permute-start(bf16[1,1,128,1024]{2,3,1,0:T(8,128)(2,1)} %constant_dynamic-slice_fusion), channel_id=1, source_target_pairs={{0,2},{2,0},{4,6},{6,4},{1,3},{3,1},{5,7},{7,5},{8,10},{10,8},{12,... | collective-permute-start | bytes 786440 | tf_op jit(solution)/shard_map/ppermute | solution.py:33
  924.7 33.8 %collective-permute-start.35 = (bf16[2,1,512,256]{2,3,1,0:T(8,128)(2,1)}, bf16[2,1,512,256]{2,3,1,0:T(8,128)(2,1)}, u32[]{:S(2)}, u32[]{:S(2)}) collective-permute-start(bf16[2,1,512,256]{2,3,1,0:T(8,128)(2,1)} %dynamic-slice_bitcast_fusion.7), channel_id=1, source_target_pairs={{0,4},{2,6},{4,0},{6,2},{1,5},{3,7},{5,1},{7,3},{8,12},{10,14},{12... | collective-permute-start | bytes 1572872 | tf_op jit(solution)/shard_map/ppermute | solution.py:33
  927.5 41.1 %collective-permute-start.40 = (bf16[2,1,128,1024]{2,3,1,0:T(8,128)(2,1)S(1)}, bf16[2,1,128,1024]{2,3,1,0:T(8,128)(2,1)S(1)}, u32[]{:S(2)}, u32[]{:S(2)}) collective-permute-start(bf16[2,1,128,1024]{2,3,1,0:T(8,128)(2,1)S(1)} %dynamic-slice_bitcast_fusion.6), channel_id=1, source_target_pairs={{0,4},{2,6},{4,0},{6,2},{1,5},{3,7},{5,1},{7,3},{8,12},{10,14},{12... | collective-permute-start | bytes 1572872 | tf_op jit(solution)/shard_map/ppermute | solution.py:33
  (275 other events, 3272.0 us)

commit v4 on v3

--- a/solution.py
+++ b/solution.py
@@ -675,7 +675,7 @@
     mixed_grad = product(att_low, output_full).astype(bf16)
     attention_g, table_g = attention.backward(mixed_grad)
     begun = []
-    inputs_g = reduce_group([(att_normed, attention_g)], True, begun)
+    inputs_g = reduce_group([(att_normed, attention_g)], False, begun)
     att_in_g, att_scale, att_shift = norm_back(
         after_first, norm_scales[1], norm_shifts[1], product(attention_g, inputs_full)
     )

time: 989 us -> 986 us (level)
  transfers between devices with their start and end apart: 73 -> 73, of which waited for: 33 -> 34; matrix products, arithmetic and copies ran while one was open for 28% -> 28% of each run, Pallas kernels for 15% -> 15%
where the time goes in v4:
time: 986 us; the launch traced here: 978 us
  waiting for transfers between devices  344 us (35%)
  Pallas kernels  144 us (15%)
  matrix products  144 us (15%)
  local copies, waits for them, and re-layouts  126 us (13%)
  other arithmetic  121 us (12%)
  starting transfers between devices  94.4 us (10%)
    ppermute x67, waiting for transfers between devices, swapped(): return lax.ppermute(shard, axis, [(i, i ^ 1 << bit) for i in range(peers)])  335 us
    pallas_call x1, Pallas kernels, attend_back(): pl.pallas_call(attend_back_kernel, out_shape=[jax.ShapeDtypeStruct(x.shap...  67.9 us
    ppermute x67, starting transfers between devices, swapped(): return lax.ppermute(shard, axis, [(i, i ^ 1 << bit) for i in range(peers)])  67.3 us
    dot_general x16, matrix products, weight_grad(): lax.dot_general(left, right, (((0,), (0,)), ((), ())), preferred_element_...  60.8 us
    unnamed x536, local copies, waits for them, and re-layouts  49.1 us
    pallas_call x6, Pallas kernels, place_whole(): pl.pallas_call(functools.partial(place_whole_kernel, splits, reverse, acr...  46.3 us
    dot_general x8, matrix products, product_t(): lax.dot_general(left, right, (((1,), (1,)), ((), ())), preferred_element_...  41.6 us
    dot_general x8, matrix products, product(): return jnp.dot(left, right, preferred_element_type=f32)  41.2 us
  transfers between devices with their start and end apart: 73, of which 34 were waited for; matrix products, arithmetic and copies ran while one was open for 28% of the time, Pallas kernels for 15%

profile of v4, /device:TPU:0, one launch (start us, length us, event | category | flops | bytes accessed | tf_op | source)
XLA Modules:
  0.0 977.8 jit_solution(2167300959011097814)
XLA Ops:
  6.2 5.9 collective-permute-done
  15.2 6.6 collective-permute-done.5
  22.0 28.6 %collective-permute-done.1 = bf16[2,512,256]{2,1,0:T(8,128)(2,1)S(1)} collective-permute-done((bf16[2,512,256]{2,1,0:T(8,128)(2,1)S(1)}, bf16[2,512,256]{2,1,0:T(8,128)(2,1)S(1)}, u32[]{:S(2)}, u32[]{:S(2)}) %collective-permute-start.1) | collective-permute-done | bytes 524320 | tf_op jit(solution)/shard_map/ppermute | solution.py:33
  52.6 6.6 collective-permute-done.6
  60.6 9.9 %collective-permute-done.2 = bf16[4,512,256]{2,1,0:T(8,128)(2,1)S(1)} collective-permute-done((bf16[4,512,256]{2,1,0:T(8,128)(2,1)S(1)}, bf16[4,512,256]{2,1,0:T(8,128)(2,1)S(1)}, u32[]{:S(2)}, u32[]{:S(2)}) %collective-permute-start.2) | collective-permute-done | bytes 1048608 | tf_op jit(solution)/shard_map/ppermute | solution.py:33
  73.2 12.2 %collective-permute-done.7 = bf16[4,128,1024]{2,1,0:T(8,128)(2,1)S(1)} collective-permute-done((bf16[4,128,1024]{2,1,0:T(8,128)(2,1)S(1)}, bf16[4,128,1024]{2,1,0:T(8,128)(2,1)S(1)}, u32[]{:S(2)}, u32[]{:S(2)}) %collective-permute-start.7) | collective-permute-done | bytes 1048608 | tf_op jit(solution)/shard_map/ppermute | solution.py:33
  93.3 7.4 collective-permute-done.10
  108.2 9.3 collective-permute-done.11
  129.9 6.1 collective-permute-done.8
  140.6 9.6 collective-permute-done.12
  164.6 24.2 %collective-permute-done.27 = bf16[2,128,1024]{2,1,0:T(8,128)(2,1)S(1)} collective-permute-done((bf16[2,128,1024]{2,1,0:T(8,128)(2,1)}, bf16[2,128,1024]{2,1,0:T(8,128)(2,1)S(1)}, u32[]{:S(2)}, u32[]{:S(2)}) %collective-permute-start.27) | collective-permute-done | bytes 524320 | tf_op jit(solution)/shard_map/ppermute | solution.py:33
  190.1 6.8 collective-permute-done.22
  207.3 12.6 %collective-permute-done.28 = bf16[4,128,1024]{2,1,0:T(8,128)(2,1)S(1)} collective-permute-done((bf16[4,128,1024]{2,1,0:T(8,128)(2,1)S(1)}, bf16[4,128,1024]{2,1,0:T(8,128)(2,1)S(1)}, u32[]{:S(2)}, u32[]{:S(2)}) %collective-permute-start.28) | collective-permute-done | bytes 1048608 | tf_op jit(solution)/shard_map/ppermute | solution.py:33
  226.1 8.2 place.6
  234.3 7.8 place.7
  242.2 11.4 %multiply_convert_fusion.1 = (bf16[384,4096]{1,0:T(8,128)(2,1)S(1)}, f32[384,4096]{1,0:T(8,128)}) fusion(f32[4096]{0:T(1024)S(1)} %bitcast.630, bf16[384,1024]{1,0:T(8,128)(2,1)S(1)} %copy-done.60, bf16[4096,1024]{1,0:T(8,128)(2,1)} %place.6), kind=kOutput, calls=%fused_computation.17 | convolution fusion | flops 3230662656 | bytes 18628608 | tf_op jit(solution)/shard_map/dot_general | solution.py:77
  259.7 8.0 place.8
  268.3 7.2 add_convert_fusion.5
  277.3 5.5 all-to-all-start
  289.5 12.1 %collective-permute-done.17 = bf16[4,384,256]{2,1,0:T(8,128)(2,1)S(1)} collective-permute-done((bf16[4,384,256]{2,1,0:T(8,128)(2,1)S(1)}, bf16[4,384,256]{2,1,0:T(8,128)(2,1)S(1)}, u32[]{:S(2)}, u32[]{:S(2)}) %collective-permute-start.17) | collective-permute-done | bytes 786464 | tf_op jit(solution)/shard_map/ppermute | solution.py:33
  318.4 29.1 %collective-permute-done.18 = bf16[8,384,256]{2,1,0:T(8,128)(2,1)S(1)} collective-permute-done((bf16[8,384,256]{2,1,0:T(8,128)(2,1)S(1)}, bf16[8,384,256]{2,1,0:T(8,128)(2,1)S(1)}, u32[]{:S(2)}, u32[]{:S(2)}) %collective-permute-start.18) | collective-permute-done | bytes 1572896 | tf_op jit(solution)/shard_map/ppermute | solution.py:33
  349.6 29.6 %attend.1 = (bf16[8,3,128,128]{3,2,1,0:T(8,128)(2,1)}, bf16[3,2,1024,1024]{3,2,1,0:T(8,128)(2,1)}) custom-call(s32[3]{0:T(128)} %lengths.1, bf16[8,3,128,384]{3,2,1,0:T(8,128)(2,1)} %all-to-all-done.x_ref, bf16[128,64]{1,0:T(8,128)(2,1)} %pad.200.table_ref), custom_call_target="tpu_custom_call" | custom-call | flops 6442450944 | bytes 12582912 | tf_op jit(solution)/shard_map/attend/pallas_call | solution.py:325
  379.1 5.7 all-to-all-start.1
  385.4 6.7 place.9
  392.1 7.9 place.10
  400.1 7.7 place.11
  423.7 7.4 fusion.147
  435.9 6.5 multiply_convert_fusion
  442.5 7.0 fusion.158
  454.3 10.7 %convert_reduce_fusion = (f32[4096]{0:T(1024)}, bf16[384,4096]{1,0:T(8,128)(2,1)S(1)}) fusion(f32[384,4096]{1,0:T(8,128)} %get-tuple-element.284, f32[4096]{0:T(1024)S(1)} %bitcast.634, bf16[384,1024]{1,0:T(8,128)(2,1)S(1)} %get-tuple-element.130, bf16[1024,4096]{1,0:T(8,128)(2,1)} %place.11), kind=kOutput, calls=%fused_computation.12 | convolution fusion | flops 3241668608 | bytes 18644992 | tf_op jit(solution)/shard_map/dot_general | solution.py:69
  485.1 10.0 %broadcast_multiply_fusion = (f32[3,128,1024]{2,1,0:T(8,128)}, f32[3,128,1024]{2,1,0:T(8,128)}, f32[3,128,1024]{2,1,0:T(8,128)}, f32[3,128,1024]{2,1,0:T(8,128)}...) fusion(f32[3,128,1024]{2,1,0:T(8,128)S(1)} %bitcast.428, ...), kind=kLoop, calls=%fused_computation.202 | loop fusion | flops 7077888 | bytes 29958144 | tf_op jit(solution)/shard_map/transpose(jvp())/mul | solution.py:65
  495.1 16.1 %pad_add_fusion = f32[3,158,1024]{2,1,0:T(8,128)S(1)} fusion(f32[3,128,1024]{2,1,0:T(8,128)S(1)} %get-tuple-element.158, f32[3,128,1024]{2,1,0:T(8,128)S(1)} %get-tuple-element.159, f32[3,128,1024]{2,1,0:T(8,128)S(1)} %get-tuple-element.160, f32[3,128,1024]{2,1,0:T(8,128)} %get-tuple-element.161, f32[3,128,1024]{2,1,0:T(8,128)} %get-tuple-element.162, ...), kind=kLoop, calls=%fused_computation.61 | loop fusion | flops 14561280 | bytes 50700288 | tf_op jit(solution)/shard_map/transpose(jvp())/add_any | solution.py:65
  541.8 6.1 all-to-all-start.2
  547.9 6.3 convolution_convert_fusion.3
  568.8 67.9 %attend_back.1 = (bf16[8,3,128,384]{3,2,1,0:T(8,128)(2,1)}, f32[3,128,64]{2,1,0:T(8,128)}) custom-call(bf16[8,3,128,384]{3,2,1,0:T(8,128)(2,1)} %all-to-all-done.x_ref, bf16[8,3,128,128]{3,2,1,0:T(8,128)(2,1)} %all-to-all-done.2.grad_ref, bf16[3,2,1024,1024]{3,2,1,0:T(8,128)(2,1)} %get-tuple-element.33.probs_ref, bf16[128,64]{1,0:T(8,128)(2,1)} %pad.200.table_ref), custom_call_target="tpu_custom_call" | custom-call | flops 12884901888 | bytes 12582912 | tf_op jit(solution)/shard_map/attend_back/pallas_call | solution.py:356
  671.7 20.1 %collective-permute-done.51 = bf16[4,1,512,256]{3,2,1,0:T(8,128)(2,1)S(1)} collective-permute-done((bf16[4,1,512,256]{3,2,1,0:T(8,128)(2,1)S(1)}, bf16[4,1,512,256]{3,2,1,0:T(8,128)(2,1)S(1)}, u32[]{:S(2)}, u32[]{:S(2)}) %collective-permute-start.51) | collective-permute-done | bytes 1048608 | tf_op jit(solution)/shard_map/ppermute | solution.py:33
  700.6 5.9 multiply_reduce_fusion.34
  709.9 10.7 %convert_reduce_fusion.1 = (f32[4096]{0:T(1024)S(1)}, bf16[384,4096]{1,0:T(8,128)(2,1)S(1)}) fusion(f32[384,4096]{1,0:T(8,128)} %get-tuple-element.276, f32[4096]{0:T(1024)S(1)} %bitcast.631, bf16[384,1024]{1,0:T(8,128)(2,1)S(1)} %get-tuple-element.125, bf16[1024,4096]{1,0:T(8,128)(2,1)} %place.7), kind=kOutput, calls=%fused_computation.13 | convolution fusion | flops 3241668608 | bytes 18644992 | tf_op jit(solution)/shard_map/dot_general | solution.py:69
  739.0 4.8 concatenate.201
  750.4 5.7 collective-permute-start.53
  771.0 17.1 %collective-permute-done.56 = bf16[4,1,512,256]{3,2,0,1:T(8,128)(2,1)S(1)} collective-permute-done((bf16[4,1,512,256]{3,2,0,1:T(8,128)(2,1)S(1)}, bf16[4,1,512,256]{3,2,0,1:T(8,128)(2,1)S(1)}, u32[]{:S(2)}, u32[]{:S(2)}) %collective-permute-start.56) | collective-permute-done | bytes 1048608 | tf_op jit(solution)/shard_map/ppermute | solution.py:33
  806.5 6.7 add_convert_fusion.2
  827.1 7.7 collective-permute-done.43
  840.7 12.1 %collective-permute-done.65 = f32[64,1024]{1,0:T(8,128)S(1)} collective-permute-done((f32[64,1024]{1,0:T(8,128)S(1)}, f32[64,1024]{1,0:T(8,128)S(1)}, u32[]{:S(2)}, u32[]{:S(2)}) %collective-permute-start.65) | collective-permute-done | bytes 262176 | tf_op jit(solution)/shard_map/ppermute | solution.py:33
  856.0 5.8 collective-permute-done.58
  863.0 20.3 %collective-permute-done.67 = f32[64,1024]{1,0:T(8,128)S(1)} collective-permute-done((f32[64,1024]{1,0:T(8,128)S(1)}, f32[64,1024]{1,0:T(8,128)S(1)}, u32[]{:S(2)}, u32[]{:S(2)}) %collective-permute-start.67) | collective-permute-done | bytes 262176 | tf_op jit(solution)/shard_map/ppermute | solution.py:33
  926.2 28.4 %collective-permute-done.35 = bf16[2,1,512,256]{2,3,1,0:T(8,128)(2,1)} collective-permute-done((bf16[2,1,512,256]{2,3,1,0:T(8,128)(2,1)}, bf16[2,1,512,256]{2,3,1,0:T(8,128)(2,1)}, u32[]{:S(2)}, u32[]{:S(2)}) %collective-permute-start.35) | collective-permute-done | bytes 524320 | tf_op jit(solution)/shard_map/ppermute | solution.py:33
  955.9 9.5 collective-permute-done.40
  (880 shorter events, 387.6 us)
Async XLA Ops:
  12.1 38.5 %collective-permute-start.1 = (bf16[2,512,256]{2,1,0:T(8,128)(2,1)S(1)}, bf16[2,512,256]{2,1,0:T(8,128)(2,1)S(1)}, u32[]{:S(2)}, u32[]{:S(2)}) collective-permute-start(bf16[2,512,256]{2,1,0:T(8,128)(2,1)S(1)} %pad_maximum_fusion.14), channel_id=1, source_target_pairs={{0,4},{2,6},{4,0},{6,2},{1,5},{3,7},{5,1},{7,3},{8,12},{10,14},{12... | collective-permute-start | bytes 1572872 | tf_op jit(solution)/shard_map/ppermute | solution.py:33
  21.9 37.2 %collective-permute-start.6 = (bf16[2,128,1024]{2,1,0:T(8,128)(2,1)S(1)}, bf16[2,128,1024]{2,1,0:T(8,128)(2,1)S(1)}, u32[]{:S(2)}, u32[]{:S(2)}) collective-permute-start(bf16[2,128,1024]{2,1,0:T(8,128)(2,1)S(1)} %pad_maximum_fusion.15), channel_id=1, source_target_pairs={{0,4},{2,6},{4,0},{6,2},{1,5},{3,7},{5,1},{7,3},{8,12},{10,14},{12... | collective-permute-start | bytes 1572872 | tf_op jit(solution)/shard_map/ppermute | solution.py:33
  59.2 26.2 %collective-permute-start.7 = (bf16[4,128,1024]{2,1,0:T(8,128)(2,1)S(1)}, bf16[4,128,1024]{2,1,0:T(8,128)(2,1)S(1)}, u32[]{:S(2)}, u32[]{:S(2)}) collective-permute-start(bf16[4,128,1024]{2,1,0:T(8,128)(2,1)S(1)} %pad_maximum_fusion.9), channel_id=1, source_target_pairs={{0,16},{8,24},{16,0},{24,8},{1,17},{9,25},{17,1},{25,9},{2,18},{10... | collective-permute-start | bytes 3145736 | tf_op jit(solution)/shard_map/ppermute | solution.py:33
  72.2 54.6 %collective-permute-start.3 = (bf16[8,512,256]{2,1,0:T(8,128)(2,1)}, bf16[8,512,256]{2,1,0:T(8,128)(2,1)}, u32[]{:S(2)}, u32[]{:S(2)}) collective-permute-start(bf16[8,512,256]{2,1,0:T(8,128)(2,1)} %pad_maximum_fusion.1), channel_id=1, source_target_pairs={{0,16},{8,24},{16,0},{24,8},{1,17},{9,25},{17,1},{25,9},{2,18},{10... | collective-permute-start | bytes 6291464 | tf_op jit(solution)/shard_map/ppermute | solution.py:33
  87.1 48.9 %collective-permute-start.8 = (bf16[8,128,1024]{2,1,0:T(8,128)(2,1)}, bf16[8,128,1024]{2,1,0:T(8,128)(2,1)}, u32[]{:S(2)}, u32[]{:S(2)}) collective-permute-start(bf16[8,128,1024]{2,1,0:T(8,128)(2,1)} %pad_maximum_fusion.2), channel_id=1, source_target_pairs={{0,1},{1,0},{2,3},{3,2},{4,5},{5,4},{6,7},{7,6},{8,9},{9,8},{10,11... | collective-permute-start | bytes 6291464 | tf_op jit(solution)/shard_map/ppermute | solution.py:33
  90.0 65.6 %collective-permute-start.26 = (bf16[1,128,1024]{2,1,0:T(8,128)(2,1)S(1)}, bf16[1,128,1024]{2,1,0:T(8,128)(2,1)S(1)}, u32[]{:S(2)}, u32[]{:S(2)}) collective-permute-start(bf16[1,128,1024]{2,1,0:T(8,128)(2,1)S(1)} %bitcast.438), channel_id=1, source_target_pairs={{0,2},{2,0},{4,6},{6,4},{1,3},{3,1},{5,7},{7,5},{8,10},{10,8},{12,... | collective-permute-start | bytes 786440 | tf_op jit(solution)/shard_map/ppermute | solution.py:33
  92.5 64.0 %collective-permute-start.21 = (bf16[1,512,256]{2,1,0:T(8,128)(2,1)S(1)}, bf16[1,512,256]{2,1,0:T(8,128)(2,1)S(1)}, u32[]{:S(2)}, u32[]{:S(2)}) collective-permute-start(bf16[1,512,256]{2,1,0:T(8,128)(2,1)S(1)} %bitcast.442), channel_id=1, source_target_pairs={{0,2},{2,0},{4,6},{6,4},{1,3},{3,1},{5,7},{7,5},{8,10},{10,8},{12,... | collective-permute-start | bytes 786440 | tf_op jit(solution)/shard_map/ppermute | solution.py:33
  117.6 32.6 %collective-permute-start.12 = (bf16[4,512,256]{2,1,0:T(8,128)(2,1)S(1)}, bf16[4,512,256]{2,1,0:T(8,128)(2,1)S(1)}, u32[]{:S(2)}, u32[]{:S(2)}) collective-permute-start(bf16[4,512,256]{2,1,0:T(8,128)(2,1)S(1)} %pad_maximum_fusion.10), channel_id=1, source_target_pairs={{0,1},{1,0},{2,3},{3,2},{4,5},{5,4},{6,7},{7,6},{8,9},{9,8},{10,11... | collective-permute-start | bytes 3145736 | tf_op jit(solution)/shard_map/ppermute | solution.py:33
  129.9 95.8 %collective-permute-start.4 = (bf16[16,512,256]{2,1,0:T(8,128)(2,1)}, bf16[16,512,256]{2,1,0:T(8,128)(2,1)}, u32[]{:S(2)}, u32[]{:S(2)}) collective-permute-start(bf16[16,512,256]{2,1,0:T(8,128)(2,1)} %constant_dynamic-update-slice_fusion), channel_id=1, source_target_pairs={{0,8},{8,0},{16,24},{24,16},{1,9},{9,1},{17,25},{25,17},{2,10},{10... | collective-permute-start | bytes 12582920 | tf_op jit(solution)/shard_map/ppermute | solution.py:33
  139.1 95.2 %collective-permute-start.9 = (bf16[16,128,1024]{2,1,0:T(8,128)(2,1)}, bf16[16,128,1024]{2,1,0:T(8,128)(2,1)}, u32[]{:S(2)}, u32[]{:S(2)}) collective-permute-start(bf16[16,128,1024]{2,1,0:T(8,128)(2,1)} %constant_dynamic-update-slice_fusion.5), channel_id=1, source_target_pairs={{0,8},{8,0},{16,24},{24,16},{1,9},{9,1},{17,25},{25,17},{2,10},{10... | collective-permute-start | bytes 12582920 | tf_op jit(solution)/shard_map/ppermute | solution.py:33
  151.9 48.7 %collective-permute-start.13 = (bf16[8,512,256]{2,1,0:T(8,128)(2,1)}, bf16[8,512,256]{2,1,0:T(8,128)(2,1)}, u32[]{:S(2)}, u32[]{:S(2)}) collective-permute-start(bf16[8,512,256]{2,1,0:T(8,128)(2,1)} %pad_maximum_fusion.3), channel_id=1, source_target_pairs={{0,16},{8,24},{16,0},{24,8},{1,17},{9,25},{17,1},{25,9},{2,18},{10... | collective-permute-start | bytes 6291464 | tf_op jit(solution)/shard_map/ppermute | solution.py:33
  156.5 32.3 %collective-permute-start.27 = (bf16[2,128,1024]{2,1,0:T(8,128)(2,1)}, bf16[2,128,1024]{2,1,0:T(8,128)(2,1)S(1)}, u32[]{:S(2)}, u32[]{:S(2)}) collective-permute-start(bf16[2,128,1024]{2,1,0:T(8,128)(2,1)} %pad_maximum_fusion.18), channel_id=1, source_target_pairs={{0,4},{2,6},{4,0},{6,2},{1,5},{3,7},{5,1},{7,3},{8,12},{10,14},{12... | collective-permute-start | bytes 1572872 | tf_op jit(solution)/shard_map/ppermute | solution.py:33
  158.0 38.8 %collective-permute-start.22 = (bf16[2,512,256]{2,1,0:T(8,128)(2,1)}, bf16[2,512,256]{2,1,0:T(8,128)(2,1)S(1)}, u32[]{:S(2)}, u32[]{:S(2)}) collective-permute-start(bf16[2,512,256]{2,1,0:T(8,128)(2,1)} %pad_maximum_fusion.17), channel_id=1, source_target_pairs={{0,4},{2,6},{4,0},{6,2},{1,5},{3,7},{5,1},{7,3},{8,12},{10,14},{12... | collective-permute-start | bytes 1572872 | tf_op jit(solution)/shard_map/ppermute | solution.py:33
  204.0 53.6 %collective-permute-start.14 = (bf16[16,512,256]{2,1,0:T(8,128)(2,1)}, bf16[16,512,256]{2,1,0:T(8,128)(2,1)S(1)}, u32[]{:S(2)}, u32[]{:S(2)}) collective-permute-start(bf16[16,512,256]{2,1,0:T(8,128)(2,1)} %constant_dynamic-update-slice_fusion.10), channel_id=1, source_target_pairs={{0,8},{8,0},{16,24},{24,16},{1,9},{9,1},{17,25},{25,17},{2,10},{10... | collective-permute-start | bytes 12582920 | tf_op jit(solution)/shard_map/ppermute | solution.py:33
  219.9 62.9 %collective-permute-start.16 = (bf16[2,384,256]{2,1,0:T(8,128)(2,1)}, bf16[2,384,256]{2,1,0:T(8,128)(2,1)}, u32[]{:S(2)}, u32[]{:S(2)}) collective-permute-start(bf16[2,384,256]{2,1,0:T(8,128)(2,1)} %pad_maximum_fusion.19), channel_id=1, source_target_pairs={{0,4},{2,6},{4,0},{6,2},{1,5},{3,7},{5,1},{7,3},{8,12},{10,14},{12... | collective-permute-start | bytes 1179656 | tf_op jit(solution)/shard_map/ppermute | solution.py:33
  223.8 86.9 %collective-permute-start.29 = (bf16[8,128,1024]{2,1,0:T(8,128)(2,1)}, bf16[8,128,1024]{2,1,0:T(8,128)(2,1)}, u32[]{:S(2)}, u32[]{:S(2)}) collective-permute-start(bf16[8,128,1024]{2,1,0:T(8,128)(2,1)} %pad_maximum_fusion.5), channel_id=1, source_target_pairs={{0,1},{1,0},{2,3},{3,2},{4,5},{5,4},{6,7},{7,6},{8,9},{9,8},{10,11... | collective-permute-start | bytes 6291464 | tf_op jit(solution)/shard_map/ppermute | solution.py:33
  225.7 81.9 %collective-permute-start.24 = (bf16[8,512,256]{2,1,0:T(8,128)(2,1)}, bf16[8,512,256]{2,1,0:T(8,128)(2,1)}, u32[]{:S(2)}, u32[]{:S(2)}) collective-permute-start(bf16[8,512,256]{2,1,0:T(8,128)(2,1)} %pad_maximum_fusion.4), channel_id=1, source_target_pairs={{0,16},{8,24},{16,0},{24,8},{1,17},{9,25},{17,1},{25,9},{2,18},{10... | collective-permute-start | bytes 6291464 | tf_op jit(solution)/shard_map/ppermute | solution.py:33
  277.3 72.3 %all-to-all-start = ((bf16[8,3,128,384]{3,2,1,0:T(8,128)(2,1)}), bf16[8,3,128,384]{3,2,1,0:T(8,128)(2,1)}, u32[]{:S(2)}, u32[]{:S(2)}) async-start(bf16[8,3,128,384]{3,2,1,0:T(8,128)(2,1)} %bitcast.433), calls=%async_computation | async-start | bytes 4718592 | tf_op jit(solution)/shard_map/all_to_all | solution.py:388
  302.8 44.7 %collective-permute-start.18 = (bf16[8,384,256]{2,1,0:T(8,128)(2,1)S(1)}, bf16[8,384,256]{2,1,0:T(8,128)(2,1)S(1)}, u32[]{:S(2)}, u32[]{:S(2)}) collective-permute-start(bf16[8,384,256]{2,1,0:T(8,128)(2,1)S(1)} %pad_maximum_fusion.6), channel_id=1, source_target_pairs={{0,1},{1,0},{2,3},{3,2},{4,5},{5,4},{6,7},{7,6},{8,9},{9,8},{10,11... | collective-permute-start | bytes 4718600 | tf_op jit(solution)/shard_map/ppermute | solution.py:33
  310.6 81.5 %collective-permute-start.25 = (bf16[16,512,256]{2,1,0:T(8,128)(2,1)}, bf16[16,512,256]{2,1,0:T(8,128)(2,1)}, u32[]{:S(2)}, u32[]{:S(2)}) collective-permute-start(bf16[16,512,256]{2,1,0:T(8,128)(2,1)} %constant_dynamic-update-slice_fusion.20), channel_id=1, source_target_pairs={{0,8},{8,0},{16,24},{24,16},{1,9},{9,1},{17,25},{25,17},{2,10},{10... | collective-permute-start | bytes 12582920 | tf_op jit(solution)/shard_map/ppermute | solution.py:33
  313.8 86.2 %collective-permute-start.30 = (bf16[16,128,1024]{2,1,0:T(8,128)(2,1)}, bf16[16,128,1024]{2,1,0:T(8,128)(2,1)}, u32[]{:S(2)}, u32[]{:S(2)}) collective-permute-start(bf16[16,128,1024]{2,1,0:T(8,128)(2,1)} %constant_dynamic-update-slice_fusion.25), channel_id=1, source_target_pairs={{0,8},{8,0},{16,24},{24,16},{1,9},{9,1},{17,25},{25,17},{2,10},{10... | collective-permute-start | bytes 12582920 | tf_op jit(solution)/shard_map/ppermute | solution.py:33
  348.8 36.6 %collective-permute-start.19 = (bf16[16,384,256]{2,1,0:T(8,128)(2,1)}, bf16[16,384,256]{2,1,0:T(8,128)(2,1)}, u32[]{:S(2)}, u32[]{:S(2)}) collective-permute-start(bf16[16,384,256]{2,1,0:T(8,128)(2,1)} %constant_dynamic-update-slice_fusion.15), channel_id=1, source_target_pairs={{0,8},{8,0},{16,24},{24,16},{1,9},{9,1},{17,25},{25,17},{2,10},{10... | collective-permute-start | bytes 9437192 | tf_op jit(solution)/shard_map/ppermute | solution.py:33
  379.1 28.6 %all-to-all-start.1 = ((bf16[8,3,128,128]{3,2,1,0:T(8,128)(2,1)}), bf16[8,3,128,128]{3,2,1,0:T(8,128)(2,1)S(1)}, u32[]{:S(2)}, u32[]{:S(2)}) async-start(bf16[8,3,128,128]{3,2,1,0:T(8,128)(2,1)} %get-tuple-element.29), calls=%async_computation.1 | async-start | bytes 1572864 | tf_op jit(solution)/shard_map/all_to_all | solution.py:388
  513.8 40.6 %collective-permute-start.48 = (bf16[1024,512]{1,0:T(8,128)(2,1)}, bf16[1024,512]{1,0:T(8,128)(2,1)}, u32[]{:S(2)}, u32[]{:S(2)}) collective-permute-start(bf16[1024,512]{1,0:T(8,128)(2,1)} %convolution_convert_fusion.7), channel_id=1, source_target_pairs={{0,8},{8,0},{16,24},{24,16},{1,9},{9,1},{17,25},{25,17},{2,10},{10... | collective-permute-start | bytes 3145736 | tf_op jit(solution)/shard_map/ppermute | solution.py:33
  519.6 135.1 %collective-permute-start.54 = (bf16[4096,512]{1,0:T(8,128)(2,1)}, bf16[4096,512]{1,0:T(8,128)(2,1)}, u32[]{:S(2)}, u32[]{:S(2)}) collective-permute-start(bf16[4096,512]{1,0:T(8,128)(2,1)} %convolution_convert_fusion), channel_id=1, source_target_pairs={{0,8},{8,0},{16,24},{24,16},{1,9},{9,1},{17,25},{25,17},{2,10},{10... | collective-permute-start | bytes 12582920 | tf_op jit(solution)/shard_map/ppermute | solution.py:33
  533.5 25.3 %collective-permute-start.47 = (bf16[2048,512]{1,0:T(8,128)(2,1)}, bf16[2048,512]{1,0:T(8,128)(2,1)}, u32[]{:S(2)}, u32[]{:S(2)}) collective-permute-start(bf16[2048,512]{1,0:T(8,128)(2,1)} %convolution_convert_fusion.5), channel_id=1, source_target_pairs={{0,8},{8,0},{16,24},{24,16},{1,9},{9,1},{17,25},{25,17},{2,10},{10... | collective-permute-start | bytes 6291464 | tf_op jit(solution)/shard_map/ppermute | solution.py:33
  541.8 27.0 %all-to-all-start.2 = ((bf16[8,3,128,128]{3,2,1,0:T(8,128)(2,1)}), bf16[8,3,128,128]{3,2,1,0:T(8,128)(2,1)}, u32[]{:S(2)}, u32[]{:S(2)}) async-start(bf16[8,3,128,128]{3,2,1,0:T(8,128)(2,1)} %bitcast.478), calls=%async_computation.2 | async-start | bytes 1572864 | tf_op jit(solution)/shard_map/all_to_all | solution.py:388
  554.2 108.9 %collective-permute-start.59 = (bf16[1024,2048]{1,0:T(8,128)(2,1)}, bf16[1024,2048]{1,0:T(8,128)(2,1)}, u32[]{:S(2)}, u32[]{:S(2)}) collective-permute-start(bf16[1024,2048]{1,0:T(8,128)(2,1)} %convolution_convert_fusion.3), channel_id=1, source_target_pairs={{0,8},{8,0},{16,24},{24,16},{1,9},{9,1},{17,25},{25,17},{2,10},{10... | collective-permute-start | bytes 12582920 | tf_op jit(solution)/shard_map/ppermute | solution.py:33
  564.9 84.9 %collective-permute-start.50 = (bf16[4,2,512,256]{3,2,1,0:T(8,128)(2,1)}, bf16[4,2,512,256]{3,2,1,0:T(8,128)(2,1)}, u32[]{:S(2)}, u32[]{:S(2)}) collective-permute-start(bf16[4,2,512,256]{3,2,1,0:T(8,128)(2,1)} %slice.614), channel_id=1, source_target_pairs={{0,16},{8,24},{16,0},{24,8},{1,17},{9,25},{17,1},{25,9},{2,18},{10... | collective-permute-start | bytes 6291464 | tf_op jit(solution)/shard_map/ppermute | solution.py:33
  636.6 59.5 %all-to-all-start.3 = ((bf16[8,3,128,384]{3,2,1,0:T(8,128)(2,1)}), bf16[8,3,128,384]{3,2,1,0:T(8,128)(2,1)}, u32[]{:S(2)}, u32[]{:S(2)}) async-start(bf16[8,3,128,384]{3,2,1,0:T(8,128)(2,1)} %get-tuple-element.34), calls=%async_computation.3 | async-start | bytes 4718592 | tf_op jit(solution)/shard_map/all_to_all | solution.py:388
  652.7 39.1 %collective-permute-start.51 = (bf16[4,1,512,256]{3,2,1,0:T(8,128)(2,1)S(1)}, bf16[4,1,512,256]{3,2,1,0:T(8,128)(2,1)S(1)}, u32[]{:S(2)}, u32[]{:S(2)}) collective-permute-start(bf16[4,1,512,256]{3,2,1,0:T(8,128)(2,1)S(1)} %constant_dynamic-slice_fusion.12), channel_id=1, source_target_pairs={{0,1},{1,0},{2,3},{3,2},{4,5},{5,4},{6,7},{7,6},{8,9},{9,8},{10,11... | collective-permute-start | bytes 3145736 | tf_op jit(solution)/shard_map/ppermute | solution.py:33
  662.2 88.2 %collective-permute-start.55 = (bf16[4,1,512,512]{3,2,0,1:T(8,128)(2,1)}, bf16[4,1,512,512]{3,2,0,1:T(8,128)(2,1)}, u32[]{:S(2)}, u32[]{:S(2)}) collective-permute-start(bf16[4,1,512,512]{3,2,0,1:T(8,128)(2,1)} %dynamic-slice_bitcast_fusion), channel_id=1, source_target_pairs={{0,1},{1,0},{2,3},{3,2},{4,5},{5,4},{6,7},{7,6},{8,9},{9,8},{10,11... | collective-permute-start | bytes 6291464 | tf_op jit(solution)/shard_map/ppermute | solution.py:33
  670.3 95.6 %collective-permute-start.60 = (bf16[4,2,128,1024]{3,2,1,0:T(8,128)(2,1)}, bf16[4,2,128,1024]{3,2,1,0:T(8,128)(2,1)}, u32[]{:S(2)}, u32[]{:S(2)}) collective-permute-start(bf16[4,2,128,1024]{3,2,1,0:T(8,128)(2,1)} %slice.621), channel_id=1, source_target_pairs={{0,16},{8,24},{16,0},{24,8},{1,17},{9,25},{17,1},{25,9},{2,18},{10... | collective-permute-start | bytes 6291464 | tf_op jit(solution)/shard_map/ppermute | solution.py:33
  693.6 51.9 %collective-permute-start.52 = (bf16[2,1,512,256]{2,3,1,0:T(8,128)(2,1)}, bf16[2,1,512,256]{2,3,1,0:T(8,128)(2,1)}, u32[]{:S(2)}, u32[]{:S(2)}) collective-permute-start(bf16[2,1,512,256]{2,3,1,0:T(8,128)(2,1)} %dynamic-slice_bitcast_fusion.4), channel_id=1, source_target_pairs={{0,4},{2,6},{4,0},{6,2},{1,5},{3,7},{5,1},{7,3},{8,12},{10,14},{12... | collective-permute-start | bytes 1572872 | tf_op jit(solution)/shard_map/ppermute | solution.py:33
  727.8 63.2 %collective-permute-start.42 = (bf16[3072,512]{1,0:T(8,128)(2,1)}, bf16[3072,512]{1,0:T(8,128)(2,1)}, u32[]{:S(2)}, u32[]{:S(2)}) collective-permute-start(bf16[3072,512]{1,0:T(8,128)(2,1)} %convolution_convert_fusion.2), channel_id=1, source_target_pairs={{0,8},{8,0},{16,24},{24,16},{1,9},{9,1},{17,25},{25,17},{2,10},{10... | collective-permute-start | bytes 9437192 | tf_op jit(solution)/shard_map/ppermute | solution.py:33
  732.3 66.2 %collective-permute-start.32 = (bf16[4096,512]{1,0:T(8,128)(2,1)}, bf16[4096,512]{1,0:T(8,128)(2,1)}, u32[]{:S(2)}, u32[]{:S(2)}) collective-permute-start(bf16[4096,512]{1,0:T(8,128)(2,1)} %convolution_convert_fusion.1), channel_id=1, source_target_pairs={{0,8},{8,0},{16,24},{24,16},{1,9},{9,1},{17,25},{25,17},{2,10},{10... | collective-permute-start | bytes 12582920 | tf_op jit(solution)/shard_map/ppermute | solution.py:33
  745.5 60.5 %collective-permute-start.37 = (bf16[1024,2048]{1,0:T(8,128)(2,1)}, bf16[1024,2048]{1,0:T(8,128)(2,1)}, u32[]{:S(2)}, u32[]{:S(2)}) collective-permute-start(bf16[1024,2048]{1,0:T(8,128)(2,1)} %convolution_convert_fusion.4), channel_id=1, source_target_pairs={{0,8},{8,0},{16,24},{24,16},{1,9},{9,1},{17,25},{25,17},{2,10},{10... | collective-permute-start | bytes 12582920 | tf_op jit(solution)/shard_map/ppermute | solution.py:33
  771.0 43.8 %collective-permute-start.61 = (bf16[4,1,128,1024]{3,2,1,0:T(8,128)(2,1)}, bf16[4,1,128,1024]{3,2,1,0:T(8,128)(2,1)}, u32[]{:S(2)}, u32[]{:S(2)}) collective-permute-start(bf16[4,1,128,1024]{3,2,1,0:T(8,128)(2,1)} %constant_dynamic-slice_fusion.1), channel_id=1, source_target_pairs={{0,1},{1,0},{2,3},{3,2},{4,5},{5,4},{6,7},{7,6},{8,9},{9,8},{10,11... | collective-permute-start | bytes 3145736 | tf_op jit(solution)/shard_map/ppermute | solution.py:33
  790.7 48.7 %collective-permute-start.57 = (bf16[2,1,512,256]{2,3,1,0:T(8,128)(2,1)S(1)}, bf16[2,1,512,256]{2,3,1,0:T(8,128)(2,1)S(1)}, u32[]{:S(2)}, u32[]{:S(2)}) collective-permute-start(bf16[2,1,512,256]{2,3,1,0:T(8,128)(2,1)S(1)} %dynamic-slice_bitcast_fusion.3), channel_id=1, source_target_pairs={{0,4},{2,6},{4,0},{6,2},{1,5},{3,7},{5,1},{7,3},{8,12},{10,14},{12... | collective-permute-start | bytes 1572872 | tf_op jit(solution)/shard_map/ppermute | solution.py:33
  797.2 37.6 %collective-permute-start.43 = (bf16[4,2,384,256]{3,2,1,0:T(8,128)(2,1)}, bf16[4,2,384,256]{3,2,1,0:T(8,128)(2,1)}, u32[]{:S(2)}, u32[]{:S(2)}) collective-permute-start(bf16[4,2,384,256]{3,2,1,0:T(8,128)(2,1)} %slice.609), channel_id=1, source_target_pairs={{0,16},{8,24},{16,0},{24,8},{1,17},{9,25},{17,1},{25,9},{2,18},{10... | collective-permute-start | bytes 4718600 | tf_op jit(solution)/shard_map/ppermute | solution.py:33
  806.1 81.9 %collective-permute-start.33 = (bf16[4,1,512,512]{3,2,0,1:T(8,128)(2,1)}, bf16[4,1,512,512]{3,2,0,1:T(8,128)(2,1)}, u32[]{:S(2)}, u32[]{:S(2)}) collective-permute-start(bf16[4,1,512,512]{3,2,0,1:T(8,128)(2,1)} %dynamic-slice_bitcast_fusion.1), channel_id=1, source_target_pairs={{0,1},{1,0},{2,3},{3,2},{4,5},{5,4},{6,7},{7,6},{8,9},{9,8},{10,11... | collective-permute-start | bytes 6291464 | tf_op jit(solution)/shard_map/ppermute | solution.py:33
  817.4 35.6 %collective-permute-start.62 = (bf16[2,1,128,1024]{2,3,1,0:T(8,128)(2,1)S(1)}, bf16[2,1,128,1024]{2,3,1,0:T(8,128)(2,1)S(1)}, u32[]{:S(2)}, u32[]{:S(2)}) collective-permute-start(bf16[2,1,128,1024]{2,3,1,0:T(8,128)(2,1)S(1)} %dynamic-slice_bitcast_fusion.2), channel_id=1, source_target_pairs={{0,4},{2,6},{4,0},{6,2},{1,5},{3,7},{5,1},{7,3},{8,12},{10,14},{12... | collective-permute-start | bytes 1572872 | tf_op jit(solution)/shard_map/ppermute | solution.py:33
  824.6 68.8 %collective-permute-start.38 = (bf16[4,2,128,1024]{3,2,1,0:T(8,128)(2,1)}, bf16[4,2,128,1024]{3,2,1,0:T(8,128)(2,1)}, u32[]{:S(2)}, u32[]{:S(2)}) collective-permute-start(bf16[4,2,128,1024]{3,2,1,0:T(8,128)(2,1)} %slice.607), channel_id=1, source_target_pairs={{0,16},{8,24},{16,0},{24,8},{1,17},{9,25},{17,1},{25,9},{2,18},{10... | collective-permute-start | bytes 6291464 | tf_op jit(solution)/shard_map/ppermute | solution.py:33
  839.5 44.5 %collective-permute-start.44 = (bf16[4,1,384,256]{3,2,1,0:T(8,128)(2,1)S(1)}, bf16[4,1,384,256]{3,2,1,0:T(8,128)(2,1)S(1)}, u32[]{:S(2)}, u32[]{:S(2)}) collective-permute-start(bf16[4,1,384,256]{3,2,1,0:T(8,128)(2,1)S(1)} %constant_dynamic-slice_fusion.26), channel_id=1, source_target_pairs={{0,1},{1,0},{2,3},{3,2},{4,5},{5,4},{6,7},{7,6},{8,9},{9,8},{10,11... | collective-permute-start | bytes 2359304 | tf_op jit(solution)/shard_map/ppermute | solution.py:33
  854.5 28.7 %collective-permute-start.67 = (f32[64,1024]{1,0:T(8,128)S(1)}, f32[64,1024]{1,0:T(8,128)S(1)}, u32[]{:S(2)}, u32[]{:S(2)}) collective-permute-start(f32[64,1024]{1,0:T(8,128)S(1)} %add.836), channel_id=1, source_target_pairs={{0,16},{8,24},{16,0},{24,8},{1,17},{9,25},{17,1},{25,9},{2,18},{10... | collective-permute-start | bytes 786440 | tf_op jit(solution)/shard_map/ppermute | solution.py:33
  861.8 37.4 %collective-permute-start.63 = (bf16[1,1,128,1024]{2,3,1,0:T(8,128)(2,1)}, bf16[1,1,128,1024]{2,3,1,0:T(8,128)(2,1)}, u32[]{:S(2)}, u32[]{:S(2)}) collective-permute-start(bf16[1,1,128,1024]{2,3,1,0:T(8,128)(2,1)} %constant_dynamic-slice_fusion), channel_id=1, source_target_pairs={{0,2},{2,0},{4,6},{6,4},{1,3},{3,1},{5,7},{7,5},{8,10},{10,8},{12,... | collective-permute-start | bytes 786440 | tf_op jit(solution)/shard_map/ppermute | solution.py:33
  919.9 34.7 %collective-permute-start.35 = (bf16[2,1,512,256]{2,3,1,0:T(8,128)(2,1)}, bf16[2,1,512,256]{2,3,1,0:T(8,128)(2,1)}, u32[]{:S(2)}, u32[]{:S(2)}) collective-permute-start(bf16[2,1,512,256]{2,3,1,0:T(8,128)(2,1)} %dynamic-slice_bitcast_fusion.6), channel_id=1, source_target_pairs={{0,4},{2,6},{4,0},{6,2},{1,5},{3,7},{5,1},{7,3},{8,12},{10,14},{12... | collective-permute-start | bytes 1572872 | tf_op jit(solution)/shard_map/ppermute | solution.py:33
  922.6 42.7 %collective-permute-start.40 = (bf16[2,1,128,1024]{2,3,1,0:T(8,128)(2,1)S(1)}, bf16[2,1,128,1024]{2,3,1,0:T(8,128)(2,1)S(1)}, u32[]{:S(2)}, u32[]{:S(2)}) collective-permute-start(bf16[2,1,128,1024]{2,3,1,0:T(8,128)(2,1)S(1)} %dynamic-slice_bitcast_fusion.5), channel_id=1, source_target_pairs={{0,4},{2,6},{4,0},{6,2},{1,5},{3,7},{5,1},{7,3},{8,12},{10,14},{12... | collective-permute-start | bytes 1572872 | tf_op jit(solution)/shard_map/ppermute | solution.py:33
  (275 other events, 3279.1 us)
